TPU v7x, 32 devices: a whole 2x2x4 slice. The times are simulated.
32 devices in a mesh: groups: 2 (over x), ex: 16 (over z, y, core).
Axes of the slice: x: 2, y: 2, z: 4, core: 2. Of those that a mesh axis runs over, the one named last changes fastest.
Arguments:
- stored_projection_inputs: bfloat16 [2, 64, 128, 8192], P(None, ('groups', 'ex')), parts along dimension 1, may hold values from -8 to 8
- key_output_gradients: bfloat16 [2, 64, 128, 1024], P(None, ('groups', 'ex')), parts along dimension 1, may hold values from -0.078125 to 0.078125
- value_output_gradients: bfloat16 [2, 64, 128, 1024], P(None, ('groups', 'ex')), parts along dimension 1, may hold values from -0.078125 to 0.078125
- key_down_factor: bfloat16 [2, 16, 8192], replicated, may hold values from -0.0625 to 0.0625
- key_up_factor: bfloat16 [2, 1024, 16], replicated, may hold values from -0.1875 to 0.1875
- value_down_factor: bfloat16 [2, 16, 8192], replicated, may hold values from -0.0625 to 0.0625
- value_up_factor: bfloat16 [2, 1024, 16], replicated, may hold values from -0.1875 to 0.1875
- validation: bfloat16 [2, 4, 294912], P(None, 'groups', 'ex'), parts along dimension 1, may hold values from -6 to 6
- lengths: int32 [64], P(('groups', 'ex')), parts along dimension 0, may hold values from 112 to 128, as said below
Outputs:
- scores: float32 [64, 2], P(('groups', 'ex')), parts along dimension 0
There are 2 independent parts, one for each index of `groups`. A program takes and returns all parts, laid end to end along the dimension named above; an argument that names none is the same for every part. Nothing has to cross between parts.
Inputs may be any that keep to these rules, and one draw needn't show every extreme that they name: `lengths`: some example of every group has all 128 tokens.
All inputs are finite; a program needn't handle non-finite values.
Results may differ from a plain program's by a relative error of at most 0.0035.
The roundings to bfloat16 on the way count: a program that leaves them out, or rounds other values in their place, can miss the bound.
Values may be sent and summed in bfloat16 or wider, within the bound.
No kernel may reach another device: no remote copies, remote signals or barrier semaphores. Data moves between devices by JAX's collectives and lax.ppermute only.
A program may use at most 128 MiB of HBM per device.

v0:
```python
import jax
import jax.numpy as jnp
from jax import lax
from jax.sharding import PartitionSpec as P


def per_example_gradients(inputs, grad_key, grad_value, a_key, b_key, a_value, b_value, token_mask):
    low_rank = a_key.shape[0]
    a_both = jnp.concatenate([a_key, a_value], axis=0)
    z_both = jnp.einsum("esd,rd->esr", inputs, a_both, preferred_element_type=jnp.float32)
    z_both = (z_both * token_mask[:, :, None]).astype(jnp.bfloat16)
    y_key = jnp.einsum("eso,or->esr", grad_key, b_key, preferred_element_type=jnp.float32)
    y_value = jnp.einsum("eso,or->esr", grad_value, b_value, preferred_element_type=jnp.float32)
    y_both = (jnp.concatenate([y_key, y_value], axis=2) * token_mask[:, :, None]).astype(
        jnp.bfloat16
    )
    grad_down = jnp.einsum("esr,esd->erd", y_both, inputs, preferred_element_type=jnp.float32)
    grad_up_key = jnp.einsum(
        "esr,eso->ero", z_both[:, :, :low_rank], grad_key, preferred_element_type=jnp.float32
    )
    grad_up_value = jnp.einsum(
        "esr,eso->ero", z_both[:, :, low_rank:], grad_value, preferred_element_type=jnp.float32
    )
    joined = jnp.concatenate(
        [grad_down[:, :low_rank], grad_up_key, grad_down[:, low_rank:], grad_up_value], axis=2
    )
    gradients = joined.reshape(joined.shape[0], -1)
    squares = jnp.sum(gradients * gradients, axis=1)
    return (gradients, squares)


def local(
    stored_projection_inputs,
    key_output_gradients,
    value_output_gradients,
    key_down_factor,
    key_up_factor,
    value_down_factor,
    value_up_factor,
    validation,
    lengths,
):
    highest = lax.Precision.HIGHEST
    num_layers, local_examples, seq_slots, model_width = stored_projection_inputs.shape
    total_count = lax.axis_size("ex") * local_examples
    token_mask = (
        lax.broadcasted_iota(jnp.int32, (local_examples, seq_slots), 1) < lengths[:, None]
    ).astype(jnp.float32)
    gradient_list = []
    square_list = []
    total_list = []
    for layer_position_index in range(num_layers):
        gradients, squares = per_example_gradients(
            stored_projection_inputs[layer_position_index],
            key_output_gradients[layer_position_index],
            value_output_gradients[layer_position_index],
            key_down_factor[layer_position_index],
            key_up_factor[layer_position_index],
            value_down_factor[layer_position_index],
            value_up_factor[layer_position_index],
            token_mask,
        )
        gradient_list.append(gradients)
        square_list.append(squares)
        total_list.append(lax.psum(jnp.sum(squares), "ex"))
    all_gradients = jnp.stack(gradient_list)
    all_squares = jnp.stack(square_list)
    norm_totals = jnp.stack(total_list)
    damping = 0.1 * norm_totals / total_count + 1e-06
    products = jnp.einsum(
        "lep,lvp->lev",
        all_gradients,
        lax.all_gather(validation, "ex", axis=2, tiled=True).astype(jnp.float32),
        precision=highest,
    )
    weights = products / (damping[:, None, None] + all_squares[:, :, None])
    directions = jnp.einsum("lev,lep->lvp", weights, all_gradients, precision=highest)
    summed = lax.psum(directions, "ex")
    correction = jnp.einsum("lep,lvp->lev", all_gradients, summed, precision=highest)
    inner = products - correction / total_count
    return -jnp.sum(inner / damping[:, None, None], axis=0)


def solution(mesh):
    in_specs = (
        P(None, ("groups", "ex"), None, None),
        P(None, ("groups", "ex"), None, None),
        P(None, ("groups", "ex"), None, None),
        P(),
        P(),
        P(),
        P(),
        P(None, "groups", "ex"),
        P(("groups", "ex")),
    )
    out_specs = P(("groups", "ex"), None)
    return jax.shard_map(local, mesh=mesh, in_specs=in_specs, out_specs=out_specs, check_vma=False)
```

profile of v0, /device:TPU:0, one launch (start us, length us, event | category | flops | bytes accessed | tf_op | source)
XLA Modules:
  0.0 287.3 jit_solution(8336601724355767451)
XLA Ops:
  6.5 0.7 all-gather.2.cloned.1.call-update
  7.3 1.3 fusion.43
  8.6 1.4 fusion.51
  10.0 1.3 fusion.39
  11.3 1.4 fusion.47
  12.7 0.7 compare_convert_fusion
  13.4 1.4 slice_bitcast_fusion
  14.8 3.8 %fusion.24 = bf16[2,128,32]{1,2,0:T(8,128)(2,1)S(1)} fusion(bf16[2,2,128,8192]{3,2,1,0:T(8,128)(2,1)} %param.9, bf16[16,8192]{1,0:T(8,128)(2,1)S(1)} %get-tuple-element.20, bf16[16,8192]{1,0:T(8,128)(2,1)S(1)} %get-tuple-element.21, f32[2,128]{1,0:T(2,128)S(1)} %compare_convert_fusion), kind=kOutput, calls=%fused_computation.22 | convolution fusion | flops 135282688 | bytes 4736000 | tf_op jit(solution)/shard_map/esd,rd->esr/dot_general | solution.py:10
  18.8 0.8 fusion.49
  19.7 1.4 fusion.27
  21.4 0.7 fusion.6
  22.1 1.1 fusion.88
  24.1 1.3 multiply_reduce_fusion.1
  25.4 3.5 %stack_reshape.7 = f32[1,2,294912]{2,1,0:T(2,128)} reshape(f32[2,16,18432]{2,1,0:T(8,128)S(1)} %get-tuple-element.12) | data formatting | bytes 4718592 | tf_op jit(solution)/shard_map/stack;reshape | solution.py:66
  28.9 2.5 multiply_reduce_fusion.3
  31.4 3.4 %stack_reshape.6 = f32[1,2,294912]{2,1,0:T(2,128)} reshape(f32[2,16,18432]{2,1,0:T(8,128)S(1)} %get-tuple-element.11) | data formatting | bytes 4718592 | tf_op jit(solution)/shard_map/stack;reshape | solution.py:66
  34.8 4.1 %constant_dynamic-update-slice_fusion.1 = f32[2,2,294912]{2,1,0:T(2,128)} fusion(f32[1,2,294912]{2,1,0:T(2,128)} %stack_reshape.6), kind=kLoop, calls=%fused_computation.81 | loop fusion | bytes 4718592
  38.9 1.9 constant_dynamic-update-slice_fusion
  40.8 35.9 %all-reduce = (f32[1]{0:T(128)}, f32[1]{0:T(128)}) all-reduce(f32[1]{0:T(128)} %bitcast.23, f32[1]{0:T(128)} %bitcast.22), channel_id=1, replica_groups=mesh['groups'=2,'ex'=16] {'ex'}, use_global_device_ids=true, to_apply=%region_3.0 | all-reduce | flops 2 | bytes 16 | tf_op jit(solution)/shard_map/psum | solution.py:65
  76.7 1.4 fusion.82
  78.1 23.1 %fusion.89 = f32[2,2,2]{2,1,0:T(2,128)S(1)} fusion(f32[2,2,294912]{2,1,0:T(2,128)} %constant_dynamic-update-slice_fusion, bf16[2,2,294912]{2,1,0:T(2,128)(2,1)} %all-gather.2.cloned.1.call-done), kind=kOutput, calls=%fused_computation.95 | convolution fusion | flops 28311552 | bytes 7077920 | tf_op jit(solution)/shard_map/lep,lvp->lev/dot_general | solution.py:70
  101.2 22.6 %fusion.79 = f32[2,2,294912]{2,1,0:T(2,128)} fusion(f32[2,2,294912]{2,1,0:T(2,128)} %constant_dynamic-update-slice_fusion, f32[2,2,2]{2,1,0:T(2,128)S(1)} %fusion.89, f32[2,2]{1,0:T(2,128)S(1)} %maximum_add_fusion), kind=kOutput, calls=%fused_computation.82 | convolution fusion | flops 28311560 | bytes 9437232 | tf_op jit(solution)/shard_map/lev,lep->lvp/dot_general | solution.py:77
  123.8 114.4 %all-reduce.3.cloned.1.call-done = f32[2,2,294912]{2,1,0:T(2,128)} async-done(((f32[2,2,294912]{2,1,0:T(2,128)}), f32[2,2,294912]{2,1,0:T(2,128)}) %all-reduce.3.cloned.1.call-update) | async-done | bytes 4718608 | tf_op jit(solution)/shard_map/psum | solution.py:78
  238.2 41.6 %fusion.32 = f32[2,2]{1,0:T(2,128)S(1)} fusion(f32[2,2,2]{2,1,0:T(2,128)S(1)} %fusion.89, f32[2,2,294912]{2,1,0:T(2,128)} %constant_dynamic-update-slice_fusion, f32[2,2,294912]{2,1,0:T(2,128)} %all-reduce.3.cloned.1.call-done, f32[2]{0:T(128)S(1)} %fusion.82), kind=kOutput, calls=%fused_computation.27 | convolution fusion | flops 28311580 | bytes 9437240 | tf_op jit(solution)/shard_map/lep,lvp->lev/dot_general | solution.py:79
  (19 shorter events, 2.1 us)
Async XLA Ops:
  6.5 71.6 %all-gather.2.cloned.1.call-start = ((), (), s32[]{:S(2)}) async-start(), calls=%async_computation | async-start | bytes 2506752 | tf_op jit(solution)/shard_map/all_gather | solution.py:73
  7.3 231.0 %all-reduce.3.cloned.1.call-start = ((), (), s32[]{:S(2)}) async-start(), calls=%async_computation.1 | async-start | bytes 9437184 | tf_op jit(solution)/shard_map/psum | solution.py:78
  8.6 10.2 %copy-start.3 = (bf16[2,2,128,1024]{3,2,1,0:T(8,128)(2,1)S(1)}, bf16[2,2,128,1024]{3,2,1,0:T(8,128)(2,1)}, u32[]{:S(2)}) copy-start(bf16[2,2,128,1024]{3,2,1,0:T(8,128)(2,1)} %param.10) | copy-start | bytes 3145732
  11.3 7.4 %copy-start.2 = (bf16[2,2,128,1024]{3,2,1,0:T(8,128)(2,1)S(1)}, bf16[2,2,128,1024]{3,2,1,0:T(8,128)(2,1)}, u32[]{:S(2)}) copy-start(bf16[2,2,128,1024]{3,2,1,0:T(8,128)(2,1)} %param.11) | copy-start | bytes 3145732
  13.4 6.2 %copy-start.1 = (bf16[2,2,128,8192]{3,2,1,0:T(8,128)(2,1)S(1)}, bf16[2,2,128,8192]{3,2,1,0:T(8,128)(2,1)}, u32[]{:S(2)}) copy-start(bf16[2,2,128,8192]{3,2,1,0:T(8,128)(2,1)} %param.9) | copy-start | bytes 25165828
  34.8 4.1 %copy-start = (f32[1,2,294912]{2,1,0:T(2,128)S(1)}, f32[1,2,294912]{2,1,0:T(2,128)}, u32[]{:S(2)}) copy-start(f32[1,2,294912]{2,1,0:T(2,128)} %stack_reshape.7) | copy-start | bytes 7077892
Sparse Core Ops, SparseCore 0:
  9.6 44.9 all-gather.1
  124.0 114.2 all-reduce.2
where the time goes:
time: 288 us; the launch traced here: 287 us
  waiting for transfers between devices  115 us (40%)
  matrix products  101 us (35%)
  blocking collectives  35.9 us (12%)
  local copies, waits for them, and re-layouts  15.5 us (5%)
  between operations  13.5 us (5%)
  other arithmetic  6.64 us (2%)
    psum x1, waiting for transfers between devices, local(): summed = lax.psum(directions, 'ex')  114 us
    dot_general x1, matrix products, local(): jnp.einsum('lep,lvp->lev', all_gradients, summed, precision=highest)  41.6 us
    psum x1, blocking collectives, local(): total_list.append(lax.psum(jnp.sum(squares), 'ex'))  35.9 us
    dot_general x1, matrix products, local(): jnp.einsum('lep,lvp->lev', all_gradients, lax.all_gather(validation, 'ex'...  23.1 us
    dot_general x1, matrix products, local(): jnp.einsum('lev,lep->lvp', weights, all_gradients, precision=highest)  22.6 us
    another operation x3, local copies, waits for them, and re-layouts, local(): all_gradients = jnp.stack(gradient_list)  8.76 us
  transfers between devices with their start and end apart: 2, of which 1 were waited for; matrix products, arithmetic and copies ran while one was open for 12% of the time, Pallas kernels for 0%

commit v1 on v0

v1 whole, which is shorter than its diff:
```python
import functools

import jax
import jax.numpy as jnp
from jax import lax
from jax.experimental import pallas as pl
from jax.experimental.pallas import tpu as pltpu
from jax.sharding import PartitionSpec as P

F32 = jnp.float32
BF16 = jnp.bfloat16
NN = (((1,), (0,)), ((), ()))
NT = (((1,), (1,)), ((), ()))
LANES = 128
VMEM_BYTES = 40 * 1024 * 1024


def general_local(inputs, grad_key, grad_value, key_down, key_up, value_down, value_up, validation, lengths):
    highest = lax.Precision.HIGHEST
    num_layers, local_examples, seq_slots, _ = inputs.shape
    total_count = lax.axis_size("ex") * local_examples
    low_rank = key_down.shape[1]
    token_mask = (
        lax.broadcasted_iota(jnp.int32, (local_examples, seq_slots), 1) < lengths[:, None]
    ).astype(F32)
    dot = functools.partial(jnp.einsum, preferred_element_type=F32)

    def masked(values):
        return (values * token_mask[None, :, :, None]).astype(BF16)

    z_key = masked(dot("lesd,lrd->lesr", inputs, key_down))
    z_value = masked(dot("lesd,lrd->lesr", inputs, value_down))
    y_key = masked(dot("leso,lor->lesr", grad_key, key_up))
    y_value = masked(dot("leso,lor->lesr", grad_value, value_up))
    pieces = [
        dot("lesr,lesd->lerd", y_key, inputs),
        dot("lesr,leso->lero", z_key, grad_key),
        dot("lesr,lesd->lerd", y_value, inputs),
        dot("lesr,leso->lero", z_value, grad_value),
    ]
    gradients = jnp.concatenate(pieces, axis=3).reshape(num_layers, local_examples, -1)
    squares = jnp.sum(gradients * gradients, axis=2)
    damping = 0.1 * lax.psum(jnp.sum(squares, axis=1), "ex") / total_count + 1e-06
    targets = lax.all_gather(validation, "ex", axis=2, tiled=True).astype(F32)
    products = jnp.einsum("lep,lvp->lev", gradients, targets, precision=highest)
    weights = products / (damping[:, None, None] + squares[:, :, None])
    directions = jnp.einsum("lev,lep->lvp", weights, gradients, precision=highest)
    summed = lax.psum(directions, "ex")
    correction = jnp.einsum("lep,lvp->lev", gradients, summed, precision=highest)
    inner = products - correction / total_count
    return -jnp.sum(inner / damping[:, None, None], axis=0)


CORE, Y, Z1, Z2 = 1, 2, 4, 8
ORDERS = ((Y, Z1), (Z1, Y))


def slot_bits(layer, position):
    first, second = ORDERS[layer]
    return (position >> 2 & 1) * first + (position >> 1 & 1) * second + (position & 1) * Z2


def swap(values, bit):
    size = lax.axis_size("ex")
    return lax.ppermute(values, "ex", [(index, index ^ bit) for index in range(size)])


def fold_lanes(values):
    tiles = [values[:, at : at + LANES] for at in range(0, values.shape[1], LANES)]
    while len(tiles) > 1:
        tiles = [sum(tiles[at : at + 2]) for at in range(0, len(tiles), 2)]
    return tiles[0]


def gradient_kernel(
    scalars, x_ref, gk_ref, gv_ref, ak_ref, av_ref, bk_ref, bv_ref, own_ref, other_ref, square_ref, *, chunk
):
    layer, example = pl.program_id(0), pl.program_id(1)
    index = scalars[0]
    rank = ak_ref.shape[1]
    seq, width = x_ref.shape[2:]
    narrow = gk_ref.shape[3]
    half = rank // 2
    row = lax.broadcasted_iota(jnp.int32, (2 * rank, 2 * rank), 0)
    column = lax.broadcasted_iota(jnp.int32, (2 * rank, 2 * rank), 1)
    position = row % half
    high, low, last = position // 4, position // 2 % 2, position % 2
    is_first = (layer == 0).astype(jnp.int32)
    first_bit = ORDERS[0][0] * is_first + ORDERS[1][0] * (1 - is_first)
    second_bit = ORDERS[0][1] * is_first + ORDERS[1][1] * (1 - is_first)
    relative = high * first_bit + low * second_bit + last * Z2 + row // half % 2
    wanted = jnp.bitwise_xor(relative, jnp.broadcast_to(index, relative.shape)) + row // rank * rank
    order = (column == wanted).astype(F32).astype(BF16)
    mask = (lax.broadcasted_iota(jnp.int32, (1, seq), 1) < scalars[1 + example]).astype(F32)

    def finish(values):
        rounded = (values * mask).astype(BF16)
        return lax.dot_general(order, rounded, NN, preferred_element_type=F32).astype(BF16)

    factor = jnp.concatenate([ak_ref[0], av_ref[0]], axis=0)
    z = finish(lax.dot_general(factor, x_ref[0, 0], NT, preferred_element_type=F32))
    y_key = lax.dot_general(bk_ref[0], gk_ref[0, 0], NT, preferred_element_type=F32)
    y_value = lax.dot_general(bv_ref[0], gv_ref[0, 0], NT, preferred_element_type=F32)
    y = finish(jnp.concatenate([y_key, y_value], axis=0))
    total = jnp.zeros((half, LANES), F32)

    def store(values, at):
        columns = values.shape[1]
        own_ref[0, 0, :, at : at + columns] = values[:half]
        other_ref[0, 0, :, at : at + columns] = values[half:]
        squared = values * values
        return fold_lanes(squared[:half] + squared[half:])

    for at in range(0, width, chunk):
        down = lax.dot_general(y, x_ref[0, 0, :, at : at + chunk], NN, preferred_element_type=F32)
        total += store(down[:rank], at)
        total += store(down[rank:], width + narrow + at)
    up_key = lax.dot_general(z[:rank], gk_ref[0, 0], NN, preferred_element_type=F32)
    total += store(up_key, width)
    up_value = lax.dot_general(z[rank:], gv_ref[0, 0], NN, preferred_element_type=F32)
    total += store(up_value, 2 * width + narrow)
    square_ref[0, 0] = total


def gradients_of(scalars, inputs, grad_key, grad_value, key_down, key_up, value_down, value_up):
    layers, examples, seq, width = inputs.shape
    narrow = grad_key.shape[3]
    rank = key_down.shape[1]
    half = rank // 2
    row_width = 2 * (width + narrow)
    per_example = lambda layer, example, _: (layer, example, 0, 0)
    per_layer = lambda layer, example, _: (layer, 0, 0)
    grad_spec = pl.BlockSpec((1, 1, seq, narrow), per_example)
    down_spec = pl.BlockSpec((1, rank, width), per_layer)
    up_spec = pl.BlockSpec((1, rank, narrow), per_layer)
    row_spec = pl.BlockSpec((1, 1, half, row_width), per_example)
    rows = jax.ShapeDtypeStruct((layers, examples, half, row_width), F32)
    return pl.pallas_call(
        functools.partial(gradient_kernel, chunk=1024),
        grid_spec=pltpu.PrefetchScalarGridSpec(
            num_scalar_prefetch=1,
            grid=(layers, examples),
            in_specs=[
                pl.BlockSpec((1, 1, seq, width), per_example),
                grad_spec,
                grad_spec,
                down_spec,
                down_spec,
                up_spec,
                up_spec,
            ],
            out_specs=[row_spec, row_spec, pl.BlockSpec((1, 1, half, LANES), per_example)],
        ),
        out_shape=[rows, rows, jax.ShapeDtypeStruct((layers, examples, half, LANES), F32)],
        compiler_params=pltpu.CompilerParams(vmem_limit_bytes=VMEM_BYTES),
        cost_estimate=pl.CostEstimate(flops=1 << 32, bytes_accessed=1 << 24, transcendentals=0),
        name="gradients",
    )(
        scalars,
        inputs,
        grad_key,
        grad_value,
        key_down,
        value_down,
        jnp.swapaxes(key_up, 1, 2),
        jnp.swapaxes(value_up, 1, 2),
    )


def dots_kernel(own_ref, received_ref, *refs, sources):
    target_refs, out_ref, rows, total = refs[:-3], refs[-3], refs[-2], refs[-1]
    at = 0
    for ref in target_refs:
        values = ref[...].reshape(ref.shape[-2:]).astype(F32)
        count = values.shape[0] // 2
        rows[0, at : at + count] = values[:count]
        rows[1, at : at + count] = values[count:]
        at += count
    parts = []
    for ref in (own_ref, received_ref):
        for example in range(2):
            gradient = ref[0, example]
            for target in range(2):
                parts.append(fold_lanes(gradient * rows[target]))

    @pl.when(pl.program_id(0) == 0)
    def _():
        total[...] = jnp.zeros_like(total)

    for number, part in enumerate(parts):
        total[number] += part

    @pl.when(pl.program_id(0) == pl.num_programs(0) - 1)
    def _():
        out_ref[...] = jnp.sum(total[...], axis=1)


def dots_of(layer, own, received, targets, columns):
    _, examples, half, row_width = own.shape
    row_spec = pl.BlockSpec((1, examples, half, columns), lambda at: (layer, 0, 0, at))
    specs = []
    for target in targets:
        if target.ndim == 3:
            specs.append(pl.BlockSpec((1, target.shape[1], columns), lambda at: (layer, 0, at)))
        else:
            specs.append(pl.BlockSpec((target.shape[0], columns), lambda at: (0, at)))
    return pl.pallas_call(
        functools.partial(dots_kernel, sources=len(targets)),
        grid=(row_width // columns,),
        in_specs=[row_spec, row_spec] + specs,
        out_specs=pl.BlockSpec((4 * examples, LANES), lambda at: (0, 0)),
        out_shape=jax.ShapeDtypeStruct((4 * examples, LANES), F32),
        scratch_shapes=[pltpu.VMEM((2, half, columns), F32), pltpu.VMEM((4 * examples, half, LANES), F32)],
        compiler_params=pltpu.CompilerParams(vmem_limit_bytes=VMEM_BYTES),
        cost_estimate=pl.CostEstimate(flops=1 << 22, bytes_accessed=3 << 20, transcendentals=0),
        name="dots",
    )(own, received, *targets)


def directions_kernel(
    products_ref, pair_ref, squares_ref, pair_squares_ref, norms_ref, own_ref, received_ref, keep_ref, send_ref, *, count, layer
):
    mine, pair = products_ref[...], pair_ref[...]
    half = mine.shape[0] // 2
    products = mine + jnp.concatenate([pair[half:], pair[:half]], axis=0)
    damping = 0.1 * jnp.sum(norms_ref[layer : layer + 1], axis=1, keepdims=True) / count + 1e-06
    parts = [None, None]
    for number in range(4):
        source = squares_ref if number < 2 else pair_squares_ref
        row = 2 * layer + number % 2
        square = jnp.sum(source[row : row + 1], axis=1, keepdims=True)
        gradient = (own_ref if number < 2 else received_ref)[0, number % 2]
        for target in range(2):
            at = 2 * number + target
            weight = jnp.sum(products[at : at + 1], axis=1, keepdims=True) / (damping + square)
            term = weight * gradient
            parts[target] = term if parts[target] is None else parts[target] + term
    for block, ref in enumerate((keep_ref, send_ref)):
        pieces = []
        for at in (4 * block, 4 * block + 2):
            pieces += [parts[0][at : at + 2], parts[1][at : at + 2]]
        ref[...] = jnp.concatenate(pieces, axis=0).astype(ref.dtype)


def directions_of(layer, products, pair, squares, pair_squares, norms, own, received, count, columns):
    _, examples, half, row_width = own.shape
    row_spec = pl.BlockSpec((1, examples, half, columns), lambda at: (layer, 0, 0, at))
    out_spec = pl.BlockSpec((half, columns), lambda at: (0, at))
    whole = [pl.BlockSpec(array.shape, lambda at: (0, 0)) for array in (products, pair, squares, pair_squares, norms)]
    return pl.pallas_call(
        functools.partial(directions_kernel, count=count, layer=layer),
        grid=(row_width // columns,),
        in_specs=whole + [row_spec, row_spec],
        out_specs=[out_spec, out_spec],
        out_shape=[
            jax.ShapeDtypeStruct((half, row_width), F32),
            jax.ShapeDtypeStruct((half, row_width), BF16),
        ],
        compiler_params=pltpu.CompilerParams(vmem_limit_bytes=VMEM_BYTES),
        cost_estimate=pl.CostEstimate(flops=1 << 22, bytes_accessed=3 << 20, transcendentals=0),
        name="directions",
    )(products, pair, squares, pair_squares, norms, own, received)


def halve_kernel(keep_ref, arrived_ref, rest_ref, send_ref):
    total = keep_ref[...] + arrived_ref[...].astype(F32)
    rest_ref[...] = total[:4]
    send_ref[...] = total[4:].astype(BF16)


def turn_kernel(keep_ref, arrived_ref, rest_ref, send_ref):
    total = keep_ref[...] + arrived_ref[...].astype(F32)
    rest_ref[...] = total
    send_ref[...] = jnp.concatenate([total[1:2], total[0:1], total[3:4], total[2:3]], axis=0).astype(BF16)


def add_call(kernel, keep, arrived, rows):
    width = keep.shape[1]
    return pl.pallas_call(
        kernel,
        out_shape=[jax.ShapeDtypeStruct((rows, width), F32), jax.ShapeDtypeStruct((rows, width), BF16)],
        compiler_params=pltpu.CompilerParams(vmem_limit_bytes=VMEM_BYTES),
        cost_estimate=pl.CostEstimate(flops=1 << 18, bytes_accessed=1 << 20, transcendentals=0),
        name="add",
    )(keep, arrived)


def paired_local(inputs, grad_key, grad_value, key_down, key_up, value_down, value_up, validation, lengths):
    layers, examples = inputs.shape[:2]
    count = lax.axis_size("ex") * examples
    index = lax.axis_index("ex").astype(jnp.int32)
    columns = 4608

    targets = {0: validation}
    for bit in (Y, Z1, Z2):
        targets[bit] = swap(validation, bit)
    scalars = jnp.concatenate([index[None], lengths])
    own, other, square_parts = gradients_of(
        scalars, inputs, grad_key, grad_value, key_down, key_up, value_down, value_up
    )
    received = swap(other, CORE)
    targets[Y | Z1] = swap(targets[Z1], Y)
    targets[Y | Z2] = swap(targets[Z2], Y)
    targets[Z1 | Z2] = swap(targets[Z2], Z1)
    targets[Y | Z1 | Z2] = swap(targets[Z1 | Z2], Y)

    squares = jnp.sum(square_parts, axis=2).reshape(layers * examples, LANES)
    pair_squares = swap(squares, CORE)
    norms = jnp.sum((squares + pair_squares).reshape(layers, examples, LANES), axis=1)
    for bit in (Y, Z1, Z2):
        norms = norms + swap(norms, bit)

    products, corrections = [], []
    for layer in range(layers):
        ordered = [targets[slot_bits(layer, position)] for position in range(8)]
        products.append(dots_of(layer, own, received, ordered, columns))
    pairs = [swap(value, CORE) for value in products]
    for layer, (first, second) in enumerate(ORDERS):
        keep, send = directions_of(
            layer, products[layer], pairs[layer], squares, pair_squares, norms, own, received, count, columns
        )
        keep, send = add_call(halve_kernel, keep, swap(send, first), 4)
        keep, send = add_call(turn_kernel, keep, swap(send, second), 4)
        block = (keep + swap(send, Z2).astype(F32)).astype(BF16)
        from_second = swap(block, second)
        blocks = [block, from_second, swap(block, first), swap(from_second, first)]
        corrections.append(dots_of(layer, own, received, blocks, columns))
    mine = jnp.stack(products) - jnp.stack(corrections) / count
    split = 2 * examples
    inner = mine[:, :split] + swap(mine[:, split:], CORE)
    damping = 0.1 * jnp.sum(norms, axis=1) / count + 1e-06
    scores = -jnp.sum(jnp.sum(inner, axis=2) / damping[:, None], axis=0)
    return scores.reshape(examples, 2)


def solution(mesh):
    in_specs = (
        P(None, ("groups", "ex"), None, None),
        P(None, ("groups", "ex"), None, None),
        P(None, ("groups", "ex"), None, None),
        P(),
        P(),
        P(),
        P(),
        P(None, "groups", "ex"),
        P(("groups", "ex")),
    )
    out_specs = P(("groups", "ex"), None)

    def local(*arguments):
        low_rank = arguments[3].shape[1]
        paired = lax.axis_size("ex") == low_rank == 16 and arguments[0].shape[:2] == (2, 2)
        return (paired_local if paired else general_local)(*arguments)

    return jax.shard_map(local, mesh=mesh, in_specs=in_specs, out_specs=out_specs, check_vma=False)
```

time: 288 us -> 112 us (0.39)
  matrix products: 101 us -> 0 us
  waiting for transfers between devices: 115 us -> 48.1 us
  blocking collectives: 35.9 us -> 0 us
  starting transfers between devices: 0.04 us -> 28.7 us
  Pallas kernels: 0 us -> 26.3 us
  between operations: 13.5 us -> 0.19 us
  local copies, waits for them, and re-layouts: 15.5 us -> 6.87 us
  other arithmetic: 6.64 us -> 1.24 us
    psum x1 -> x0, waiting for transfers between devices: 114 us -> none  [local(): summed = lax.psum(directions, 'ex')]
    dot_general x15 -> x0, matrix products: 101 us -> none  [the longest x1 41.6 us: local(): jnp.einsum('lep,lvp->lev', all_gradients, summed, precision=highest)]
    ppermute x0 -> x27, waiting for transfers between devices: none -> 48.1 us  [swap(): lax.ppermute(values, 'ex', [(index, index ^ bit) for index in range(size)])]
    psum x1 -> x0, blocking collectives: 35.9 us -> none  [local(): total_list.append(lax.psum(jnp.sum(squares), 'ex'))]
    ppermute x0 -> x27, starting transfers between devices: none -> 28.7 us  [swap(): lax.ppermute(values, 'ex', [(index, index ^ bit) for index in range(size)])]
    pallas_call x0 -> x11, Pallas kernels: none -> 26.3 us  [the longest x4 10.5 us: dots_of(): pl.pallas_call(functools.partial(dots_kernel, sources=len(targets)), grid...]
    another operation x3 -> x0, local copies, waits for them, and re-layouts: 8.76 us -> none  [local(): all_gradients = jnp.stack(gradient_list)]
    reduce_sum x2 -> x5, other arithmetic: 3.89 us -> 0.33 us  [the longest x2 0.17 us: paired_local(): scores = -jnp.sum(jnp.sum(inner, axis=2) / damping[:, None], axis=0)]
  transfers between devices with their start and end apart: 2 -> 27, of which waited for: 1 -> 20; matrix products, arithmetic and copies ran while one was open for 12% -> 0% of each run, Pallas kernels for 0% -> 10%
where the time goes in v1:
time: 112 us; the launch traced here: 111 us
  waiting for transfers between devices  48.1 us (43%)
  starting transfers between devices  28.7 us (26%)
  Pallas kernels  26.3 us (23%)
  local copies, waits for them, and re-layouts  6.87 us (6%)
  other arithmetic  1.24 us (1%)
    ppermute x27, waiting for transfers between devices, swap(): lax.ppermute(values, 'ex', [(index, index ^ bit) for index in range(size)])  48.1 us
    ppermute x27, starting transfers between devices, swap(): lax.ppermute(values, 'ex', [(index, index ^ bit) for index in range(size)])  28.7 us
    pallas_call x4, Pallas kernels, dots_of(): pl.pallas_call(functools.partial(dots_kernel, sources=len(targets)), grid...  10.5 us
    pallas_call x1, Pallas kernels, gradients_of(): pl.pallas_call(functools.partial(gradient_kernel, chunk=1024), grid_spec=...  9.42 us
    unnamed x14, local copies, waits for them, and re-layouts  6.21 us
    pallas_call x2, Pallas kernels, directions_of(): pl.pallas_call(functools.partial(directions_kernel, count=count, layer=la...  5.87 us
  transfers between devices with their start and end apart: 27, of which 20 were waited for; matrix products, arithmetic and copies ran while one was open for 0% of the time, Pallas kernels for 10%

profile of v1, /device:TPU:0, one launch (start us, length us, event | category | flops | bytes accessed | tf_op | source)
XLA Modules:
  0.0 111.5 jit_solution(10231177648749414905)
XLA Ops:
  6.9 9.4 %gradients.1 = (f32[2,2,8,18432]{3,2,1,0:T(8,128)S(1)}, f32[2,2,8,18432]{3,2,1,0:T(8,128)}, f32[2,2,8,128]{3,2,1,0:T(8,128)S(1)}) custom-call(s32[3]{0:T(128)S(1)} %pad_add_fusion.scalars, bf16[2,2,128,8192]{3,2,1,0:T(8,128)(2,1)} %x_ref.1, bf16[2,2,128,1024]{3,2,1,0:T(8,128)(2,1)S(1)} %copy-done.1, bf16[2,2,128,1024]{3,2,1,0:T(8,128)(2,1)S(1)} %copy-done.2, ...), custom_call_target="tpu_custom_call" | custom-call | flops 4294967296 | bytes 16777216 | tf_op jit(solution)/shard_map/gradients/pallas_call | solution.py:138
  16.8 3.6 %collective-permute-start.1 = (bf16[2,2,18432]{2,1,0:T(2,128)(2,1)S(1)}, bf16[2,2,18432]{2,1,0:T(2,128)(2,1)S(1)}, u32[]{:S(2)}, u32[]{:S(2)}) collective-permute-start(bf16[2,2,18432]{2,1,0:T(2,128)(2,1)S(1)} %copy-done), channel_id=1, source_target_pairs={{0,8},{1,9},{2,10},{3,11},{4,12},{5,13},{6,14},{7,15},{8,0},{9,1},... | collective-permute-start | bytes 442376 | tf_op jit(solution)/shard_map/ppermute | solution.py:65
  20.4 1.6 %collective-permute-start.2 = (bf16[2,2,18432]{2,1,0:T(2,128)(2,1)S(1)}, bf16[2,2,18432]{2,1,0:T(2,128)(2,1)S(1)}, u32[]{:S(2)}, u32[]{:S(2)}) collective-permute-start(bf16[2,2,18432]{2,1,0:T(2,128)(2,1)S(1)} %copy-done), channel_id=1, source_target_pairs={{0,4},{1,5},{2,6},{3,7},{4,0},{5,1},{6,2},{7,3},{8,12},{9,13},{10,... | collective-permute-start | bytes 442376 | tf_op jit(solution)/shard_map/ppermute | solution.py:65
  22.0 6.2 %collective-permute-done.1.refs_1_ = bf16[2,2,18432]{2,1,0:T(2,128)(2,1)S(1)} collective-permute-done((bf16[2,2,18432]{2,1,0:T(2,128)(2,1)S(1)}, bf16[2,2,18432]{2,1,0:T(2,128)(2,1)S(1)}, u32[]{:S(2)}, u32[]{:S(2)}) %collective-permute-start.1) | collective-permute-done | bytes 147488 | tf_op jit(solution)/shard_map/ppermute | solution.py:65
  31.7 2.0 %collective-permute-done.10 = f32[2,128]{1,0:T(2,128)S(1)} collective-permute-done((f32[2,128]{1,0:T(2,128)S(1)}, f32[2,128]{1,0:T(2,128)S(1)}, u32[]{:S(2)}, u32[]{:S(2)}) %collective-permute-start.10) | collective-permute-done | bytes 1056 | tf_op jit(solution)/shard_map/ppermute | solution.py:65
  41.9 2.3 %collective-permute-start.12 = (f32[2,128]{1,0:T(2,128)S(1)}, f32[2,128]{1,0:T(2,128)S(1)}, u32[]{:S(2)}, u32[]{:S(2)}) collective-permute-start(f32[2,128]{1,0:T(2,128)S(1)} %add.34), channel_id=1, source_target_pairs={{0,8},{1,9},{2,10},{3,11},{4,12},{5,13},{6,14},{7,15},{8,0},{9,1},... | collective-permute-start | bytes 3080 | tf_op jit(solution)/shard_map/ppermute | solution.py:65
  45.1 2.7 %collective-permute-done.6.refs_6_ = bf16[2,2,18432]{2,1,0:T(2,128)(2,1)S(1)} collective-permute-done((bf16[2,2,18432]{2,1,0:T(2,128)(2,1)S(1)}, bf16[2,2,18432]{2,1,0:T(2,128)(2,1)S(1)}, u32[]{:S(2)}, u32[]{:S(2)}) %collective-permute-start.6) | collective-permute-done | bytes 147488 | tf_op jit(solution)/shard_map/ppermute | solution.py:65
  47.8 1.6 %collective-permute-done.7.refs_7_ = bf16[2,2,18432]{2,1,0:T(2,128)(2,1)S(1)} collective-permute-done((bf16[2,2,18432]{2,1,0:T(2,128)(2,1)S(1)}, bf16[2,2,18432]{2,1,0:T(2,128)(2,1)S(1)}, u32[]{:S(2)}, u32[]{:S(2)}) %collective-permute-start.7) | collective-permute-done | bytes 147488 | tf_op jit(solution)/shard_map/ppermute | solution.py:65
  49.4 2.6 %dots.4.products_ref = f32[8,128]{1,0:T(8,128)S(1)} custom-call(f32[2,2,8,18432]{3,2,1,0:T(8,128)S(1)} %get-tuple-element.20.own_ref, f32[2,2,8,18432]{3,2,1,0:T(8,128)} %collective-permute-done.received_ref, bf16[2,2,18432]{2,1,0:T(2,128)(2,1)S(1)} %copy-done, bf16[2,2,18432]{2,1,0:T(2,128)(2,1)S(1)} %collective-permute-done.1.refs_1_, ...), custom_call_target="tpu_custom_call" | custom-call | flops 4194304 | bytes 3145728 | tf_op jit(solution)/shard_map/dots/pallas_call | solution.py:207
  53.2 2.9 %directions.2 = (f32[8,18432]{1,0:T(8,128)S(1)}, bf16[8,18432]{1,0:T(8,128)(2,1)S(1)}) custom-call(f32[8,128]{1,0:T(8,128)S(1)} %dots.4.products_ref, f32[8,128]{1,0:T(8,128)S(1)} %collective-permute-done.8.pair_ref, f32[4,128]{1,0:T(4,128)S(1)} %bitcast.13, f32[4,128]{1,0:T(4,128)S(1)} %collective-permute-done.9.pair_squares_ref, ...), custom_call_target="tpu_custom_call" | custom-call | flops 4194304 | bytes 3145728 | tf_op jit(solution)/shard_map/directions/pallas_call | solution.py:250
  56.2 1.6 %collective-permute-start.13 = (bf16[8,18432]{1,0:T(8,128)(2,1)S(1)}, bf16[8,18432]{1,0:T(8,128)(2,1)S(1)}, u32[]{:S(2)}, u32[]{:S(2)}) collective-permute-start(bf16[8,18432]{1,0:T(8,128)(2,1)S(1)} %get-tuple-element.24), channel_id=1, source_target_pairs={{0,2},{1,3},{2,0},{3,1},{4,6},{5,7},{6,4},{7,5},{8,10},{9,11},{10,... | collective-permute-start | bytes 884744 | tf_op jit(solution)/shard_map/ppermute | solution.py:65
  57.8 2.6 %dots.5.products_ref = f32[8,128]{1,0:T(8,128)S(1)} custom-call(f32[2,2,8,18432]{3,2,1,0:T(8,128)S(1)} %get-tuple-element.20.own_ref, f32[2,2,8,18432]{3,2,1,0:T(8,128)} %collective-permute-done.received_ref, bf16[2,2,18432]{2,1,0:T(2,128)(2,1)S(1)} %copy-done, bf16[2,2,18432]{2,1,0:T(2,128)(2,1)S(1)} %collective-permute-done.1.refs_1_, ...), custom_call_target="tpu_custom_call" | custom-call | flops 4194304 | bytes 3145728 | tf_op jit(solution)/shard_map/dots/pallas_call | solution.py:207
  61.7 2.9 %directions.3 = (f32[8,18432]{1,0:T(8,128)S(1)}, bf16[8,18432]{1,0:T(8,128)(2,1)S(1)}) custom-call(f32[8,128]{1,0:T(8,128)S(1)} %dots.5.products_ref, f32[8,128]{1,0:T(8,128)S(1)} %collective-permute-done.19.pair_ref, f32[4,128]{1,0:T(4,128)S(1)} %bitcast.14, f32[4,128]{1,0:T(4,128)S(1)} %collective-permute-done.9.pair_squares_ref, ...), custom_call_target="tpu_custom_call" | custom-call | flops 4194304 | bytes 3145728 | tf_op jit(solution)/shard_map/directions/pallas_call | solution.py:250
  66.8 7.7 %collective-permute-done.20.arrived_ref = bf16[8,18432]{1,0:T(8,128)(2,1)S(1)} collective-permute-done((bf16[8,18432]{1,0:T(8,128)(2,1)S(1)}, bf16[8,18432]{1,0:T(8,128)(2,1)S(1)}, u32[]{:S(2)}, u32[]{:S(2)}) %collective-permute-start.20) | collective-permute-done | bytes 294944 | tf_op jit(solution)/shard_map/ppermute | solution.py:65
  75.1 1.8 %collective-permute-done.14.arrived_ref = bf16[4,18432]{1,0:T(4,128)(2,1)S(1)} collective-permute-done((bf16[4,18432]{1,0:T(4,128)(2,1)S(1)}, bf16[4,18432]{1,0:T(4,128)(2,1)S(1)}, u32[]{:S(2)}, u32[]{:S(2)}) %collective-permute-start.14) | collective-permute-done | bytes 147488 | tf_op jit(solution)/shard_map/ppermute | solution.py:65
  77.1 2.3 %collective-permute-start.15 = (bf16[4,18432]{1,0:T(4,128)(2,1)S(1)}, bf16[4,18432]{1,0:T(4,128)(2,1)S(1)}, u32[]{:S(2)}, u32[]{:S(2)}) collective-permute-start(bf16[4,18432]{1,0:T(4,128)(2,1)S(1)} %get-tuple-element.28), channel_id=1, source_target_pairs={{0,8},{1,9},{2,10},{3,11},{4,12},{5,13},{6,14},{7,15},{8,0},{9,1},... | collective-permute-start | bytes 442376 | tf_op jit(solution)/shard_map/ppermute | solution.py:65
  80.0 2.3 %collective-permute-start.22 = (bf16[4,18432]{1,0:T(4,128)(2,1)S(1)}, bf16[4,18432]{1,0:T(4,128)(2,1)S(1)}, u32[]{:S(2)}, u32[]{:S(2)}) collective-permute-start(bf16[4,18432]{1,0:T(4,128)(2,1)S(1)} %get-tuple-element.34), channel_id=1, source_target_pairs={{0,8},{1,9},{2,10},{3,11},{4,12},{5,13},{6,14},{7,15},{8,0},{9,1},... | collective-permute-start | bytes 442376 | tf_op jit(solution)/shard_map/ppermute | solution.py:65
  82.3 8.0 %collective-permute-done.15 = bf16[4,18432]{1,0:T(4,128)(2,1)S(1)} collective-permute-done((bf16[4,18432]{1,0:T(4,128)(2,1)S(1)}, bf16[4,18432]{1,0:T(4,128)(2,1)S(1)}, u32[]{:S(2)}, u32[]{:S(2)}) %collective-permute-start.15) | collective-permute-done | bytes 147488 | tf_op jit(solution)/shard_map/ppermute | solution.py:65
  90.5 2.2 %collective-permute-done.22 = bf16[4,18432]{1,0:T(4,128)(2,1)S(1)} collective-permute-done((bf16[4,18432]{1,0:T(4,128)(2,1)S(1)}, bf16[4,18432]{1,0:T(4,128)(2,1)S(1)}, u32[]{:S(2)}, u32[]{:S(2)}) %collective-permute-start.22) | collective-permute-done | bytes 147488 | tf_op jit(solution)/shard_map/ppermute | solution.py:65
  96.3 3.4 %collective-permute-done.23.refs_1_ = bf16[4,18432]{1,0:T(4,128)(2,1)S(1)} collective-permute-done((bf16[4,18432]{1,0:T(4,128)(2,1)S(1)}, bf16[4,18432]{1,0:T(4,128)(2,1)S(1)}, u32[]{:S(2)}, u32[]{:S(2)}) %collective-permute-start.23) | collective-permute-done | bytes 147488 | tf_op jit(solution)/shard_map/ppermute | solution.py:65
  99.8 2.6 %collective-permute-done.17.refs_2_ = bf16[4,18432]{1,0:T(4,128)(2,1)S(1)} collective-permute-done((bf16[4,18432]{1,0:T(4,128)(2,1)S(1)}, bf16[4,18432]{1,0:T(4,128)(2,1)S(1)}, u32[]{:S(2)}, u32[]{:S(2)}) %collective-permute-start.17) | collective-permute-done | bytes 147488 | tf_op jit(solution)/shard_map/ppermute | solution.py:65
  102.5 1.6 %collective-permute-done.18.refs_3_ = bf16[4,18432]{1,0:T(4,128)(2,1)S(1)} collective-permute-done((bf16[4,18432]{1,0:T(4,128)(2,1)S(1)}, bf16[4,18432]{1,0:T(4,128)(2,1)S(1)}, u32[]{:S(2)}, u32[]{:S(2)}) %collective-permute-start.18) | collective-permute-done | bytes 147488 | tf_op jit(solution)/shard_map/ppermute | solution.py:65
  104.1 2.6 %dots.6 = f32[8,128]{1,0:T(8,128)S(1)} custom-call(f32[2,2,8,18432]{3,2,1,0:T(8,128)S(1)} %get-tuple-element.20.own_ref, f32[2,2,8,18432]{3,2,1,0:T(8,128)} %collective-permute-done.received_ref, bf16[4,18432]{1,0:T(4,128)(2,1)S(1)} %add_convert_fusion.1.refs_0_, bf16[4,18432]{1,0:T(4,128)(2,1)S(1)} %collective-permute-done.16.refs_1_, ...), custom_call_target="tpu_custom_call" | custom-call | flops 4194304 | bytes 3145728 | tf_op jit(solution)/shard_map/dots/pallas_call | solution.py:207
  106.7 2.6 %dots.7 = f32[8,128]{1,0:T(8,128)S(1)} custom-call(f32[2,2,8,18432]{3,2,1,0:T(8,128)S(1)} %get-tuple-element.20.own_ref, f32[2,2,8,18432]{3,2,1,0:T(8,128)} %collective-permute-done.received_ref, bf16[4,18432]{1,0:T(4,128)(2,1)S(1)} %add_convert_fusion.refs_0_, bf16[4,18432]{1,0:T(4,128)(2,1)S(1)} %collective-permute-done.23.refs_1_, ...), custom_call_target="tpu_custom_call" | custom-call | flops 4194304 | bytes 3145728 | tf_op jit(solution)/shard_map/dots/pallas_call | solution.py:207
  (71 shorter events, 31.8 us)
Async XLA Ops:
  16.4 33.0 %collective-permute-start = (f32[2,2,8,18432]{3,2,1,0:T(8,128)}, f32[2,2,8,18432]{3,2,1,0:T(8,128)}, u32[]{:S(2)}, u32[]{:S(2)}) collective-permute-start(f32[2,2,8,18432]{3,2,1,0:T(8,128)} %get-tuple-element.21), channel_id=1, source_target_pairs={{0,1},{1,0},{2,3},{3,2},{4,5},{5,4},{6,7},{7,6},{8,9},{9,8},{10,11... | collective-permute-start | bytes 7077896 | tf_op jit(solution)/shard_map/ppermute | solution.py:65
  16.8 11.4 %collective-permute-start.1 = (bf16[2,2,18432]{2,1,0:T(2,128)(2,1)S(1)}, bf16[2,2,18432]{2,1,0:T(2,128)(2,1)S(1)}, u32[]{:S(2)}, u32[]{:S(2)}) collective-permute-start(bf16[2,2,18432]{2,1,0:T(2,128)(2,1)S(1)} %copy-done), channel_id=1, source_target_pairs={{0,8},{1,9},{2,10},{3,11},{4,12},{5,13},{6,14},{7,15},{8,0},{9,1},... | collective-permute-start | bytes 442376 | tf_op jit(solution)/shard_map/ppermute | solution.py:65
  20.4 18.4 %collective-permute-start.2 = (bf16[2,2,18432]{2,1,0:T(2,128)(2,1)S(1)}, bf16[2,2,18432]{2,1,0:T(2,128)(2,1)S(1)}, u32[]{:S(2)}, u32[]{:S(2)}) collective-permute-start(bf16[2,2,18432]{2,1,0:T(2,128)(2,1)S(1)} %copy-done), channel_id=1, source_target_pairs={{0,4},{1,5},{2,6},{3,7},{4,0},{5,1},{6,2},{7,3},{8,12},{9,13},{10,... | collective-permute-start | bytes 442376 | tf_op jit(solution)/shard_map/ppermute | solution.py:65
  28.2 11.1 %collective-permute-start.3 = (bf16[2,2,18432]{2,1,0:T(2,128)(2,1)S(1)}, bf16[2,2,18432]{2,1,0:T(2,128)(2,1)S(1)}, u32[]{:S(2)}, u32[]{:S(2)}) collective-permute-start(bf16[2,2,18432]{2,1,0:T(2,128)(2,1)S(1)} %collective-permute-done.1.refs_1_), channel_id=1, source_target_pairs={{0,4},{1,5},{2,6},{3,7},{4,0},{5,1},{6,2},{7,3},{8,12},{9,13},{10,... | collective-permute-start | bytes 442376 | tf_op jit(solution)/shard_map/ppermute | solution.py:65
  30.1 3.6 %collective-permute-start.10 = (f32[2,128]{1,0:T(2,128)S(1)}, f32[2,128]{1,0:T(2,128)S(1)}, u32[]{:S(2)}, u32[]{:S(2)}) collective-permute-start(f32[2,128]{1,0:T(2,128)S(1)} %reduce_sum.46), channel_id=1, source_target_pairs={{0,2},{1,3},{2,0},{3,1},{4,6},{5,7},{6,4},{7,5},{8,10},{9,11},{10,... | collective-permute-start | bytes 3080 | tf_op jit(solution)/shard_map/ppermute | solution.py:65
  33.7 3.6 %collective-permute-start.11 = (f32[2,128]{1,0:T(2,128)S(1)}, f32[2,128]{1,0:T(2,128)S(1)}, u32[]{:S(2)}, u32[]{:S(2)}) collective-permute-start(f32[2,128]{1,0:T(2,128)S(1)} %add.33), channel_id=1, source_target_pairs={{0,4},{1,5},{2,6},{3,7},{4,0},{5,1},{6,2},{7,3},{8,12},{9,13},{10,... | collective-permute-start | bytes 3080 | tf_op jit(solution)/shard_map/ppermute | solution.py:65
  35.1 6.8 %collective-permute-start.4 = (bf16[2,2,18432]{2,1,0:T(2,128)(2,1)S(1)}, bf16[2,2,18432]{2,1,0:T(2,128)(2,1)S(1)}, u32[]{:S(2)}, u32[]{:S(2)}) collective-permute-start(bf16[2,2,18432]{2,1,0:T(2,128)(2,1)S(1)} %copy-done), channel_id=1, source_target_pairs={{0,2},{1,3},{2,0},{3,1},{4,6},{5,7},{6,4},{7,5},{8,10},{9,11},{10,... | collective-permute-start | bytes 442376 | tf_op jit(solution)/shard_map/ppermute | solution.py:65
  37.3 7.8 %collective-permute-start.5 = (bf16[2,2,18432]{2,1,0:T(2,128)(2,1)S(1)}, bf16[2,2,18432]{2,1,0:T(2,128)(2,1)S(1)}, u32[]{:S(2)}, u32[]{:S(2)}) collective-permute-start(bf16[2,2,18432]{2,1,0:T(2,128)(2,1)S(1)} %collective-permute-done.1.refs_1_), channel_id=1, source_target_pairs={{0,2},{1,3},{2,0},{3,1},{4,6},{5,7},{6,4},{7,5},{8,10},{9,11},{10,... | collective-permute-start | bytes 442376 | tf_op jit(solution)/shard_map/ppermute | solution.py:65
  38.8 9.0 %collective-permute-start.6 = (bf16[2,2,18432]{2,1,0:T(2,128)(2,1)S(1)}, bf16[2,2,18432]{2,1,0:T(2,128)(2,1)S(1)}, u32[]{:S(2)}, u32[]{:S(2)}) collective-permute-start(bf16[2,2,18432]{2,1,0:T(2,128)(2,1)S(1)} %collective-permute-done.2.refs_2_.refs_4_), channel_id=1, source_target_pairs={{0,2},{1,3},{2,0},{3,1},{4,6},{5,7},{6,4},{7,5},{8,10},{9,11},{10,... | collective-permute-start | bytes 442376 | tf_op jit(solution)/shard_map/ppermute | solution.py:65
  39.3 10.1 %collective-permute-start.7 = (bf16[2,2,18432]{2,1,0:T(2,128)(2,1)S(1)}, bf16[2,2,18432]{2,1,0:T(2,128)(2,1)S(1)}, u32[]{:S(2)}, u32[]{:S(2)}) collective-permute-start(bf16[2,2,18432]{2,1,0:T(2,128)(2,1)S(1)} %collective-permute-done.3.refs_3_.refs_5_), channel_id=1, source_target_pairs={{0,2},{1,3},{2,0},{3,1},{4,6},{5,7},{6,4},{7,5},{8,10},{9,11},{10,... | collective-permute-start | bytes 442376 | tf_op jit(solution)/shard_map/ppermute | solution.py:65
  41.9 10.2 %collective-permute-start.12 = (f32[2,128]{1,0:T(2,128)S(1)}, f32[2,128]{1,0:T(2,128)S(1)}, u32[]{:S(2)}, u32[]{:S(2)}) collective-permute-start(f32[2,128]{1,0:T(2,128)S(1)} %add.34), channel_id=1, source_target_pairs={{0,8},{1,9},{2,10},{3,11},{4,12},{5,13},{6,14},{7,15},{8,0},{9,1},... | collective-permute-start | bytes 3080 | tf_op jit(solution)/shard_map/ppermute | solution.py:65
  52.0 1.2 %collective-permute-start.8 = (f32[8,128]{1,0:T(8,128)S(1)}, f32[8,128]{1,0:T(8,128)S(1)}, u32[]{:S(2)}, u32[]{:S(2)}) collective-permute-start(f32[8,128]{1,0:T(8,128)S(1)} %dots.4.products_ref), channel_id=1, source_target_pairs={{0,1},{1,0},{2,3},{3,2},{4,5},{5,4},{6,7},{7,6},{8,9},{9,8},{10,11... | collective-permute-start | bytes 12296 | tf_op jit(solution)/shard_map/ppermute | solution.py:65
  56.2 9.4 %collective-permute-start.13 = (bf16[8,18432]{1,0:T(8,128)(2,1)S(1)}, bf16[8,18432]{1,0:T(8,128)(2,1)S(1)}, u32[]{:S(2)}, u32[]{:S(2)}) collective-permute-start(bf16[8,18432]{1,0:T(8,128)(2,1)S(1)} %get-tuple-element.24), channel_id=1, source_target_pairs={{0,2},{1,3},{2,0},{3,1},{4,6},{5,7},{6,4},{7,5},{8,10},{9,11},{10,... | collective-permute-start | bytes 884744 | tf_op jit(solution)/shard_map/ppermute | solution.py:65
  64.6 9.9 %collective-permute-start.20 = (bf16[8,18432]{1,0:T(8,128)(2,1)S(1)}, bf16[8,18432]{1,0:T(8,128)(2,1)S(1)}, u32[]{:S(2)}, u32[]{:S(2)}) collective-permute-start(bf16[8,18432]{1,0:T(8,128)(2,1)S(1)} %get-tuple-element.30), channel_id=1, source_target_pairs={{0,4},{1,5},{2,6},{3,7},{4,0},{5,1},{6,2},{7,3},{8,12},{9,13},{10,... | collective-permute-start | bytes 884744 | tf_op jit(solution)/shard_map/ppermute | solution.py:65
  65.7 11.2 %collective-permute-start.14 = (bf16[4,18432]{1,0:T(4,128)(2,1)S(1)}, bf16[4,18432]{1,0:T(4,128)(2,1)S(1)}, u32[]{:S(2)}, u32[]{:S(2)}) collective-permute-start(bf16[4,18432]{1,0:T(4,128)(2,1)S(1)} %get-tuple-element.26), channel_id=1, source_target_pairs={{0,4},{1,5},{2,6},{3,7},{4,0},{5,1},{6,2},{7,3},{8,12},{9,13},{10,... | collective-permute-start | bytes 442376 | tf_op jit(solution)/shard_map/ppermute | solution.py:65
  74.6 5.2 %collective-permute-start.21 = (bf16[4,18432]{1,0:T(4,128)(2,1)S(1)}, bf16[4,18432]{1,0:T(4,128)(2,1)S(1)}, u32[]{:S(2)}, u32[]{:S(2)}) collective-permute-start(bf16[4,18432]{1,0:T(4,128)(2,1)S(1)} %get-tuple-element.32), channel_id=1, source_target_pairs={{0,2},{1,3},{2,0},{3,1},{4,6},{5,7},{6,4},{7,5},{8,10},{9,11},{10,... | collective-permute-start | bytes 442376 | tf_op jit(solution)/shard_map/ppermute | solution.py:65
  77.1 13.3 %collective-permute-start.15 = (bf16[4,18432]{1,0:T(4,128)(2,1)S(1)}, bf16[4,18432]{1,0:T(4,128)(2,1)S(1)}, u32[]{:S(2)}, u32[]{:S(2)}) collective-permute-start(bf16[4,18432]{1,0:T(4,128)(2,1)S(1)} %get-tuple-element.28), channel_id=1, source_target_pairs={{0,8},{1,9},{2,10},{3,11},{4,12},{5,13},{6,14},{7,15},{8,0},{9,1},... | collective-permute-start | bytes 442376 | tf_op jit(solution)/shard_map/ppermute | solution.py:65
  80.0 12.7 %collective-permute-start.22 = (bf16[4,18432]{1,0:T(4,128)(2,1)S(1)}, bf16[4,18432]{1,0:T(4,128)(2,1)S(1)}, u32[]{:S(2)}, u32[]{:S(2)}) collective-permute-start(bf16[4,18432]{1,0:T(4,128)(2,1)S(1)} %get-tuple-element.34), channel_id=1, source_target_pairs={{0,8},{1,9},{2,10},{3,11},{4,12},{5,13},{6,14},{7,15},{8,0},{9,1},... | collective-permute-start | bytes 442376 | tf_op jit(solution)/shard_map/ppermute | solution.py:65
  90.4 5.3 %collective-permute-start.16 = (bf16[4,18432]{1,0:T(4,128)(2,1)S(1)}, bf16[4,18432]{1,0:T(4,128)(2,1)S(1)}, u32[]{:S(2)}, u32[]{:S(2)}) collective-permute-start(bf16[4,18432]{1,0:T(4,128)(2,1)S(1)} %add_convert_fusion.1.refs_0_), channel_id=1, source_target_pairs={{0,4},{1,5},{2,6},{3,7},{4,0},{5,1},{6,2},{7,3},{8,12},{9,13},{10,... | collective-permute-start | bytes 442376 | tf_op jit(solution)/shard_map/ppermute | solution.py:65
  92.8 6.9 %collective-permute-start.23 = (bf16[4,18432]{1,0:T(4,128)(2,1)S(1)}, bf16[4,18432]{1,0:T(4,128)(2,1)S(1)}, u32[]{:S(2)}, u32[]{:S(2)}) collective-permute-start(bf16[4,18432]{1,0:T(4,128)(2,1)S(1)} %add_convert_fusion.refs_0_), channel_id=1, source_target_pairs={{0,2},{1,3},{2,0},{3,1},{4,6},{5,7},{6,4},{7,5},{8,10},{9,11},{10,... | collective-permute-start | bytes 442376 | tf_op jit(solution)/shard_map/ppermute | solution.py:65
  93.3 9.1 %collective-permute-start.17 = (bf16[4,18432]{1,0:T(4,128)(2,1)S(1)}, bf16[4,18432]{1,0:T(4,128)(2,1)S(1)}, u32[]{:S(2)}, u32[]{:S(2)}) collective-permute-start(bf16[4,18432]{1,0:T(4,128)(2,1)S(1)} %add_convert_fusion.1.refs_0_), channel_id=1, source_target_pairs={{0,2},{1,3},{2,0},{3,1},{4,6},{5,7},{6,4},{7,5},{8,10},{9,11},{10,... | collective-permute-start | bytes 442376 | tf_op jit(solution)/shard_map/ppermute | solution.py:65
  95.8 8.3 %collective-permute-start.18 = (bf16[4,18432]{1,0:T(4,128)(2,1)S(1)}, bf16[4,18432]{1,0:T(4,128)(2,1)S(1)}, u32[]{:S(2)}, u32[]{:S(2)}) collective-permute-start(bf16[4,18432]{1,0:T(4,128)(2,1)S(1)} %collective-permute-done.16.refs_1_), channel_id=1, source_target_pairs={{0,2},{1,3},{2,0},{3,1},{4,6},{5,7},{6,4},{7,5},{8,10},{9,11},{10,... | collective-permute-start | bytes 442376 | tf_op jit(solution)/shard_map/ppermute | solution.py:65
  96.2 10.5 %collective-permute-start.24 = (bf16[4,18432]{1,0:T(4,128)(2,1)S(1)}, bf16[4,18432]{1,0:T(4,128)(2,1)S(1)}, u32[]{:S(2)}, u32[]{:S(2)}) collective-permute-start(bf16[4,18432]{1,0:T(4,128)(2,1)S(1)} %add_convert_fusion.refs_0_), channel_id=1, source_target_pairs={{0,4},{1,5},{2,6},{3,7},{4,0},{5,1},{6,2},{7,3},{8,12},{9,13},{10,... | collective-permute-start | bytes 442376 | tf_op jit(solution)/shard_map/ppermute | solution.py:65
  99.7 7.1 %collective-permute-start.25 = (bf16[4,18432]{1,0:T(4,128)(2,1)S(1)}, bf16[4,18432]{1,0:T(4,128)(2,1)S(1)}, u32[]{:S(2)}, u32[]{:S(2)}) collective-permute-start(bf16[4,18432]{1,0:T(4,128)(2,1)S(1)} %collective-permute-done.23.refs_1_), channel_id=1, source_target_pairs={{0,4},{1,5},{2,6},{3,7},{4,0},{5,1},{6,2},{7,3},{8,12},{9,13},{10,... | collective-permute-start | bytes 442376 | tf_op jit(solution)/shard_map/ppermute | solution.py:65
  (10 other events, 19.8 us)

commit v2 on v1

v2 whole, which is shorter than its diff:
```python
import functools

import jax
import jax.numpy as jnp
from jax import lax
from jax.experimental import pallas as pl
from jax.experimental.pallas import tpu as pltpu
from jax.sharding import PartitionSpec as P

F32 = jnp.float32
BF16 = jnp.bfloat16
NN = (((1,), (0,)), ((), ()))
NT = (((1,), (1,)), ((), ()))
LANES = 128
GRADIENT_VMEM = 18 * 1024 * 1024
SMALL_VMEM = 6 * 1024 * 1024


def general_local(inputs, grad_key, grad_value, key_down, key_up, value_down, value_up, validation, lengths):
    highest = lax.Precision.HIGHEST
    num_layers, local_examples, seq_slots, _ = inputs.shape
    total_count = lax.axis_size("ex") * local_examples
    low_rank = key_down.shape[1]
    token_mask = (
        lax.broadcasted_iota(jnp.int32, (local_examples, seq_slots), 1) < lengths[:, None]
    ).astype(F32)
    dot = functools.partial(jnp.einsum, preferred_element_type=F32)

    def masked(values):
        return (values * token_mask[None, :, :, None]).astype(BF16)

    z_key = masked(dot("lesd,lrd->lesr", inputs, key_down))
    z_value = masked(dot("lesd,lrd->lesr", inputs, value_down))
    y_key = masked(dot("leso,lor->lesr", grad_key, key_up))
    y_value = masked(dot("leso,lor->lesr", grad_value, value_up))
    pieces = [
        dot("lesr,lesd->lerd", y_key, inputs),
        dot("lesr,leso->lero", z_key, grad_key),
        dot("lesr,lesd->lerd", y_value, inputs),
        dot("lesr,leso->lero", z_value, grad_value),
    ]
    gradients = jnp.concatenate(pieces, axis=3).reshape(num_layers, local_examples, -1)
    squares = jnp.sum(gradients * gradients, axis=2)
    damping = 0.1 * lax.psum(jnp.sum(squares, axis=1), "ex") / total_count + 1e-06
    targets = lax.all_gather(validation, "ex", axis=2, tiled=True).astype(F32)
    products = jnp.einsum("lep,lvp->lev", gradients, targets, precision=highest)
    weights = products / (damping[:, None, None] + squares[:, :, None])
    directions = jnp.einsum("lev,lep->lvp", weights, gradients, precision=highest)
    summed = lax.psum(directions, "ex")
    correction = jnp.einsum("lep,lvp->lev", gradients, summed, precision=highest)
    inner = products - correction / total_count
    return -jnp.sum(inner / damping[:, None, None], axis=0)


CORE, Y, Z1, Z2 = 1, 2, 4, 8
ORDERS = ((Y, Z1), (Z1, Y))


def slot_bits(layer, position):
    first, second = ORDERS[layer]
    return (position >> 2 & 1) * first + (position >> 1 & 1) * second + (position & 1) * Z2


def swap(values, bit):
    size = lax.axis_size("ex")
    return lax.ppermute(values, "ex", [(index, index ^ bit) for index in range(size)])


def fold_lanes(values):
    tiles = [values[:, at : at + LANES] for at in range(0, values.shape[1], LANES)]
    while len(tiles) > 1:
        tiles = [sum(tiles[at : at + 2]) for at in range(0, len(tiles), 2)]
    return tiles[0]


def gradient_kernel(
    index_ref, lengths_ref, x_hbm, gk_hbm, gv_hbm, ak_hbm, av_hbm, bk_hbm, bv_hbm, *refs, layer, after, chunk
):
    own_ref, other_ref, square_ref, x_ref, gk_ref, gv_ref, a_ref, b_ref, semaphores = refs[after:]
    examples, seq, width = x_ref.shape
    narrow = gk_ref.shape[2]
    rank = bk_hbm.shape[1]
    half = rank // 2
    copies = {}

    def start(name, source, target):
        copies[name] = pltpu.make_async_copy(source, target, semaphores.at[len(copies)])
        copies[name].start()

    start("bk", bk_hbm.at[layer], b_ref.at[0])
    start("bv", bv_hbm.at[layer], b_ref.at[1])
    start("gk", gk_hbm.at[layer], gk_ref)
    start("gv", gv_hbm.at[layer], gv_ref)
    start("ak", ak_hbm.at[layer], a_ref.at[0])
    start("av", av_hbm.at[layer], a_ref.at[1])
    for at in range(0, width, chunk):
        columns = pl.ds(at, chunk)
        start(("x", at), x_hbm.at[layer, :, :, columns], x_ref.at[:, :, columns])

    row = lax.broadcasted_iota(jnp.int32, (2 * rank, 2 * rank), 0)
    column = lax.broadcasted_iota(jnp.int32, (2 * rank, 2 * rank), 1)
    position = row % half
    first_bit, second_bit = ORDERS[layer]
    relative = position // 4 * first_bit + position // 2 % 2 * second_bit + position % 2 * Z2 + row // half % 2
    wanted = jnp.bitwise_xor(relative, jnp.broadcast_to(index_ref[0], relative.shape)) + row // rank * rank
    order = (column == wanted).astype(F32).astype(BF16)
    token = lax.broadcasted_iota(jnp.int32, (1, examples * seq), 1)
    mask = jnp.zeros(token.shape, F32)
    for example in range(examples):
        inside = (token >= example * seq) & (token < example * seq + lengths_ref[example])
        mask = jnp.where(inside, 1.0, mask)
    own_tokens = [slice(example * seq, (example + 1) * seq) for example in range(examples)]
    totals = [jnp.zeros((half, LANES), F32) for _ in range(examples)]

    def finish(values):
        rounded = (values * mask).astype(BF16)
        return lax.dot_general(order, rounded, NN, preferred_element_type=F32).astype(BF16)

    def store(example, values, at):
        columns = values.shape[1]
        own_ref[example, :, at : at + columns] = values[:half]
        other_ref[example, :, at : at + columns] = values[half:]
        squared = values * values
        totals[example] += fold_lanes(squared[:half] + squared[half:])

    for name in ("bk", "bv", "gk", "gv"):
        copies[name].wait()
    grad_key = gk_ref[...].reshape(examples * seq, narrow)
    grad_value = gv_ref[...].reshape(examples * seq, narrow)
    y_key = lax.dot_general(b_ref[0], grad_key, NT, preferred_element_type=F32)
    y_value = lax.dot_general(b_ref[1], grad_value, NT, preferred_element_type=F32)
    y = finish(jnp.concatenate([y_key, y_value], axis=0))
    copies["ak"].wait()
    copies["av"].wait()
    z = jnp.zeros((2 * rank, examples * seq), F32)
    for at in range(0, width, chunk):
        copies["x", at].wait()
        columns = slice(at, at + chunk)
        x = x_ref[:, :, columns].reshape(examples * seq, chunk)
        factor = jnp.concatenate([a_ref[0, :, columns], a_ref[1, :, columns]], axis=0)
        z += lax.dot_general(factor, x, NT, preferred_element_type=F32)
        for example, tokens in enumerate(own_tokens):
            down = lax.dot_general(y[:, tokens], x_ref[example, :, columns], NN, preferred_element_type=F32)
            store(example, down[:rank], at)
            store(example, down[rank:], width + narrow + at)
    z = finish(z)
    for example, tokens in enumerate(own_tokens):
        up_key = lax.dot_general(z[:rank, tokens], gk_ref[example], NN, preferred_element_type=F32)
        store(example, up_key, width)
        up_value = lax.dot_general(z[rank:, tokens], gv_ref[example], NN, preferred_element_type=F32)
        store(example, up_value, 2 * width + narrow)
        square_ref[example : example + 1] = jnp.sum(totals[example], axis=0, keepdims=True)


IN_VMEM = pl.BlockSpec(memory_space=pltpu.VMEM)
ANYWHERE = pl.BlockSpec(memory_space=pl.ANY)
COLUMNS = 1024


def in_hbm(array):
    return pltpu.with_memory_space_constraint(array, pltpu.HBM)


def gradients_of(layer, index, lengths, inputs, grad_key, grad_value, key_down, key_up, value_down, value_up, after=()):
    _, examples, seq, width = inputs.shape
    narrow = grad_key.shape[3]
    rank = key_down.shape[1]
    row_width = 2 * (width + narrow)
    chunk = 2048
    copies = 6 + width // chunk
    rows = jax.ShapeDtypeStruct((examples, rank // 2, row_width), F32)
    return pl.pallas_call(
        functools.partial(gradient_kernel, layer=layer, after=len(after), chunk=chunk),
        in_specs=[pl.BlockSpec(memory_space=pltpu.SMEM)] * 2 + [ANYWHERE] * (7 + len(after)),
        out_specs=[IN_VMEM] * 3,
        out_shape=[rows, rows, jax.ShapeDtypeStruct((examples, LANES), F32)],
        scratch_shapes=[
            pltpu.VMEM((examples, seq, width), BF16),
            pltpu.VMEM((examples, seq, narrow), BF16),
            pltpu.VMEM((examples, seq, narrow), BF16),
            pltpu.VMEM((2, rank, width), BF16),
            pltpu.VMEM((2, rank, narrow), BF16),
            pltpu.SemaphoreType.DMA((copies,)),
        ],
        compiler_params=pltpu.CompilerParams(vmem_limit_bytes=GRADIENT_VMEM),
        cost_estimate=pl.CostEstimate(flops=1 << 32, bytes_accessed=1 << 24, transcendentals=0),
        name="gradients",
    )(
        index,
        lengths,
        in_hbm(inputs),
        in_hbm(grad_key),
        in_hbm(grad_value),
        in_hbm(key_down),
        in_hbm(value_down),
        in_hbm(jnp.swapaxes(key_up, 1, 2)),
        in_hbm(jnp.swapaxes(value_up, 1, 2)),
        *after,
    )


def chunks(ref):
    def run(body, init):
        def step(number, carry):
            return body(pl.ds(pl.multiple_of(number * COLUMNS, COLUMNS), COLUMNS), carry)

        return lax.fori_loop(0, ref.shape[-1] // COLUMNS, step, init)

    return run


def dots_kernel(*refs, layers, groups, started):
    out_ref = refs[-1]
    at = 2 * layers
    for layer in range(layers):
        own_ref, received_ref = refs[2 * layer : 2 * layer + 2]
        target_refs = refs[at : at + len(groups[layer])]
        at += len(groups[layer])
        slots = own_ref.shape[1]

        def body(columns, totals):
            pieces, filled = ([], []), 0
            for start, ref in sorted(zip(groups[layer], target_refs), key=lambda pair: pair[0]):
                index = (layer, slice(None), columns) if len(ref.shape) == 3 else (slice(None), columns)
                values = ref[index].astype(F32)
                count = values.shape[0] // 2
                for target in range(2):
                    if start > filled:
                        pieces[target].append(jnp.zeros((start - filled, values.shape[1]), F32))
                    pieces[target].append(values[target * count : (target + 1) * count])
                filled = start + count
            if filled < slots:
                for target in range(2):
                    pieces[target].append(jnp.zeros((slots - filled, COLUMNS), F32))
            rows = [jnp.concatenate(group, axis=0) for group in pieces]
            updated = []
            for number, total in enumerate(totals):
                gradient = (own_ref if number < 4 else received_ref)[number // 2 % 2, :, columns]
                updated.append(total + fold_lanes(gradient * rows[number % 2]))
            return tuple(updated)

        zero = jnp.zeros((slots, LANES), F32)
        totals = chunks(own_ref)(body, (zero,) * 8)
        for number, total in enumerate(totals):
            row = layer * 8 + number
            value = jnp.sum(total, axis=0, keepdims=True)
            out_ref[row : row + 1] = value + refs[-2][row : row + 1] if started else value


def dots_of(rows, targets, start=None):
    layers = len(rows)
    flat = [array for pair in rows for array in pair] + [array for group in targets for array in group.values()]
    flat += [] if start is None else [start]
    return pl.pallas_call(
        functools.partial(
            dots_kernel, layers=layers, groups=[tuple(group) for group in targets], started=start is not None
        ),
        in_specs=[IN_VMEM] * len(flat),
        out_specs=IN_VMEM,
        out_shape=jax.ShapeDtypeStruct((8 * layers, LANES), F32),
        compiler_params=pltpu.CompilerParams(vmem_limit_bytes=SMALL_VMEM),
        cost_estimate=pl.CostEstimate(flops=1 << 22, bytes_accessed=3 << 20, transcendentals=0),
        name="dots",
    )(*flat)


def directions_kernel(
    products_ref, pair_ref, squares_ref, pair_squares_ref, norm_ref, own_ref, received_ref, keep_ref, send_ref, *, count, layer
):
    mine, pair = products_ref[8 * layer : 8 * layer + 8], pair_ref[8 * layer : 8 * layer + 8]
    products = mine + jnp.concatenate([pair[4:], pair[:4]], axis=0)
    damping = 0.1 * jnp.sum(norm_ref[layer : layer + 1], axis=1, keepdims=True) / count + 1e-06
    weights = []
    for number in range(4):
        source = squares_ref if number < 2 else pair_squares_ref
        row = 2 * layer + number % 2
        scale = damping + jnp.sum(source[row : row + 1], axis=1, keepdims=True)
        for target in range(2):
            at = 2 * number + target
            weights.append(jnp.sum(products[at : at + 1], axis=1, keepdims=True) / scale)

    def body(columns, carry):
        gradients = [ref[example, :, columns] for ref in (own_ref, received_ref) for example in range(2)]
        parts = [sum(weights[2 * number + target] * gradients[number] for number in range(4)) for target in range(2)]
        for block, ref in enumerate((keep_ref, send_ref)):
            pieces = []
            for at in (4 * block, 4 * block + 2):
                pieces += [parts[0][at : at + 2], parts[1][at : at + 2]]
            ref[:, columns] = jnp.concatenate(pieces, axis=0).astype(ref.dtype)
        return carry

    chunks(own_ref)(body, 0)


def directions_of(layer, products, pair, squares, pair_squares, norms, own, received, count):
    _, half, row_width = own.shape
    return pl.pallas_call(
        functools.partial(directions_kernel, count=count, layer=layer),
        in_specs=[IN_VMEM] * 7,
        out_specs=[IN_VMEM] * 2,
        out_shape=[
            jax.ShapeDtypeStruct((half, row_width), F32),
            jax.ShapeDtypeStruct((half, row_width), BF16),
        ],
        compiler_params=pltpu.CompilerParams(vmem_limit_bytes=SMALL_VMEM),
        cost_estimate=pl.CostEstimate(flops=1 << 22, bytes_accessed=3 << 20, transcendentals=0),
        name="directions",
    )(products, pair, squares, pair_squares, norms, own, received)


def halve_kernel(keep_ref, arrived_ref, rest_ref, send_ref):
    total = keep_ref[...] + arrived_ref[...].astype(F32)
    rest_ref[...] = total[:4]
    send_ref[...] = total[4:].astype(BF16)


def turn_kernel(keep_ref, arrived_ref, rest_ref, send_ref):
    total = keep_ref[...] + arrived_ref[...].astype(F32)
    rest_ref[...] = total
    send_ref[...] = jnp.concatenate([total[1:2], total[0:1], total[3:4], total[2:3]], axis=0).astype(BF16)


def add_call(kernel, keep, arrived, rows):
    width = keep.shape[1]
    return pl.pallas_call(
        kernel,
        out_shape=[jax.ShapeDtypeStruct((rows, width), F32), jax.ShapeDtypeStruct((rows, width), BF16)],
        compiler_params=pltpu.CompilerParams(vmem_limit_bytes=SMALL_VMEM),
        cost_estimate=pl.CostEstimate(flops=1 << 18, bytes_accessed=1 << 20, transcendentals=0),
        name="add",
    )(keep, arrived)


def paired_local(inputs, grad_key, grad_value, key_down, key_up, value_down, value_up, validation, lengths):
    layers, examples = inputs.shape[:2]
    count = lax.axis_size("ex") * examples
    index = lax.axis_index("ex").astype(jnp.int32)[None]
    arguments = (index, lengths, inputs, grad_key, grad_value, key_down, key_up, value_down, value_up)

    targets = {0: validation}
    for bit in (Z2, Y, Z1):
        targets[bit] = swap(validation, bit)
    rows, parts = [], []
    for layer in range(layers):
        after = [targets[bit] for bit in (Z2, Y, Z1)] if layer else []
        own, other, square_parts = gradients_of(layer, *arguments, after=after)
        rows.append((own, swap(other, CORE)))
        parts.append(square_parts)
    targets[Y | Z2] = swap(targets[Z2], Y)
    targets[Z1 | Z2] = swap(targets[Z2], Z1)
    targets[Y | Z1] = swap(targets[Z1], Y)
    targets[Y | Z1 | Z2] = swap(targets[Y | Z2], Z1)

    squares = jnp.concatenate(parts)
    pair_squares = swap(squares, CORE)
    norms = squares + pair_squares
    norms = jnp.stack([norms[0] + norms[1], norms[2] + norms[3]])
    for bit in (Y, Z1, Z2):
        norms = norms + swap(norms, bit)

    slots = [[slot_bits(layer, position) for position in range(8)] for layer in range(layers)]
    early = [{at: targets[slot] for at, slot in enumerate(row) if slot != Y | Z1 | Z2} for row in slots]
    late = [{at: targets[slot] for at, slot in enumerate(row) if slot == Y | Z1 | Z2} for row in slots]
    products = dots_of(rows, late, dots_of(rows, early))
    pair = swap(products, CORE)
    early, late = [], []
    for layer, (first, second) in enumerate(ORDERS):
        keep, send = directions_of(layer, products, pair, squares, pair_squares, norms, *rows[layer], count)
        keep, send = add_call(halve_kernel, keep, swap(send, first), 4)
        keep, send = add_call(turn_kernel, keep, swap(send, second), 4)
        block = (keep + swap(send, Z2).astype(F32)).astype(BF16)
        from_second = swap(block, second)
        early.append({0: block, 2: from_second, 4: swap(block, first)})
        late.append({6: swap(from_second, first)})
    corrections = dots_of(rows, late, dots_of(rows, early))
    mine = (products - corrections / count).reshape(layers, 4 * examples, LANES)
    split = 2 * examples
    inner = mine[:, :split] + swap(mine[:, split:], CORE)
    damping = 0.1 * jnp.sum(norms, axis=1) / count + 1e-06
    scores = -jnp.sum(jnp.sum(inner, axis=2) / damping[:, None], axis=0)
    return scores.reshape(examples, 2)


def solution(mesh):
    in_specs = (
        P(None, ("groups", "ex"), None, None),
        P(None, ("groups", "ex"), None, None),
        P(None, ("groups", "ex"), None, None),
        P(),
        P(),
        P(),
        P(),
        P(None, "groups", "ex"),
        P(("groups", "ex")),
    )
    out_specs = P(("groups", "ex"), None)

    def local(*arguments):
        low_rank = arguments[3].shape[1]
        paired = lax.axis_size("ex") == low_rank == 16 and arguments[0].shape[:2] == (2, 2)
        return (paired_local if paired else general_local)(*arguments)

    return jax.shard_map(local, mesh=mesh, in_specs=in_specs, out_specs=out_specs, check_vma=False)
```

time: 112 us -> 84.7 us (0.76)
  waiting for transfers between devices: 48.1 us -> 33.7 us
  Pallas kernels: 26.3 us -> 19.8 us
  local copies, waits for them, and re-layouts: 6.87 us -> 1.32 us
    ppermute x27, waiting for transfers between devices: 48.1 us -> 33.7 us  [swap(): lax.ppermute(values, 'ex', [(index, index ^ bit) for index in range(size)])]
    unnamed x14 -> x4, local copies, waits for them, and re-layouts: 6.21 us -> 0.66 us
    pallas_call x2, Pallas kernels: 5.87 us -> 2.55 us  [directions_of(): pl.pallas_call(functools.partial(directions_kernel, count=count, layer=la...]
    pallas_call x5 -> x6, Pallas kernels: 19.9 us -> 16.7 us  [the longest x2 11.1 us: gradients_of(): pl.pallas_call(functools.partial(gradient_kernel, layer=layer, after=len(...]
  transfers between devices with their start and end apart: 27 -> 27, of which waited for: 20 -> 17; matrix products, arithmetic and copies ran while one was open for 0% -> 0% of each run, Pallas kernels for 10% -> 21%
where the time goes in v2:
time: 84.7 us; the launch traced here: 84.5 us
  waiting for transfers between devices  33.7 us (40%)
  starting transfers between devices  29 us (34%)
  Pallas kernels  19.8 us (23%)
  local copies, waits for them, and re-layouts  1.32 us (2%)
    ppermute x27, waiting for transfers between devices, swap(): lax.ppermute(values, 'ex', [(index, index ^ bit) for index in range(size)])  33.7 us
    ppermute x27, starting transfers between devices, swap(): lax.ppermute(values, 'ex', [(index, index ^ bit) for index in range(size)])  29 us
    pallas_call x2, Pallas kernels, gradients_of(): pl.pallas_call(functools.partial(gradient_kernel, layer=layer, after=len(...  11.1 us
    pallas_call x4, Pallas kernels, dots_of(): pl.pallas_call(functools.partial(dots_kernel, layers=layers, groups=[tupl...  5.55 us
    pallas_call x2, Pallas kernels, directions_of(): pl.pallas_call(functools.partial(directions_kernel, count=count, layer=la...  2.55 us
  transfers between devices with their start and end apart: 27, of which 17 were waited for; matrix products, arithmetic and copies ran while one was open for 0% of the time, Pallas kernels for 21%

profile of v2, /device:TPU:0, one launch (start us, length us, event | category | flops | bytes accessed | tf_op | source)
XLA Modules:
  0.0 84.5 jit_solution(5322327524057634388)
XLA Ops:
  0.0 4.0 %collective-permute-start.1 = (bf16[2,2,18432]{2,1,0:T(2,128)(2,1)}, bf16[2,2,18432]{2,1,0:T(2,128)(2,1)S(1)}, u32[]{:S(2)}, u32[]{:S(2)}) collective-permute-start(bf16[2,2,18432]{2,1,0:T(2,128)(2,1)} %refs_11_.1), channel_id=1, source_target_pairs={{0,8},{1,9},{2,10},{3,11},{4,12},{5,13},{6,14},{7,15},{8,0},{9,1},... | collective-permute-start | bytes 442376 | tf_op jit(solution)/shard_map/ppermute | solution.py:66
  4.0 1.6 %collective-permute-start.3 = (bf16[2,2,18432]{2,1,0:T(2,128)(2,1)}, bf16[2,2,18432]{2,1,0:T(2,128)(2,1)S(1)}, u32[]{:S(2)}, u32[]{:S(2)}) collective-permute-start(bf16[2,2,18432]{2,1,0:T(2,128)(2,1)} %refs_11_.1), channel_id=1, source_target_pairs={{0,4},{1,5},{2,6},{3,7},{4,0},{5,1},{6,2},{7,3},{8,12},{9,13},{10,... | collective-permute-start | bytes 442376 | tf_op jit(solution)/shard_map/ppermute | solution.py:66
  5.6 1.5 %collective-permute-start.2 = (bf16[2,2,18432]{2,1,0:T(2,128)(2,1)}, bf16[2,2,18432]{2,1,0:T(2,128)(2,1)S(1)}, u32[]{:S(2)}, u32[]{:S(2)}) collective-permute-start(bf16[2,2,18432]{2,1,0:T(2,128)(2,1)} %refs_11_.1), channel_id=1, source_target_pairs={{0,2},{1,3},{2,0},{3,1},{4,6},{5,7},{6,4},{7,5},{8,10},{9,11},{10,... | collective-permute-start | bytes 442376 | tf_op jit(solution)/shard_map/ppermute | solution.py:66
  7.8 5.5 %gradients.2 = (f32[2,8,18432]{2,1,0:T(8,128)S(1)}, f32[2,8,18432]{2,1,0:T(8,128)S(1)}, f32[2,128]{1,0:T(2,128)S(1)}) custom-call(s32[1]{0:T(128)} %bitcast.index_ref, s32[2]{0:T(128)S(1)} %copy-done.1, bf16[2,2,128,8192]{3,2,1,0:T(8,128)(2,1)} %x_hbm.3, bf16[2,2,128,1024]{3,2,1,0:T(8,128)(2,1)} %gk_hbm.3, bf16[2,2,128,1024]{3,2,1,0:T(8,128)(2,1)} %gv_hbm.3, ...), custom_call_target="tpu_custom_call" | custom-call | flops 4294967296 | bytes 16777216 | tf_op jit(solution)/shard_map/gradients/pallas_call | solution.py:172
  13.5 5.6 %gradients.3 = (f32[2,8,18432]{2,1,0:T(8,128)S(1)}, f32[2,8,18432]{2,1,0:T(8,128)S(1)}, f32[2,128]{1,0:T(2,128)S(1)}) custom-call(s32[1]{0:T(128)} %bitcast.index_ref, s32[2]{0:T(128)S(1)} %copy-done.1, bf16[2,2,128,8192]{3,2,1,0:T(8,128)(2,1)} %x_hbm.3, bf16[2,2,128,1024]{3,2,1,0:T(8,128)(2,1)} %gk_hbm.3, bf16[2,2,128,1024]{3,2,1,0:T(8,128)(2,1)} %gv_hbm.3, ...), custom_call_target="tpu_custom_call" | custom-call | flops 4294967296 | bytes 16777216 | tf_op jit(solution)/shard_map/gradients/pallas_call | solution.py:172
  19.7 2.4 %collective-permute-done.10.pair_squares_ref = f32[4,128]{1,0:T(4,128)S(1)} collective-permute-done((f32[4,128]{1,0:T(4,128)S(1)}, f32[4,128]{1,0:T(4,128)S(1)}, u32[]{:S(2)}, u32[]{:S(2)}) %collective-permute-start.10) | collective-permute-done | bytes 2080 | tf_op jit(solution)/shard_map/ppermute | solution.py:66
  22.7 1.5 %collective-permute-start.5 = (bf16[2,2,18432]{2,1,0:T(2,128)(2,1)S(1)}, bf16[2,2,18432]{2,1,0:T(2,128)(2,1)S(1)}, u32[]{:S(2)}, u32[]{:S(2)}) collective-permute-start(bf16[2,2,18432]{2,1,0:T(2,128)(2,1)S(1)} %collective-permute-done.1.refs_0_.refs_5_.refs_12_), channel_id=1, source_target_pairs={{0,2},{1,3},{2,0},{3,1},{4,6},{5,7},{6,4},{7,5},{8,10},{9,11},{10,... | collective-permute-start | bytes 442376 | tf_op jit(solution)/shard_map/ppermute | solution.py:66
  24.2 1.5 %collective-permute-done.11 = f32[2,128]{1,0:T(2,128)S(1)} collective-permute-done((f32[2,128]{1,0:T(2,128)S(1)}, f32[2,128]{1,0:T(2,128)S(1)}, u32[]{:S(2)}, u32[]{:S(2)}) %collective-permute-start.11) | collective-permute-done | bytes 1056 | tf_op jit(solution)/shard_map/ppermute | solution.py:66
  26.3 1.6 %collective-permute-start.7 = (bf16[2,2,18432]{2,1,0:T(2,128)(2,1)S(1)}, bf16[2,2,18432]{2,1,0:T(2,128)(2,1)S(1)}, u32[]{:S(2)}, u32[]{:S(2)}) collective-permute-start(bf16[2,2,18432]{2,1,0:T(2,128)(2,1)S(1)} %collective-permute-done.1.refs_0_.refs_5_.refs_12_), channel_id=1, source_target_pairs={{0,4},{1,5},{2,6},{3,7},{4,0},{5,1},{6,2},{7,3},{8,12},{9,13},{10,... | collective-permute-start | bytes 442376 | tf_op jit(solution)/shard_map/ppermute | solution.py:66
  27.8 1.5 %collective-permute-done.12 = f32[2,128]{1,0:T(2,128)S(1)} collective-permute-done((f32[2,128]{1,0:T(2,128)S(1)}, f32[2,128]{1,0:T(2,128)S(1)}, u32[]{:S(2)}, u32[]{:S(2)}) %collective-permute-start.12) | collective-permute-done | bytes 1056 | tf_op jit(solution)/shard_map/ppermute | solution.py:66
  30.4 1.9 %collective-permute-done.7.refs_7_.refs_16_ = bf16[2,2,18432]{2,1,0:T(2,128)(2,1)S(1)} collective-permute-done((bf16[2,2,18432]{2,1,0:T(2,128)(2,1)S(1)}, bf16[2,2,18432]{2,1,0:T(2,128)(2,1)S(1)}, u32[]{:S(2)}, u32[]{:S(2)}) %collective-permute-start.7) | collective-permute-done | bytes 147488 | tf_op jit(solution)/shard_map/ppermute | solution.py:66
  32.3 1.8 %collective-permute-start.13 = (f32[2,128]{1,0:T(2,128)S(1)}, f32[2,128]{1,0:T(2,128)S(1)}, u32[]{:S(2)}, u32[]{:S(2)}) collective-permute-start(f32[2,128]{1,0:T(2,128)S(1)} %fusion.4), channel_id=1, source_target_pairs={{0,8},{1,9},{2,10},{3,11},{4,12},{5,13},{6,14},{7,15},{8,0},{9,1},... | collective-permute-start | bytes 3080 | tf_op jit(solution)/shard_map/ppermute | solution.py:66
  34.5 2.1 %dots.4.refs_6_ = f32[16,128]{1,0:T(8,128)S(1)} custom-call(f32[2,8,18432]{2,1,0:T(8,128)S(1)} %get-tuple-element.23.refs_0_.own_ref, f32[2,8,18432]{2,1,0:T(8,128)S(1)} %collective-permute-done.refs_1_.received_ref, f32[2,8,18432]{2,1,0:T(8,128)S(1)} %get-tuple-element.25.refs_2_.own_ref, f32[2,8,18432]{2,1,0:T(8,128)S(1)} %collective-permute-done.4.refs_3_.received_ref, ...), custom_call_target="tpu_custom_call" | custom-call | flops 4194304 | bytes 3145728 | tf_op jit(solution)/shard_map/dots/pallas_call | solution.py:254
  42.7 6.7 %collective-permute-done.19.arrived_ref = bf16[8,18432]{1,0:T(8,128)(2,1)S(1)} collective-permute-done((bf16[8,18432]{1,0:T(8,128)(2,1)S(1)}, bf16[8,18432]{1,0:T(8,128)(2,1)S(1)}, u32[]{:S(2)}, u32[]{:S(2)}) %collective-permute-start.19) | collective-permute-done | bytes 294944 | tf_op jit(solution)/shard_map/ppermute | solution.py:66
  51.0 2.1 %collective-permute-start.15 = (bf16[4,18432]{1,0:T(4,128)(2,1)S(1)}, bf16[4,18432]{1,0:T(4,128)(2,1)S(1)}, u32[]{:S(2)}, u32[]{:S(2)}) collective-permute-start(bf16[4,18432]{1,0:T(4,128)(2,1)S(1)} %get-tuple-element.32), channel_id=1, source_target_pairs={{0,4},{1,5},{2,6},{3,7},{4,0},{5,1},{6,2},{7,3},{8,12},{9,13},{10,... | collective-permute-start | bytes 442376 | tf_op jit(solution)/shard_map/ppermute | solution.py:66
  53.1 1.6 %collective-permute-done.20.arrived_ref = bf16[4,18432]{1,0:T(4,128)(2,1)S(1)} collective-permute-done((bf16[4,18432]{1,0:T(4,128)(2,1)S(1)}, bf16[4,18432]{1,0:T(4,128)(2,1)S(1)}, u32[]{:S(2)}, u32[]{:S(2)}) %collective-permute-start.20) | collective-permute-done | bytes 147488 | tf_op jit(solution)/shard_map/ppermute | solution.py:66
  54.8 1.6 %collective-permute-start.21 = (bf16[4,18432]{1,0:T(4,128)(2,1)S(1)}, bf16[4,18432]{1,0:T(4,128)(2,1)S(1)}, u32[]{:S(2)}, u32[]{:S(2)}) collective-permute-start(bf16[4,18432]{1,0:T(4,128)(2,1)S(1)} %get-tuple-element.40), channel_id=1, source_target_pairs={{0,8},{1,9},{2,10},{3,11},{4,12},{5,13},{6,14},{7,15},{8,0},{9,1},... | collective-permute-start | bytes 442376 | tf_op jit(solution)/shard_map/ppermute | solution.py:66
  56.6 2.9 %collective-permute-start.16 = (bf16[4,18432]{1,0:T(4,128)(2,1)S(1)}, bf16[4,18432]{1,0:T(4,128)(2,1)S(1)}, u32[]{:S(2)}, u32[]{:S(2)}) collective-permute-start(bf16[4,18432]{1,0:T(4,128)(2,1)S(1)} %get-tuple-element.34), channel_id=1, source_target_pairs={{0,8},{1,9},{2,10},{3,11},{4,12},{5,13},{6,14},{7,15},{8,0},{9,1},... | collective-permute-start | bytes 442376 | tf_op jit(solution)/shard_map/ppermute | solution.py:66
  59.5 8.2 %collective-permute-done.21 = bf16[4,18432]{1,0:T(4,128)(2,1)S(1)} collective-permute-done((bf16[4,18432]{1,0:T(4,128)(2,1)S(1)}, bf16[4,18432]{1,0:T(4,128)(2,1)S(1)}, u32[]{:S(2)}, u32[]{:S(2)}) %collective-permute-start.21) | collective-permute-done | bytes 147488 | tf_op jit(solution)/shard_map/ppermute | solution.py:66
  69.5 2.0 %collective-permute-start.25 = (bf16[4,18432]{1,0:T(4,128)(2,1)S(1)}, bf16[4,18432]{1,0:T(4,128)(2,1)S(1)}, u32[]{:S(2)}, u32[]{:S(2)}) collective-permute-start(bf16[4,18432]{1,0:T(4,128)(2,1)S(1)} %add_convert_fusion.refs_7_), channel_id=1, source_target_pairs={{0,4},{1,5},{2,6},{3,7},{4,0},{5,1},{6,2},{7,3},{8,12},{9,13},{10,... | collective-permute-start | bytes 442376 | tf_op jit(solution)/shard_map/ppermute | solution.py:66
  72.5 1.6 %collective-permute-done.22.refs_8_ = bf16[4,18432]{1,0:T(4,128)(2,1)S(1)} collective-permute-done((bf16[4,18432]{1,0:T(4,128)(2,1)S(1)}, bf16[4,18432]{1,0:T(4,128)(2,1)S(1)}, u32[]{:S(2)}, u32[]{:S(2)}) %collective-permute-start.22) | collective-permute-done | bytes 147488 | tf_op jit(solution)/shard_map/ppermute | solution.py:66
  74.1 2.2 %collective-permute-done.17.refs_5_ = bf16[4,18432]{1,0:T(4,128)(2,1)S(1)} collective-permute-done((bf16[4,18432]{1,0:T(4,128)(2,1)S(1)}, bf16[4,18432]{1,0:T(4,128)(2,1)S(1)}, u32[]{:S(2)}, u32[]{:S(2)}) %collective-permute-start.17) | collective-permute-done | bytes 147488 | tf_op jit(solution)/shard_map/ppermute | solution.py:66
  78.4 1.4 %dots.6.refs_6_ = f32[16,128]{1,0:T(8,128)S(1)} custom-call(f32[2,8,18432]{2,1,0:T(8,128)S(1)} %get-tuple-element.23.refs_0_.own_ref, f32[2,8,18432]{2,1,0:T(8,128)S(1)} %collective-permute-done.refs_1_.received_ref, f32[2,8,18432]{2,1,0:T(8,128)S(1)} %get-tuple-element.25.refs_2_.own_ref, f32[2,8,18432]{2,1,0:T(8,128)S(1)} %collective-permute-done.4.refs_3_.received_ref, ...), custom_call_target="tpu_custom_call" | custom-call | flops 4194304 | bytes 3145728 | tf_op jit(solution)/shard_map/dots/pallas_call | solution.py:254
  80.0 1.4 %collective-permute-done.18.refs_4_ = bf16[4,18432]{1,0:T(4,128)(2,1)S(1)} collective-permute-done((bf16[4,18432]{1,0:T(4,128)(2,1)S(1)}, bf16[4,18432]{1,0:T(4,128)(2,1)S(1)}, u32[]{:S(2)}, u32[]{:S(2)}) %collective-permute-start.18) | collective-permute-done | bytes 147488 | tf_op jit(solution)/shard_map/ppermute | solution.py:66
  (62 shorter events, 20.3 us)
Async XLA Ops:
  0.0 13.4 %collective-permute-start.1 = (bf16[2,2,18432]{2,1,0:T(2,128)(2,1)}, bf16[2,2,18432]{2,1,0:T(2,128)(2,1)S(1)}, u32[]{:S(2)}, u32[]{:S(2)}) collective-permute-start(bf16[2,2,18432]{2,1,0:T(2,128)(2,1)} %refs_11_.1), channel_id=1, source_target_pairs={{0,8},{1,9},{2,10},{3,11},{4,12},{5,13},{6,14},{7,15},{8,0},{9,1},... | collective-permute-start | bytes 442376 | tf_op jit(solution)/shard_map/ppermute | solution.py:66
  4.0 9.4 %collective-permute-start.3 = (bf16[2,2,18432]{2,1,0:T(2,128)(2,1)}, bf16[2,2,18432]{2,1,0:T(2,128)(2,1)S(1)}, u32[]{:S(2)}, u32[]{:S(2)}) collective-permute-start(bf16[2,2,18432]{2,1,0:T(2,128)(2,1)} %refs_11_.1), channel_id=1, source_target_pairs={{0,4},{1,5},{2,6},{3,7},{4,0},{5,1},{6,2},{7,3},{8,12},{9,13},{10,... | collective-permute-start | bytes 442376 | tf_op jit(solution)/shard_map/ppermute | solution.py:66
  5.6 7.8 %collective-permute-start.2 = (bf16[2,2,18432]{2,1,0:T(2,128)(2,1)}, bf16[2,2,18432]{2,1,0:T(2,128)(2,1)S(1)}, u32[]{:S(2)}, u32[]{:S(2)}) collective-permute-start(bf16[2,2,18432]{2,1,0:T(2,128)(2,1)} %refs_11_.1), channel_id=1, source_target_pairs={{0,2},{1,3},{2,0},{3,1},{4,6},{5,7},{6,4},{7,5},{8,10},{9,11},{10,... | collective-permute-start | bytes 442376 | tf_op jit(solution)/shard_map/ppermute | solution.py:66
  13.4 21.2 %collective-permute-start = (f32[2,8,18432]{2,1,0:T(8,128)S(1)}, f32[2,8,18432]{2,1,0:T(8,128)S(1)}, u32[]{:S(2)}, u32[]{:S(2)}) collective-permute-start(f32[2,8,18432]{2,1,0:T(8,128)S(1)} %get-tuple-element.24), channel_id=1, source_target_pairs={{0,1},{1,0},{2,3},{3,2},{4,5},{5,4},{6,7},{7,6},{8,9},{9,8},{10,11... | collective-permute-start | bytes 3538952 | tf_op jit(solution)/shard_map/ppermute | solution.py:66
  19.0 15.5 %collective-permute-start.4 = (f32[2,8,18432]{2,1,0:T(8,128)S(1)}, f32[2,8,18432]{2,1,0:T(8,128)S(1)}, u32[]{:S(2)}, u32[]{:S(2)}) collective-permute-start(f32[2,8,18432]{2,1,0:T(8,128)S(1)} %get-tuple-element.26), channel_id=1, source_target_pairs={{0,1},{1,0},{2,3},{3,2},{4,5},{5,4},{6,7},{7,6},{8,9},{9,8},{10,11... | collective-permute-start | bytes 3538952 | tf_op jit(solution)/shard_map/ppermute | solution.py:66
  22.1 3.7 %collective-permute-start.11 = (f32[2,128]{1,0:T(2,128)S(1)}, f32[2,128]{1,0:T(2,128)S(1)}, u32[]{:S(2)}, u32[]{:S(2)}) collective-permute-start(f32[2,128]{1,0:T(2,128)S(1)} %pad_maximum_fusion.1), channel_id=1, source_target_pairs={{0,2},{1,3},{2,0},{3,1},{4,6},{5,7},{6,4},{7,5},{8,10},{9,11},{10,... | collective-permute-start | bytes 3080 | tf_op jit(solution)/shard_map/ppermute | solution.py:66
  22.7 7.2 %collective-permute-start.5 = (bf16[2,2,18432]{2,1,0:T(2,128)(2,1)S(1)}, bf16[2,2,18432]{2,1,0:T(2,128)(2,1)S(1)}, u32[]{:S(2)}, u32[]{:S(2)}) collective-permute-start(bf16[2,2,18432]{2,1,0:T(2,128)(2,1)S(1)} %collective-permute-done.1.refs_0_.refs_5_.refs_12_), channel_id=1, source_target_pairs={{0,2},{1,3},{2,0},{3,1},{4,6},{5,7},{6,4},{7,5},{8,10},{9,11},{10,... | collective-permute-start | bytes 442376 | tf_op jit(solution)/shard_map/ppermute | solution.py:66
  25.7 3.6 %collective-permute-start.12 = (f32[2,128]{1,0:T(2,128)S(1)}, f32[2,128]{1,0:T(2,128)S(1)}, u32[]{:S(2)}, u32[]{:S(2)}) collective-permute-start(f32[2,128]{1,0:T(2,128)S(1)} %fusion.1), channel_id=1, source_target_pairs={{0,4},{1,5},{2,6},{3,7},{4,0},{5,1},{6,2},{7,3},{8,12},{9,13},{10,... | collective-permute-start | bytes 3080 | tf_op jit(solution)/shard_map/ppermute | solution.py:66
  26.3 6.0 %collective-permute-start.7 = (bf16[2,2,18432]{2,1,0:T(2,128)(2,1)S(1)}, bf16[2,2,18432]{2,1,0:T(2,128)(2,1)S(1)}, u32[]{:S(2)}, u32[]{:S(2)}) collective-permute-start(bf16[2,2,18432]{2,1,0:T(2,128)(2,1)S(1)} %collective-permute-done.1.refs_0_.refs_5_.refs_12_), channel_id=1, source_target_pairs={{0,4},{1,5},{2,6},{3,7},{4,0},{5,1},{6,2},{7,3},{8,12},{9,13},{10,... | collective-permute-start | bytes 442376 | tf_op jit(solution)/shard_map/ppermute | solution.py:66
  29.4 5.1 %collective-permute-start.8 = (bf16[2,2,18432]{2,1,0:T(2,128)(2,1)S(1)}, bf16[2,2,18432]{2,1,0:T(2,128)(2,1)S(1)}, u32[]{:S(2)}, u32[]{:S(2)}) collective-permute-start(bf16[2,2,18432]{2,1,0:T(2,128)(2,1)S(1)} %collective-permute-done.3.refs_2_.refs_6_.refs_15_), channel_id=1, source_target_pairs={{0,2},{1,3},{2,0},{3,1},{4,6},{5,7},{6,4},{7,5},{8,10},{9,11},{10,... | collective-permute-start | bytes 442376 | tf_op jit(solution)/shard_map/ppermute | solution.py:66
  29.9 6.7 %collective-permute-start.6 = (bf16[2,2,18432]{2,1,0:T(2,128)(2,1)S(1)}, bf16[2,2,18432]{2,1,0:T(2,128)(2,1)S(1)}, u32[]{:S(2)}, u32[]{:S(2)}) collective-permute-start(bf16[2,2,18432]{2,1,0:T(2,128)(2,1)S(1)} %collective-permute-done.5.refs_9_.refs_14_), channel_id=1, source_target_pairs={{0,4},{1,5},{2,6},{3,7},{4,0},{5,1},{6,2},{7,3},{8,12},{9,13},{10,... | collective-permute-start | bytes 442376 | tf_op jit(solution)/shard_map/ppermute | solution.py:66
  32.3 5.5 %collective-permute-start.13 = (f32[2,128]{1,0:T(2,128)S(1)}, f32[2,128]{1,0:T(2,128)S(1)}, u32[]{:S(2)}, u32[]{:S(2)}) collective-permute-start(f32[2,128]{1,0:T(2,128)S(1)} %fusion.4), channel_id=1, source_target_pairs={{0,8},{1,9},{2,10},{3,11},{4,12},{5,13},{6,14},{7,15},{8,0},{9,1},... | collective-permute-start | bytes 3080 | tf_op jit(solution)/shard_map/ppermute | solution.py:66
  40.2 9.1 %collective-permute-start.19 = (bf16[8,18432]{1,0:T(8,128)(2,1)S(1)}, bf16[8,18432]{1,0:T(8,128)(2,1)S(1)}, u32[]{:S(2)}, u32[]{:S(2)}) collective-permute-start(bf16[8,18432]{1,0:T(8,128)(2,1)S(1)} %get-tuple-element.36), channel_id=1, source_target_pairs={{0,4},{1,5},{2,6},{3,7},{4,0},{5,1},{6,2},{7,3},{8,12},{9,13},{10,... | collective-permute-start | bytes 884744 | tf_op jit(solution)/shard_map/ppermute | solution.py:66
  42.0 8.9 %collective-permute-start.14 = (bf16[8,18432]{1,0:T(8,128)(2,1)S(1)}, bf16[8,18432]{1,0:T(8,128)(2,1)S(1)}, u32[]{:S(2)}, u32[]{:S(2)}) collective-permute-start(bf16[8,18432]{1,0:T(8,128)(2,1)S(1)} %get-tuple-element.30), channel_id=1, source_target_pairs={{0,2},{1,3},{2,0},{3,1},{4,6},{5,7},{6,4},{7,5},{8,10},{9,11},{10,... | collective-permute-start | bytes 884744 | tf_op jit(solution)/shard_map/ppermute | solution.py:66
  49.4 5.2 %collective-permute-start.20 = (bf16[4,18432]{1,0:T(4,128)(2,1)S(1)}, bf16[4,18432]{1,0:T(4,128)(2,1)S(1)}, u32[]{:S(2)}, u32[]{:S(2)}) collective-permute-start(bf16[4,18432]{1,0:T(4,128)(2,1)S(1)} %get-tuple-element.38), channel_id=1, source_target_pairs={{0,2},{1,3},{2,0},{3,1},{4,6},{5,7},{6,4},{7,5},{8,10},{9,11},{10,... | collective-permute-start | bytes 442376 | tf_op jit(solution)/shard_map/ppermute | solution.py:66
  51.0 5.5 %collective-permute-start.15 = (bf16[4,18432]{1,0:T(4,128)(2,1)S(1)}, bf16[4,18432]{1,0:T(4,128)(2,1)S(1)}, u32[]{:S(2)}, u32[]{:S(2)}) collective-permute-start(bf16[4,18432]{1,0:T(4,128)(2,1)S(1)} %get-tuple-element.32), channel_id=1, source_target_pairs={{0,4},{1,5},{2,6},{3,7},{4,0},{5,1},{6,2},{7,3},{8,12},{9,13},{10,... | collective-permute-start | bytes 442376 | tf_op jit(solution)/shard_map/ppermute | solution.py:66
  54.8 12.9 %collective-permute-start.21 = (bf16[4,18432]{1,0:T(4,128)(2,1)S(1)}, bf16[4,18432]{1,0:T(4,128)(2,1)S(1)}, u32[]{:S(2)}, u32[]{:S(2)}) collective-permute-start(bf16[4,18432]{1,0:T(4,128)(2,1)S(1)} %get-tuple-element.40), channel_id=1, source_target_pairs={{0,8},{1,9},{2,10},{3,11},{4,12},{5,13},{6,14},{7,15},{8,0},{9,1},... | collective-permute-start | bytes 442376 | tf_op jit(solution)/shard_map/ppermute | solution.py:66
  56.6 12.7 %collective-permute-start.16 = (bf16[4,18432]{1,0:T(4,128)(2,1)S(1)}, bf16[4,18432]{1,0:T(4,128)(2,1)S(1)}, u32[]{:S(2)}, u32[]{:S(2)}) collective-permute-start(bf16[4,18432]{1,0:T(4,128)(2,1)S(1)} %get-tuple-element.34), channel_id=1, source_target_pairs={{0,8},{1,9},{2,10},{3,11},{4,12},{5,13},{6,14},{7,15},{8,0},{9,1},... | collective-permute-start | bytes 442376 | tf_op jit(solution)/shard_map/ppermute | solution.py:66
  67.8 6.3 %collective-permute-start.22 = (bf16[4,18432]{1,0:T(4,128)(2,1)S(1)}, bf16[4,18432]{1,0:T(4,128)(2,1)S(1)}, u32[]{:S(2)}, u32[]{:S(2)}) collective-permute-start(bf16[4,18432]{1,0:T(4,128)(2,1)S(1)} %add_convert_fusion.refs_7_), channel_id=1, source_target_pairs={{0,2},{1,3},{2,0},{3,1},{4,6},{5,7},{6,4},{7,5},{8,10},{9,11},{10,... | collective-permute-start | bytes 442376 | tf_op jit(solution)/shard_map/ppermute | solution.py:66
  69.4 6.9 %collective-permute-start.17 = (bf16[4,18432]{1,0:T(4,128)(2,1)S(1)}, bf16[4,18432]{1,0:T(4,128)(2,1)S(1)}, u32[]{:S(2)}, u32[]{:S(2)}) collective-permute-start(bf16[4,18432]{1,0:T(4,128)(2,1)S(1)} %add_convert_fusion.1.refs_4_), channel_id=1, source_target_pairs={{0,4},{1,5},{2,6},{3,7},{4,0},{5,1},{6,2},{7,3},{8,12},{9,13},{10,... | collective-permute-start | bytes 442376 | tf_op jit(solution)/shard_map/ppermute | solution.py:66
  69.5 9.0 %collective-permute-start.25 = (bf16[4,18432]{1,0:T(4,128)(2,1)S(1)}, bf16[4,18432]{1,0:T(4,128)(2,1)S(1)}, u32[]{:S(2)}, u32[]{:S(2)}) collective-permute-start(bf16[4,18432]{1,0:T(4,128)(2,1)S(1)} %add_convert_fusion.refs_7_), channel_id=1, source_target_pairs={{0,4},{1,5},{2,6},{3,7},{4,0},{5,1},{6,2},{7,3},{8,12},{9,13},{10,... | collective-permute-start | bytes 442376 | tf_op jit(solution)/shard_map/ppermute | solution.py:66
  71.5 7.0 %collective-permute-start.24 = (bf16[4,18432]{1,0:T(4,128)(2,1)S(1)}, bf16[4,18432]{1,0:T(4,128)(2,1)S(1)}, u32[]{:S(2)}, u32[]{:S(2)}) collective-permute-start(bf16[4,18432]{1,0:T(4,128)(2,1)S(1)} %add_convert_fusion.1.refs_4_), channel_id=1, source_target_pairs={{0,2},{1,3},{2,0},{3,1},{4,6},{5,7},{6,4},{7,5},{8,10},{9,11},{10,... | collective-permute-start | bytes 442376 | tf_op jit(solution)/shard_map/ppermute | solution.py:66
  74.1 6.0 %collective-permute-start.23 = (bf16[4,18432]{1,0:T(4,128)(2,1)S(1)}, bf16[4,18432]{1,0:T(4,128)(2,1)S(1)}, u32[]{:S(2)}, u32[]{:S(2)}) collective-permute-start(bf16[4,18432]{1,0:T(4,128)(2,1)S(1)} %collective-permute-done.22.refs_8_), channel_id=1, source_target_pairs={{0,4},{1,5},{2,6},{3,7},{4,0},{5,1},{6,2},{7,3},{8,12},{9,13},{10,... | collective-permute-start | bytes 442376 | tf_op jit(solution)/shard_map/ppermute | solution.py:66
  76.2 5.1 %collective-permute-start.18 = (bf16[4,18432]{1,0:T(4,128)(2,1)S(1)}, bf16[4,18432]{1,0:T(4,128)(2,1)S(1)}, u32[]{:S(2)}, u32[]{:S(2)}) collective-permute-start(bf16[4,18432]{1,0:T(4,128)(2,1)S(1)} %collective-permute-done.17.refs_5_), channel_id=1, source_target_pairs={{0,2},{1,3},{2,0},{3,1},{4,6},{5,7},{6,4},{7,5},{8,10},{9,11},{10,... | collective-permute-start | bytes 442376 | tf_op jit(solution)/shard_map/ppermute | solution.py:66
  (5 other events, 26.8 us)

commit v3 on v2

v3 whole, which is shorter than its diff:
```python
import functools

import jax
import jax.numpy as jnp
from jax import lax
from jax.experimental import pallas as pl
from jax.experimental.pallas import tpu as pltpu
from jax.sharding import PartitionSpec as P

F32 = jnp.float32
BF16 = jnp.bfloat16
NN = (((1,), (0,)), ((), ()))
NT = (((1,), (1,)), ((), ()))
LANES = 128
GRADIENT_VMEM = 18 * 1024 * 1024
SMALL_VMEM = 6 * 1024 * 1024


def general_local(inputs, grad_key, grad_value, key_down, key_up, value_down, value_up, validation, lengths):
    highest = lax.Precision.HIGHEST
    num_layers, local_examples, seq_slots, _ = inputs.shape
    total_count = lax.axis_size("ex") * local_examples
    low_rank = key_down.shape[1]
    token_mask = (
        lax.broadcasted_iota(jnp.int32, (local_examples, seq_slots), 1) < lengths[:, None]
    ).astype(F32)
    dot = functools.partial(jnp.einsum, preferred_element_type=F32)

    def masked(values):
        return (values * token_mask[None, :, :, None]).astype(BF16)

    z_key = masked(dot("lesd,lrd->lesr", inputs, key_down))
    z_value = masked(dot("lesd,lrd->lesr", inputs, value_down))
    y_key = masked(dot("leso,lor->lesr", grad_key, key_up))
    y_value = masked(dot("leso,lor->lesr", grad_value, value_up))
    pieces = [
        dot("lesr,lesd->lerd", y_key, inputs),
        dot("lesr,leso->lero", z_key, grad_key),
        dot("lesr,lesd->lerd", y_value, inputs),
        dot("lesr,leso->lero", z_value, grad_value),
    ]
    gradients = jnp.concatenate(pieces, axis=3).reshape(num_layers, local_examples, -1)
    squares = jnp.sum(gradients * gradients, axis=2)
    damping = 0.1 * lax.psum(jnp.sum(squares, axis=1), "ex") / total_count + 1e-06
    targets = lax.all_gather(validation, "ex", axis=2, tiled=True).astype(F32)
    products = jnp.einsum("lep,lvp->lev", gradients, targets, precision=highest)
    weights = products / (damping[:, None, None] + squares[:, :, None])
    directions = jnp.einsum("lev,lep->lvp", weights, gradients, precision=highest)
    summed = lax.psum(directions, "ex")
    correction = jnp.einsum("lep,lvp->lev", gradients, summed, precision=highest)
    inner = products - correction / total_count
    return -jnp.sum(inner / damping[:, None, None], axis=0)


CORE, Y, Z1, Z2 = 1, 2, 4, 8
ORDERS = ((Y, Z1), (Z1, Y))


def slot_bits(layer, position):
    first, second = ORDERS[layer]
    return (position >> 2 & 1) * first + (position >> 1 & 1) * second + (position & 1) * Z2


def swap(values, bit):
    size = lax.axis_size("ex")
    return lax.ppermute(values, "ex", [(index, index ^ bit) for index in range(size)])


def fold_lanes(values):
    tiles = [values[:, at : at + LANES] for at in range(0, values.shape[1], LANES)]
    while len(tiles) > 1:
        tiles = [sum(tiles[at : at + 2]) for at in range(0, len(tiles), 2)]
    return tiles[0]


def rank_order(index, layer, rank):
    half = rank // 2
    row = lax.broadcasted_iota(jnp.int32, (2 * rank, 2 * rank), 0)
    column = lax.broadcasted_iota(jnp.int32, (2 * rank, 2 * rank), 1)
    position = row % half
    first_bit, second_bit = ORDERS[layer]
    relative = position // 4 * first_bit + position // 2 % 2 * second_bit + position % 2 * Z2 + row // half % 2
    wanted = jnp.bitwise_xor(relative, jnp.broadcast_to(index, relative.shape)) + row // rank * rank
    return (column == wanted).astype(F32).astype(BF16)


def ordered(order, key, value):
    both = jnp.concatenate([key, value], axis=0)
    return lax.dot_general(order, both, NN, preferred_element_type=F32).astype(BF16)


class Unit:
    def __init__(self, number, length, up_factor, gk, gv, outputs):
        self.number, self.gk, self.gv = number, gk, gv
        self.own_ref, self.other_ref, self.square_ref = outputs
        self.seq, self.narrow = gk.shape
        self.rank = up_factor.shape[0] // 2
        token = lax.broadcasted_iota(jnp.int32, (1, self.seq), 1)
        self.mask = (token < length).astype(F32)
        y_key = lax.dot_general(up_factor[: self.rank], gk, NT, preferred_element_type=F32)
        y_value = lax.dot_general(up_factor[self.rank :], gv, NT, preferred_element_type=F32)
        self.y = (jnp.concatenate([y_key, y_value], axis=0) * self.mask).astype(BF16)
        self.z = jnp.zeros((2 * self.rank, self.seq), F32)
        self.total = jnp.zeros((self.rank // 2, LANES), F32)

    def store(self, values, at):
        columns, half = values.shape[1], self.rank // 2
        self.own_ref[self.number, :, at : at + columns] = values[:half]
        self.other_ref[self.number, :, at : at + columns] = values[half:]
        squared = values * values
        self.total += fold_lanes(squared[:half] + squared[half:])

    def chunk(self, factor, x, at, width):
        self.z += lax.dot_general(factor, x, NT, preferred_element_type=F32)
        down = lax.dot_general(self.y, x, NN, preferred_element_type=F32)
        self.store(down[: self.rank], at)
        self.store(down[self.rank :], width + self.narrow + at)

    def finish(self, width):
        z = (self.z * self.mask).astype(BF16)
        self.store(lax.dot_general(z[: self.rank], self.gk, NN, preferred_element_type=F32), width)
        up_value = lax.dot_general(z[self.rank :], self.gv, NN, preferred_element_type=F32)
        self.store(up_value, 2 * width + self.narrow)
        self.square_ref[self.number : self.number + 1] = jnp.sum(self.total, axis=0, keepdims=True)


def first_gradients_kernel(
    index_ref, lengths_ref, x_hbm, gk_hbm, gv_hbm, ak_hbm, av_hbm, bk_hbm, bv_hbm, *refs, chunk
):
    outputs, (x_last, gk_last, gv_last, factor_last, up_last) = refs[:3], refs[3:8]
    x_ref, gk_ref, gv_ref, a_ref, b_ref, semaphores = refs[8:]
    rank, width = a_ref.shape[2:]
    copies = {}

    def start(name, source, target):
        copies[name] = pltpu.make_async_copy(source, target, semaphores.at[len(copies)])
        copies[name].start()

    def wait(*names):
        for name in names:
            copies[name].wait()

    for layer in range(2):
        start(("bk", layer), bk_hbm.at[layer], b_ref.at[layer, 0])
        start(("bv", layer), bv_hbm.at[layer], b_ref.at[layer, 1])
        if layer == 0:
            start(("gk", 0), gk_hbm.at[0], gk_ref.at[0:2])
            start(("gv", 0), gv_hbm.at[0], gv_ref.at[0:2])
        else:
            start(("gk", 1), gk_hbm.at[1, 0], gk_ref.at[2])
            start(("gv", 1), gv_hbm.at[1, 0], gv_ref.at[2])
        start(("ak", layer), ak_hbm.at[layer], a_ref.at[layer, 0])
        start(("av", layer), av_hbm.at[layer], a_ref.at[layer, 1])
        if layer == 0:
            for at in range(0, width, chunk):
                columns = pl.ds(at, chunk)
                start(("x", at), x_hbm.at[0, :, :, columns], x_ref.at[0:2, :, columns])
        else:
            start("x", x_hbm.at[1, 0], x_ref.at[2])
    start("gk", gk_hbm.at[1, 1], gk_last)
    start("gv", gv_hbm.at[1, 1], gv_last)
    start("x last", x_hbm.at[1, 1], x_last)

    order = rank_order(index_ref[0], 0, rank)
    wait(("bk", 0), ("bv", 0), ("gk", 0), ("gv", 0))
    up_factor = ordered(order, b_ref[0, 0], b_ref[0, 1])
    units = [Unit(number, lengths_ref[number], up_factor, gk_ref[number], gv_ref[number], outputs) for number in range(2)]
    wait(("ak", 0), ("av", 0))
    for at in range(0, width, chunk):
        columns = slice(at, at + chunk)
        factor = ordered(order, a_ref[0, 0, :, columns], a_ref[0, 1, :, columns])
        wait(("x", at))
        for unit in units:
            unit.chunk(factor, x_ref[unit.number, :, columns], at, width)
    for unit in units:
        unit.finish(width)

    order = rank_order(index_ref[0], 1, rank)
    wait(("bk", 1), ("bv", 1), ("gk", 1), ("gv", 1), ("ak", 1), ("av", 1), "x")
    up_factor = ordered(order, b_ref[1, 0], b_ref[1, 1])
    up_last[...] = up_factor
    unit = Unit(2, lengths_ref[0], up_factor, gk_ref[2], gv_ref[2], outputs)
    for at in range(0, width, chunk):
        columns = slice(at, at + chunk)
        factor = ordered(order, a_ref[1, 0, :, columns], a_ref[1, 1, :, columns])
        factor_last[:, columns] = factor
        unit.chunk(factor, x_ref[2, :, columns], at, width)
    unit.finish(width)
    wait("gk", "gv", "x last")


def last_gradients_kernel(lengths_ref, x_ref, gk_ref, gv_ref, factor_ref, up_ref, *refs, chunk):
    width = x_ref.shape[1]
    unit = Unit(3, lengths_ref[1], up_ref[...], gk_ref[...], gv_ref[...], refs[-3:])
    for at in range(0, width, chunk):
        columns = slice(at, at + chunk)
        unit.chunk(factor_ref[:, columns], x_ref[:, columns], at, width)
    unit.finish(width)


IN_VMEM = pl.BlockSpec(memory_space=pltpu.VMEM)
IN_SMEM = pl.BlockSpec(memory_space=pltpu.SMEM)
ANYWHERE = pl.BlockSpec(memory_space=pl.ANY)
COLUMNS = 1024
SQUARES, NORMS = 16, 20


def in_hbm(array):
    return pltpu.with_memory_space_constraint(array, pltpu.HBM)


def gradients_of(index, lengths, inputs, grad_key, grad_value, key_down, key_up, value_down, value_up, after):
    _, _, seq, width = inputs.shape
    narrow = grad_key.shape[3]
    rank = key_down.shape[1]
    rows = jax.ShapeDtypeStruct((4, rank // 2, 2 * (width + narrow)), F32)
    outputs = [rows, rows, jax.ShapeDtypeStruct((4, LANES), F32)]
    lengths = in_hbm(lengths)
    parameters = pltpu.CompilerParams(vmem_limit_bytes=GRADIENT_VMEM)
    *results, x, gk, gv, factor, up_factor = pl.pallas_call(
        functools.partial(first_gradients_kernel, chunk=2048),
        in_specs=[IN_SMEM] * 2 + [ANYWHERE] * 7,
        out_specs=[IN_VMEM] * 8,
        out_shape=outputs
        + [
            jax.ShapeDtypeStruct(shape, BF16)
            for shape in ((seq, width), (seq, narrow), (seq, narrow), (2 * rank, width), (2 * rank, narrow))
        ],
        scratch_shapes=[
            pltpu.VMEM((3, seq, width), BF16),
            pltpu.VMEM((3, seq, narrow), BF16),
            pltpu.VMEM((3, seq, narrow), BF16),
            pltpu.VMEM((2, 2, rank, width), BF16),
            pltpu.VMEM((2, 2, rank, narrow), BF16),
            pltpu.SemaphoreType.DMA((20,)),
        ],
        compiler_params=parameters,
        cost_estimate=pl.CostEstimate(flops=1 << 32, bytes_accessed=1 << 24, transcendentals=0),
        name="first_gradients",
    )(
        index,
        lengths,
        in_hbm(inputs),
        in_hbm(grad_key),
        in_hbm(grad_value),
        in_hbm(key_down),
        in_hbm(value_down),
        in_hbm(jnp.swapaxes(key_up, 1, 2)),
        in_hbm(jnp.swapaxes(value_up, 1, 2)),
    )
    return pl.pallas_call(
        functools.partial(last_gradients_kernel, chunk=2048),
        in_specs=[IN_SMEM] + [IN_VMEM] * 8 + [ANYWHERE] * len(after),
        out_specs=[IN_VMEM] * 3,
        out_shape=outputs,
        input_output_aliases={6: 0, 7: 1, 8: 2},
        compiler_params=parameters,
        cost_estimate=pl.CostEstimate(flops=1 << 30, bytes_accessed=1 << 22, transcendentals=0),
        name="last_gradients",
    )(lengths, x, gk, gv, factor, up_factor, *results, *after)


def example_of(refs, layer, number):
    return refs[number // 2], 2 * layer + number % 2


def chunks(ref):
    def run(body, init):
        def step(number, carry):
            return body(pl.ds(pl.multiple_of(number * COLUMNS, COLUMNS), COLUMNS), carry)

        return lax.fori_loop(0, ref.shape[-1] // COLUMNS, step, init)

    return run


def dots_kernel(*refs, layers, groups, extras):
    out_ref, extra_refs = refs[-1], refs[-1 - extras : -1]
    start_ref, tables = (extra_refs[0], extra_refs[1:]) if extras else (None, ())
    slots = refs[0].shape[1]
    at = 2
    for layer in range(layers):
        target_refs = refs[at : at + len(groups[layer])]
        at += len(groups[layer])
        examples = [example_of(refs, layer, number) for number in range(4)]

        def body(columns, totals):
            pieces, filled = ([], []), 0
            for start, ref in sorted(zip(groups[layer], target_refs), key=lambda pair: pair[0]):
                index = (layer, slice(None), columns) if len(ref.shape) == 3 else (slice(None), columns)
                values = ref[index].astype(F32)
                count = values.shape[0] // 2
                for target in range(2):
                    if start > filled:
                        pieces[target].append(jnp.zeros((start - filled, values.shape[1]), F32))
                    pieces[target].append(values[target * count : (target + 1) * count])
                filled = start + count
            if filled < slots:
                for target in range(2):
                    pieces[target].append(jnp.zeros((slots - filled, COLUMNS), F32))
            rows = [jnp.concatenate(group, axis=0) for group in pieces]
            updated = []
            for number, total in enumerate(totals):
                ref, place = examples[number // 2]
                updated.append(total + fold_lanes(ref[place, :, columns] * rows[number % 2]))
            return tuple(updated)

        zero = jnp.zeros((slots, LANES), F32)
        totals = chunks(refs[0])(body, (zero,) * 8)
        for number, total in enumerate(totals):
            row = layer * 8 + number
            value = jnp.sum(total, axis=0, keepdims=True)
            out_ref[row : row + 1] = value + start_ref[row : row + 1] if start_ref is not None else value
    if tables:
        squares_ref, norms_ref, arrived_ref = tables
        out_ref[SQUARES:NORMS] = squares_ref[...]
        out_ref[NORMS:] = norms_ref[...] + arrived_ref[...]


def dots_of(rows, targets, extras=()):
    layers = len(targets)
    flat = [*rows] + [array for group in targets for array in group.values()] + [*extras]
    out_rows = NORMS + layers if len(extras) > 1 else SQUARES
    return pl.pallas_call(
        functools.partial(
            dots_kernel, layers=layers, groups=[tuple(group) for group in targets], extras=len(extras)
        ),
        in_specs=[IN_VMEM] * len(flat),
        out_specs=IN_VMEM,
        out_shape=jax.ShapeDtypeStruct((out_rows, LANES), F32),
        compiler_params=pltpu.CompilerParams(vmem_limit_bytes=SMALL_VMEM),
        cost_estimate=pl.CostEstimate(flops=1 << 22, bytes_accessed=3 << 20, transcendentals=0),
        name="dots",
    )(*flat)


def directions_kernel(mine_ref, pair_ref, *refs, count, layer):
    keep_ref, send_ref = refs[2:]
    mine, pair = mine_ref[8 * layer : 8 * layer + 8], pair_ref[8 * layer : 8 * layer + 8]
    products = mine + jnp.concatenate([pair[4:], pair[:4]], axis=0)
    row = NORMS + layer
    norm = mine_ref[row : row + 1] + pair_ref[row : row + 1]
    damping = 0.1 * jnp.sum(norm, axis=1, keepdims=True) / count + 1e-06
    weights = []
    for number in range(4):
        source = mine_ref if number < 2 else pair_ref
        row = SQUARES + 2 * layer + number % 2
        scale = damping + jnp.sum(source[row : row + 1], axis=1, keepdims=True)
        for target in range(2):
            at = 2 * number + target
            weights.append(jnp.sum(products[at : at + 1], axis=1, keepdims=True) / scale)
    examples = [example_of(refs, layer, number) for number in range(4)]

    def body(columns, carry):
        gradients = [ref[place, :, columns] for ref, place in examples]
        parts = [sum(weights[2 * number + target] * gradients[number] for number in range(4)) for target in range(2)]
        for block, ref in enumerate((keep_ref, send_ref)):
            pieces = []
            for at in (4 * block, 4 * block + 2):
                pieces += [parts[0][at : at + 2], parts[1][at : at + 2]]
            ref[:, columns] = jnp.concatenate(pieces, axis=0).astype(ref.dtype)
        return carry

    chunks(keep_ref)(body, 0)


def directions_of(layer, mine, pair, rows, count):
    _, half, row_width = rows[0].shape
    return pl.pallas_call(
        functools.partial(directions_kernel, count=count, layer=layer),
        in_specs=[IN_VMEM] * 4,
        out_specs=[IN_VMEM] * 2,
        out_shape=[
            jax.ShapeDtypeStruct((half, row_width), F32),
            jax.ShapeDtypeStruct((half, row_width), BF16),
        ],
        compiler_params=pltpu.CompilerParams(vmem_limit_bytes=SMALL_VMEM),
        cost_estimate=pl.CostEstimate(flops=1 << 22, bytes_accessed=3 << 20, transcendentals=0),
        name="directions",
    )(mine, pair, *rows)


def halve_kernel(keep_ref, arrived_ref, rest_ref, send_ref):
    total = keep_ref[...] + arrived_ref[...].astype(F32)
    rest_ref[...] = total[:4]
    send_ref[...] = total[4:].astype(BF16)


def turn_kernel(keep_ref, arrived_ref, rest_ref, send_ref):
    total = keep_ref[...] + arrived_ref[...].astype(F32)
    rest_ref[...] = total
    send_ref[...] = jnp.concatenate([total[1:2], total[0:1], total[3:4], total[2:3]], axis=0).astype(BF16)


def add_call(kernel, keep, arrived, rows):
    width = keep.shape[1]
    return pl.pallas_call(
        kernel,
        out_shape=[jax.ShapeDtypeStruct((rows, width), F32), jax.ShapeDtypeStruct((rows, width), BF16)],
        compiler_params=pltpu.CompilerParams(vmem_limit_bytes=SMALL_VMEM),
        cost_estimate=pl.CostEstimate(flops=1 << 18, bytes_accessed=1 << 20, transcendentals=0),
        name="add",
    )(keep, arrived)


def paired_local(inputs, grad_key, grad_value, key_down, key_up, value_down, value_up, validation, lengths):
    layers, examples = inputs.shape[:2]
    count = lax.axis_size("ex") * examples
    index = lax.axis_index("ex").astype(jnp.int32)[None]
    arguments = (index, lengths, inputs, grad_key, grad_value, key_down, key_up, value_down, value_up)

    targets = {0: validation}
    first_bits = (Z2, Y, Z1, Y | Z1)
    for bits in first_bits:
        targets[bits] = swap(validation, bits)
    own, other, squares = gradients_of(*arguments, after=[targets[bits] for bits in first_bits])
    rows = (own, swap(other, CORE))
    for bits in (Y, Z1):
        targets[bits | Z2] = swap(targets[Z2], bits)
    targets[Y | Z1 | Z2] = swap(targets[Y | Z2], Z1)

    norms = jnp.stack([squares[0] + squares[1], squares[2] + squares[3]])
    for bit in (Y, Z1):
        norms = norms + swap(norms, bit)
    arrived = swap(norms, Z2)

    slots = [[slot_bits(layer, position) for position in range(8)] for layer in range(layers)]
    early = [{at: targets[bits] for at, bits in enumerate(row) if bits in (0, *first_bits)} for row in slots]
    late = [{at: targets[bits] for at, bits in enumerate(row) if bits not in (0, *first_bits)} for row in slots]
    mine = dots_of(rows, late, [dots_of(rows, early), squares, norms, arrived])
    pair = swap(mine, CORE)
    early, late = [], []
    for layer, (first, second) in enumerate(ORDERS):
        keep, send = directions_of(layer, mine, pair, rows, count)
        keep, send = add_call(halve_kernel, keep, swap(send, first), 4)
        keep, send = add_call(turn_kernel, keep, swap(send, second), 4)
        block = (keep + swap(send, Z2).astype(F32)).astype(BF16)
        from_second = swap(block, second)
        early.append({0: block, 2: from_second})
        late.append({4: swap(block, first), 6: swap(from_second, first)})
    corrections = dots_of(rows, late, [dots_of(rows, early)])
    damping = 0.1 * jnp.sum(mine[NORMS:] + pair[NORMS:], axis=1) / count + 1e-06
    inner = (mine[:SQUARES] - corrections / count).reshape(layers, 4 * examples, LANES)
    split = 2 * examples
    inner = inner[:, :split] + swap(inner[:, split:], CORE)
    scores = -jnp.sum(jnp.sum(inner, axis=2) / damping[:, None], axis=0)
    return scores.reshape(examples, 2)


def solution(mesh):
    in_specs = (
        P(None, ("groups", "ex"), None, None),
        P(None, ("groups", "ex"), None, None),
        P(None, ("groups", "ex"), None, None),
        P(),
        P(),
        P(),
        P(),
        P(None, "groups", "ex"),
        P(("groups", "ex")),
    )
    out_specs = P(("groups", "ex"), None)

    def local(*arguments):
        low_rank = arguments[3].shape[1]
        paired = lax.axis_size("ex") == low_rank == 16 and arguments[0].shape[:2] == (2, 2)
        return (paired_local if paired else general_local)(*arguments)

    return jax.shard_map(local, mesh=mesh, in_specs=in_specs, out_specs=out_specs, check_vma=False)
```

time: 84.7 us -> 82 us (0.968)
  starting transfers between devices: 29 us -> 27.5 us
    ppermute x27 -> x25, starting transfers between devices: 29 us -> 27.5 us  [swap(): lax.ppermute(values, 'ex', [(index, index ^ bit) for index in range(size)])]
    pallas_call x2, Pallas kernels: 11.1 us -> 10.2 us  [the longest x1 7.55 us: gradients_of(): pl.pallas_call(functools.partial(first_gradients_kernel, chunk=2048), in_...]
    ppermute x27 -> x25, waiting for transfers between devices: 33.7 us -> 33.9 us  [swap(): lax.ppermute(values, 'ex', [(index, index ^ bit) for index in range(size)])]
  transfers between devices with their start and end apart: 27 -> 25, of which waited for: 17 -> 16; matrix products, arithmetic and copies ran while one was open for 0% -> 0% of each run, Pallas kernels for 21% -> 15%
where the time goes in v3:
time: 82 us; the launch traced here: 81.9 us
  waiting for transfers between devices  33.9 us (41%)
  starting transfers between devices  27.5 us (34%)
  Pallas kernels  19.1 us (23%)
    ppermute x25, waiting for transfers between devices, swap(): lax.ppermute(values, 'ex', [(index, index ^ bit) for index in range(size)])  33.9 us
    ppermute x25, starting transfers between devices, swap(): lax.ppermute(values, 'ex', [(index, index ^ bit) for index in range(size)])  27.5 us
    pallas_call x1, Pallas kernels, gradients_of(): pl.pallas_call(functools.partial(first_gradients_kernel, chunk=2048), in_...  7.55 us
    pallas_call x4, Pallas kernels, dots_of(): pl.pallas_call(functools.partial(dots_kernel, layers=layers, groups=[tupl...  5.79 us
    pallas_call x1, Pallas kernels, gradients_of(): pl.pallas_call(functools.partial(last_gradients_kernel, chunk=2048), in_s...  2.6 us
    pallas_call x2, Pallas kernels, directions_of(): pl.pallas_call(functools.partial(directions_kernel, count=count, layer=la...  2.58 us
  transfers between devices with their start and end apart: 25, of which 16 were waited for; matrix products, arithmetic and copies ran while one was open for 0% of the time, Pallas kernels for 15%

profile of v3, /device:TPU:0, one launch (start us, length us, event | category | flops | bytes accessed | tf_op | source)
XLA Modules:
  0.0 81.9 jit_solution(4521728201738149054)
XLA Ops:
  0.0 4.0 %collective-permute-start = (bf16[2,2,18432]{2,1,0:T(2,128)(2,1)}, bf16[2,2,18432]{2,1,0:T(2,128)(2,1)S(1)}, u32[]{:S(2)}, u32[]{:S(2)}) collective-permute-start(bf16[2,2,18432]{2,1,0:T(2,128)(2,1)} %refs_7_.1), channel_id=1, source_target_pairs={{0,8},{1,9},{2,10},{3,11},{4,12},{5,13},{6,14},{7,15},{8,0},{9,1},... | collective-permute-start | bytes 442376 | tf_op jit(solution)/shard_map/ppermute | solution.py:66
  4.0 1.5 %collective-permute-start.1 = (bf16[2,2,18432]{2,1,0:T(2,128)(2,1)}, bf16[2,2,18432]{2,1,0:T(2,128)(2,1)S(1)}, u32[]{:S(2)}, u32[]{:S(2)}) collective-permute-start(bf16[2,2,18432]{2,1,0:T(2,128)(2,1)} %refs_7_.1), channel_id=1, source_target_pairs={{0,2},{1,3},{2,0},{3,1},{4,6},{5,7},{6,4},{7,5},{8,10},{9,11},{10,... | collective-permute-start | bytes 442376 | tf_op jit(solution)/shard_map/ppermute | solution.py:66
  5.6 1.6 %collective-permute-start.2 = (bf16[2,2,18432]{2,1,0:T(2,128)(2,1)}, bf16[2,2,18432]{2,1,0:T(2,128)(2,1)S(1)}, u32[]{:S(2)}, u32[]{:S(2)}) collective-permute-start(bf16[2,2,18432]{2,1,0:T(2,128)(2,1)} %refs_7_.1), channel_id=1, source_target_pairs={{0,4},{1,5},{2,6},{3,7},{4,0},{5,1},{6,2},{7,3},{8,12},{9,13},{10,... | collective-permute-start | bytes 442376 | tf_op jit(solution)/shard_map/ppermute | solution.py:66
  7.5 7.6 %first_gradients.1 = (f32[4,8,18432]{2,1,0:T(8,128)S(1)}, f32[4,8,18432]{2,1,0:T(8,128)S(1)}, f32[4,128]{1,0:T(4,128)S(1)}, bf16[128,8192]{1,0:T(8,128)(2,1)S(1)...) custom-call(s32[1]{0:T(128)} %bitcast.index_ref, ...), custom_call_target="tpu_custom_call" | custom-call | flops 4294967296 | bytes 16777216 | tf_op jit(solution)/shard_map/first_gradients/pallas_call | solution.py:220
  16.0 2.6 %last_gradients.1 = (f32[4,8,18432]{2,1,0:T(8,128)S(1)}, f32[4,8,18432]{2,1,0:T(8,128)S(1)}, f32[4,128]{1,0:T(4,128)S(1)}) custom-call(s32[2]{0:T(128)} %lengths_ref.3, bf16[128,8192]{1,0:T(8,128)(2,1)S(1)} %get-tuple-element.28.x_ref, bf16[128,1024]{1,0:T(8,128)(2,1)S(1)} %get-tuple-element.29.gk_ref, ...), custom_call_target="tpu_custom_call", output_to_operand_aliasing={{0}: (6, {}), {1}: (7, {}), {2}: (8, {})} | custom-call | flops 1073741824 | bytes 4194304 | tf_op jit(solution)/shard_map/last_gradients/pallas_call | solution.py:251
  18.7 1.5 %collective-permute-start.8 = (f32[2,128]{1,0:T(2,128)S(1)}, f32[2,128]{1,0:T(2,128)S(1)}, u32[]{:S(2)}, u32[]{:S(2)}) collective-permute-start(f32[2,128]{1,0:T(2,128)S(1)} %pad_maximum_fusion), channel_id=1, source_target_pairs={{0,2},{1,3},{2,0},{3,1},{4,6},{5,7},{6,4},{7,5},{8,10},{9,11},{10,... | collective-permute-start | bytes 3080 | tf_op jit(solution)/shard_map/ppermute | solution.py:66
  20.8 1.5 %collective-permute-done.8 = f32[2,128]{1,0:T(2,128)S(1)} collective-permute-done((f32[2,128]{1,0:T(2,128)S(1)}, f32[2,128]{1,0:T(2,128)S(1)}, u32[]{:S(2)}, u32[]{:S(2)}) %collective-permute-start.8) | collective-permute-done | bytes 1056 | tf_op jit(solution)/shard_map/ppermute | solution.py:66
  24.5 1.7 %collective-permute-done.6.refs_3_.refs_5_ = bf16[2,2,18432]{2,1,0:T(2,128)(2,1)S(1)} collective-permute-done((bf16[2,2,18432]{2,1,0:T(2,128)(2,1)S(1)}, bf16[2,2,18432]{2,1,0:T(2,128)(2,1)S(1)}, u32[]{:S(2)}, u32[]{:S(2)}) %collective-permute-start.6) | collective-permute-done | bytes 147488 | tf_op jit(solution)/shard_map/ppermute | solution.py:66
  27.0 2.3 %collective-permute-start.10 = (f32[2,128]{1,0:T(2,128)S(1)}, f32[2,128]{1,0:T(2,128)S(1)}, u32[]{:S(2)}, u32[]{:S(2)}) collective-permute-start(f32[2,128]{1,0:T(2,128)S(1)} %fusion.4.refs_10_), channel_id=1, source_target_pairs={{0,8},{1,9},{2,10},{3,11},{4,12},{5,13},{6,14},{7,15},{8,0},{9,1},... | collective-permute-start | bytes 3080 | tf_op jit(solution)/shard_map/ppermute | solution.py:66
  29.3 1.8 %dots.4.refs_8_ = f32[16,128]{1,0:T(8,128)S(1)} custom-call(f32[4,8,18432]{2,1,0:T(8,128)S(1)} %get-tuple-element.36.refs_0_, f32[4,8,18432]{2,1,0:T(8,128)S(1)} %collective-permute-done.4.refs_1_, bf16[2,2,18432]{2,1,0:T(2,128)(2,1)S(1)} %copy-done, bf16[2,2,18432]{2,1,0:T(2,128)(2,1)S(1)} %collective-permute-done.refs_3_.refs_8_, ...), custom_call_target="tpu_custom_call" | custom-call | flops 4194304 | bytes 3145728 | tf_op jit(solution)/shard_map/dots/pallas_call | solution.py:324
  31.9 1.5 %dots.5.mine_ref = f32[22,128]{1,0:T(8,128)S(1)} custom-call(f32[4,8,18432]{2,1,0:T(8,128)S(1)} %get-tuple-element.36.refs_0_, f32[4,8,18432]{2,1,0:T(8,128)S(1)} %collective-permute-done.4.refs_1_, bf16[2,2,18432]{2,1,0:T(2,128)(2,1)S(1)} %collective-permute-done.5.refs_2_.refs_6_, bf16[2,2,18432]{2,1,0:T(2,128)(2,1)S(1)} %collective-permute-done.6.refs_3_.refs_5_, ...), custom_call_target="tpu_custom_call" | custom-call | flops 4194304 | bytes 3145728 | tf_op jit(solution)/shard_map/dots/pallas_call | solution.py:324
  34.7 1.3 %directions.3 = (f32[8,18432]{1,0:T(8,128)S(1)}, bf16[8,18432]{1,0:T(8,128)(2,1)S(1)}) custom-call(f32[22,128]{1,0:T(8,128)S(1)} %dots.5.mine_ref, f32[22,128]{1,0:T(8,128)S(1)} %collective-permute-done.11.pair_ref, f32[4,8,18432]{2,1,0:T(8,128)S(1)} %get-tuple-element.36.refs_0_, f32[4,8,18432]{2,1,0:T(8,128)S(1)} %collective-permute-done.4.refs_1_), custom_call_target="tpu_custom_call" | custom-call | flops 4194304 | bytes 3145728 | tf_op jit(solution)/shard_map/directions/pallas_call | solution.py:369
  36.0 1.9 %collective-permute-start.18 = (bf16[8,18432]{1,0:T(8,128)(2,1)S(1)}, bf16[8,18432]{1,0:T(8,128)(2,1)S(1)}, u32[]{:S(2)}, u32[]{:S(2)}) collective-permute-start(bf16[8,18432]{1,0:T(8,128)(2,1)S(1)} %get-tuple-element.46), channel_id=1, source_target_pairs={{0,4},{1,5},{2,6},{3,7},{4,0},{5,1},{6,2},{7,3},{8,12},{9,13},{10,... | collective-permute-start | bytes 884744 | tf_op jit(solution)/shard_map/ppermute | solution.py:66
  37.9 1.3 %directions.2 = (f32[8,18432]{1,0:T(8,128)S(1)}, bf16[8,18432]{1,0:T(8,128)(2,1)S(1)}) custom-call(f32[22,128]{1,0:T(8,128)S(1)} %dots.5.mine_ref, f32[22,128]{1,0:T(8,128)S(1)} %collective-permute-done.11.pair_ref, f32[4,8,18432]{2,1,0:T(8,128)S(1)} %get-tuple-element.36.refs_0_, f32[4,8,18432]{2,1,0:T(8,128)S(1)} %collective-permute-done.4.refs_1_), custom_call_target="tpu_custom_call" | custom-call | flops 4194304 | bytes 3145728 | tf_op jit(solution)/shard_map/directions/pallas_call | solution.py:369
  40.4 4.8 %collective-permute-done.18.arrived_ref = bf16[8,18432]{1,0:T(8,128)(2,1)S(1)} collective-permute-done((bf16[8,18432]{1,0:T(8,128)(2,1)S(1)}, bf16[8,18432]{1,0:T(8,128)(2,1)S(1)}, u32[]{:S(2)}, u32[]{:S(2)}) %collective-permute-start.18) | collective-permute-done | bytes 294944 | tf_op jit(solution)/shard_map/ppermute | solution.py:66
  46.5 2.1 %collective-permute-done.12.arrived_ref = bf16[8,18432]{1,0:T(8,128)(2,1)S(1)} collective-permute-done((bf16[8,18432]{1,0:T(8,128)(2,1)S(1)}, bf16[8,18432]{1,0:T(8,128)(2,1)S(1)}, u32[]{:S(2)}, u32[]{:S(2)}) %collective-permute-start.12) | collective-permute-done | bytes 294944 | tf_op jit(solution)/shard_map/ppermute | solution.py:66
  48.8 2.4 %collective-permute-done.19.arrived_ref = bf16[4,18432]{1,0:T(4,128)(2,1)S(1)} collective-permute-done((bf16[4,18432]{1,0:T(4,128)(2,1)S(1)}, bf16[4,18432]{1,0:T(4,128)(2,1)S(1)}, u32[]{:S(2)}, u32[]{:S(2)}) %collective-permute-start.19) | collective-permute-done | bytes 147488 | tf_op jit(solution)/shard_map/ppermute | solution.py:66
  52.6 1.4 %collective-permute-done.13.arrived_ref = bf16[4,18432]{1,0:T(4,128)(2,1)S(1)} collective-permute-done((bf16[4,18432]{1,0:T(4,128)(2,1)S(1)}, bf16[4,18432]{1,0:T(4,128)(2,1)S(1)}, u32[]{:S(2)}, u32[]{:S(2)}) %collective-permute-start.13) | collective-permute-done | bytes 147488 | tf_op jit(solution)/shard_map/ppermute | solution.py:66
  54.7 8.6 %collective-permute-done.20 = bf16[4,18432]{1,0:T(4,128)(2,1)S(1)} collective-permute-done((bf16[4,18432]{1,0:T(4,128)(2,1)S(1)}, bf16[4,18432]{1,0:T(4,128)(2,1)S(1)}, u32[]{:S(2)}, u32[]{:S(2)}) %collective-permute-start.20) | collective-permute-done | bytes 147488 | tf_op jit(solution)/shard_map/ppermute | solution.py:66
  63.3 1.8 %collective-permute-start.22 = (bf16[4,18432]{1,0:T(4,128)(2,1)S(1)}, bf16[4,18432]{1,0:T(4,128)(2,1)S(1)}, u32[]{:S(2)}, u32[]{:S(2)}) collective-permute-start(bf16[4,18432]{1,0:T(4,128)(2,1)S(1)} %add_convert_fusion.refs_4_), channel_id=1, source_target_pairs={{0,2},{1,3},{2,0},{3,1},{4,6},{5,7},{6,4},{7,5},{8,10},{9,11},{10,... | collective-permute-start | bytes 442376 | tf_op jit(solution)/shard_map/ppermute | solution.py:66
  66.5 2.0 %collective-permute-start.21 = (bf16[4,18432]{1,0:T(4,128)(2,1)S(1)}, bf16[4,18432]{1,0:T(4,128)(2,1)S(1)}, u32[]{:S(2)}, u32[]{:S(2)}) collective-permute-start(bf16[4,18432]{1,0:T(4,128)(2,1)S(1)} %add_convert_fusion.refs_4_), channel_id=1, source_target_pairs={{0,4},{1,5},{2,6},{3,7},{4,0},{5,1},{6,2},{7,3},{8,12},{9,13},{10,... | collective-permute-start | bytes 442376 | tf_op jit(solution)/shard_map/ppermute | solution.py:66
  69.7 3.5 %collective-permute-done.16.refs_3_ = bf16[4,18432]{1,0:T(4,128)(2,1)S(1)} collective-permute-done((bf16[4,18432]{1,0:T(4,128)(2,1)S(1)}, bf16[4,18432]{1,0:T(4,128)(2,1)S(1)}, u32[]{:S(2)}, u32[]{:S(2)}) %collective-permute-start.16) | collective-permute-done | bytes 147488 | tf_op jit(solution)/shard_map/ppermute | solution.py:66
  76.3 2.2 %collective-permute-done.23.refs_5_ = bf16[4,18432]{1,0:T(4,128)(2,1)S(1)} collective-permute-done((bf16[4,18432]{1,0:T(4,128)(2,1)S(1)}, bf16[4,18432]{1,0:T(4,128)(2,1)S(1)}, u32[]{:S(2)}, u32[]{:S(2)}) %collective-permute-start.23) | collective-permute-done | bytes 147488 | tf_op jit(solution)/shard_map/ppermute | solution.py:66
  78.5 1.2 %dots.7 = f32[16,128]{1,0:T(8,128)S(1)} custom-call(f32[4,8,18432]{2,1,0:T(8,128)S(1)} %get-tuple-element.36.refs_0_, f32[4,8,18432]{2,1,0:T(8,128)S(1)} %collective-permute-done.4.refs_1_, bf16[4,18432]{1,0:T(4,128)(2,1)S(1)} %collective-permute-done.15.refs_2_, bf16[4,18432]{1,0:T(4,128)(2,1)S(1)} %collective-permute-done.17.refs_3_, ...), custom_call_target="tpu_custom_call" | custom-call | flops 4194304 | bytes 3145728 | tf_op jit(solution)/shard_map/dots/pallas_call | solution.py:324
  (54 shorter events, 19.5 us)
Async XLA Ops:
  0.0 15.1 %collective-permute-start = (bf16[2,2,18432]{2,1,0:T(2,128)(2,1)}, bf16[2,2,18432]{2,1,0:T(2,128)(2,1)S(1)}, u32[]{:S(2)}, u32[]{:S(2)}) collective-permute-start(bf16[2,2,18432]{2,1,0:T(2,128)(2,1)} %refs_7_.1), channel_id=1, source_target_pairs={{0,8},{1,9},{2,10},{3,11},{4,12},{5,13},{6,14},{7,15},{8,0},{9,1},... | collective-permute-start | bytes 442376 | tf_op jit(solution)/shard_map/ppermute | solution.py:66
  4.0 11.1 %collective-permute-start.1 = (bf16[2,2,18432]{2,1,0:T(2,128)(2,1)}, bf16[2,2,18432]{2,1,0:T(2,128)(2,1)S(1)}, u32[]{:S(2)}, u32[]{:S(2)}) collective-permute-start(bf16[2,2,18432]{2,1,0:T(2,128)(2,1)} %refs_7_.1), channel_id=1, source_target_pairs={{0,2},{1,3},{2,0},{3,1},{4,6},{5,7},{6,4},{7,5},{8,10},{9,11},{10,... | collective-permute-start | bytes 442376 | tf_op jit(solution)/shard_map/ppermute | solution.py:66
  5.6 9.6 %collective-permute-start.2 = (bf16[2,2,18432]{2,1,0:T(2,128)(2,1)}, bf16[2,2,18432]{2,1,0:T(2,128)(2,1)S(1)}, u32[]{:S(2)}, u32[]{:S(2)}) collective-permute-start(bf16[2,2,18432]{2,1,0:T(2,128)(2,1)} %refs_7_.1), channel_id=1, source_target_pairs={{0,4},{1,5},{2,6},{3,7},{4,0},{5,1},{6,2},{7,3},{8,12},{9,13},{10,... | collective-permute-start | bytes 442376 | tf_op jit(solution)/shard_map/ppermute | solution.py:66
  7.1 8.9 %collective-permute-start.3 = (bf16[2,2,18432]{2,1,0:T(2,128)(2,1)}, bf16[2,2,18432]{2,1,0:T(2,128)(2,1)S(1)}, u32[]{:S(2)}, u32[]{:S(2)}) collective-permute-start(bf16[2,2,18432]{2,1,0:T(2,128)(2,1)} %refs_7_.1), channel_id=1, source_target_pairs={{0,6},{1,7},{2,4},{3,5},{4,2},{5,3},{6,0},{7,1},{8,14},{9,15},{10,... | collective-permute-start | bytes 442376 | tf_op jit(solution)/shard_map/ppermute | solution.py:66
  18.6 10.7 %collective-permute-start.4 = (f32[4,8,18432]{2,1,0:T(8,128)S(1)}, f32[4,8,18432]{2,1,0:T(8,128)S(1)}, u32[]{:S(2)}, u32[]{:S(2)}) collective-permute-start(f32[4,8,18432]{2,1,0:T(8,128)S(1)} %get-tuple-element.37), channel_id=1, source_target_pairs={{0,1},{1,0},{2,3},{3,2},{4,5},{5,4},{6,7},{7,6},{8,9},{9,8},{10,11... | collective-permute-start | bytes 7077896 | tf_op jit(solution)/shard_map/ppermute | solution.py:66
  18.7 3.6 %collective-permute-start.8 = (f32[2,128]{1,0:T(2,128)S(1)}, f32[2,128]{1,0:T(2,128)S(1)}, u32[]{:S(2)}, u32[]{:S(2)}) collective-permute-start(f32[2,128]{1,0:T(2,128)S(1)} %pad_maximum_fusion), channel_id=1, source_target_pairs={{0,2},{1,3},{2,0},{3,1},{4,6},{5,7},{6,4},{7,5},{8,10},{9,11},{10,... | collective-permute-start | bytes 3080 | tf_op jit(solution)/shard_map/ppermute | solution.py:66
  20.2 6.0 %collective-permute-start.6 = (bf16[2,2,18432]{2,1,0:T(2,128)(2,1)S(1)}, bf16[2,2,18432]{2,1,0:T(2,128)(2,1)S(1)}, u32[]{:S(2)}, u32[]{:S(2)}) collective-permute-start(bf16[2,2,18432]{2,1,0:T(2,128)(2,1)S(1)} %collective-permute-done.refs_3_.refs_8_), channel_id=1, source_target_pairs={{0,2},{1,3},{2,0},{3,1},{4,6},{5,7},{6,4},{7,5},{8,10},{9,11},{10,... | collective-permute-start | bytes 442376 | tf_op jit(solution)/shard_map/ppermute | solution.py:66
  22.4 4.6 %collective-permute-start.9 = (f32[2,128]{1,0:T(2,128)S(1)}, f32[2,128]{1,0:T(2,128)S(1)}, u32[]{:S(2)}, u32[]{:S(2)}) collective-permute-start(f32[2,128]{1,0:T(2,128)S(1)} %fusion.3), channel_id=1, source_target_pairs={{0,4},{1,5},{2,6},{3,7},{4,0},{5,1},{6,2},{7,3},{8,12},{9,13},{10,... | collective-permute-start | bytes 3080 | tf_op jit(solution)/shard_map/ppermute | solution.py:66
  23.6 8.0 %collective-permute-start.5 = (bf16[2,2,18432]{2,1,0:T(2,128)(2,1)S(1)}, bf16[2,2,18432]{2,1,0:T(2,128)(2,1)S(1)}, u32[]{:S(2)}, u32[]{:S(2)}) collective-permute-start(bf16[2,2,18432]{2,1,0:T(2,128)(2,1)S(1)} %collective-permute-done.refs_3_.refs_8_), channel_id=1, source_target_pairs={{0,4},{1,5},{2,6},{3,7},{4,0},{5,1},{6,2},{7,3},{8,12},{9,13},{10,... | collective-permute-start | bytes 442376 | tf_op jit(solution)/shard_map/ppermute | solution.py:66
  26.2 5.8 %collective-permute-start.7 = (bf16[2,2,18432]{2,1,0:T(2,128)(2,1)S(1)}, bf16[2,2,18432]{2,1,0:T(2,128)(2,1)S(1)}, u32[]{:S(2)}, u32[]{:S(2)}) collective-permute-start(bf16[2,2,18432]{2,1,0:T(2,128)(2,1)S(1)} %collective-permute-done.6.refs_3_.refs_5_), channel_id=1, source_target_pairs={{0,4},{1,5},{2,6},{3,7},{4,0},{5,1},{6,2},{7,3},{8,12},{9,13},{10,... | collective-permute-start | bytes 442376 | tf_op jit(solution)/shard_map/ppermute | solution.py:66
  27.0 4.5 %collective-permute-start.10 = (f32[2,128]{1,0:T(2,128)S(1)}, f32[2,128]{1,0:T(2,128)S(1)}, u32[]{:S(2)}, u32[]{:S(2)}) collective-permute-start(f32[2,128]{1,0:T(2,128)S(1)} %fusion.4.refs_10_), channel_id=1, source_target_pairs={{0,8},{1,9},{2,10},{3,11},{4,12},{5,13},{6,14},{7,15},{8,0},{9,1},... | collective-permute-start | bytes 3080 | tf_op jit(solution)/shard_map/ppermute | solution.py:66
  33.5 1.2 %collective-permute-start.11 = (f32[22,128]{1,0:T(8,128)S(1)}, f32[22,128]{1,0:T(8,128)S(1)}, u32[]{:S(2)}, u32[]{:S(2)}) collective-permute-start(f32[22,128]{1,0:T(8,128)S(1)} %dots.5.mine_ref), channel_id=1, source_target_pairs={{0,1},{1,0},{2,3},{3,2},{4,5},{5,4},{6,7},{7,6},{8,9},{9,8},{10,11... | collective-permute-start | bytes 33800 | tf_op jit(solution)/shard_map/ppermute | solution.py:66
  36.0 9.2 %collective-permute-start.18 = (bf16[8,18432]{1,0:T(8,128)(2,1)S(1)}, bf16[8,18432]{1,0:T(8,128)(2,1)S(1)}, u32[]{:S(2)}, u32[]{:S(2)}) collective-permute-start(bf16[8,18432]{1,0:T(8,128)(2,1)S(1)} %get-tuple-element.46), channel_id=1, source_target_pairs={{0,4},{1,5},{2,6},{3,7},{4,0},{5,1},{6,2},{7,3},{8,12},{9,13},{10,... | collective-permute-start | bytes 884744 | tf_op jit(solution)/shard_map/ppermute | solution.py:66
  39.2 9.4 %collective-permute-start.12 = (bf16[8,18432]{1,0:T(8,128)(2,1)S(1)}, bf16[8,18432]{1,0:T(8,128)(2,1)S(1)}, u32[]{:S(2)}, u32[]{:S(2)}) collective-permute-start(bf16[8,18432]{1,0:T(8,128)(2,1)S(1)} %get-tuple-element.40), channel_id=1, source_target_pairs={{0,2},{1,3},{2,0},{3,1},{4,6},{5,7},{6,4},{7,5},{8,10},{9,11},{10,... | collective-permute-start | bytes 884744 | tf_op jit(solution)/shard_map/ppermute | solution.py:66
  45.3 5.9 %collective-permute-start.19 = (bf16[4,18432]{1,0:T(4,128)(2,1)S(1)}, bf16[4,18432]{1,0:T(4,128)(2,1)S(1)}, u32[]{:S(2)}, u32[]{:S(2)}) collective-permute-start(bf16[4,18432]{1,0:T(4,128)(2,1)S(1)} %get-tuple-element.48), channel_id=1, source_target_pairs={{0,2},{1,3},{2,0},{3,1},{4,6},{5,7},{6,4},{7,5},{8,10},{9,11},{10,... | collective-permute-start | bytes 442376 | tf_op jit(solution)/shard_map/ppermute | solution.py:66
  48.7 5.2 %collective-permute-start.13 = (bf16[4,18432]{1,0:T(4,128)(2,1)S(1)}, bf16[4,18432]{1,0:T(4,128)(2,1)S(1)}, u32[]{:S(2)}, u32[]{:S(2)}) collective-permute-start(bf16[4,18432]{1,0:T(4,128)(2,1)S(1)} %get-tuple-element.42), channel_id=1, source_target_pairs={{0,4},{1,5},{2,6},{3,7},{4,0},{5,1},{6,2},{7,3},{8,12},{9,13},{10,... | collective-permute-start | bytes 442376 | tf_op jit(solution)/shard_map/ppermute | solution.py:66
  51.4 11.8 %collective-permute-start.20 = (bf16[4,18432]{1,0:T(4,128)(2,1)S(1)}, bf16[4,18432]{1,0:T(4,128)(2,1)S(1)}, u32[]{:S(2)}, u32[]{:S(2)}) collective-permute-start(bf16[4,18432]{1,0:T(4,128)(2,1)S(1)} %get-tuple-element.50), channel_id=1, source_target_pairs={{0,8},{1,9},{2,10},{3,11},{4,12},{5,13},{6,14},{7,15},{8,0},{9,1},... | collective-permute-start | bytes 442376 | tf_op jit(solution)/shard_map/ppermute | solution.py:66
  54.1 12.2 %collective-permute-start.14 = (bf16[4,18432]{1,0:T(4,128)(2,1)S(1)}, bf16[4,18432]{1,0:T(4,128)(2,1)S(1)}, u32[]{:S(2)}, u32[]{:S(2)}) collective-permute-start(bf16[4,18432]{1,0:T(4,128)(2,1)S(1)} %get-tuple-element.44), channel_id=1, source_target_pairs={{0,8},{1,9},{2,10},{3,11},{4,12},{5,13},{6,14},{7,15},{8,0},{9,1},... | collective-permute-start | bytes 442376 | tf_op jit(solution)/shard_map/ppermute | solution.py:66
  63.3 6.3 %collective-permute-start.22 = (bf16[4,18432]{1,0:T(4,128)(2,1)S(1)}, bf16[4,18432]{1,0:T(4,128)(2,1)S(1)}, u32[]{:S(2)}, u32[]{:S(2)}) collective-permute-start(bf16[4,18432]{1,0:T(4,128)(2,1)S(1)} %add_convert_fusion.refs_4_), channel_id=1, source_target_pairs={{0,2},{1,3},{2,0},{3,1},{4,6},{5,7},{6,4},{7,5},{8,10},{9,11},{10,... | collective-permute-start | bytes 442376 | tf_op jit(solution)/shard_map/ppermute | solution.py:66
  66.4 6.8 %collective-permute-start.16 = (bf16[4,18432]{1,0:T(4,128)(2,1)S(1)}, bf16[4,18432]{1,0:T(4,128)(2,1)S(1)}, u32[]{:S(2)}, u32[]{:S(2)}) collective-permute-start(bf16[4,18432]{1,0:T(4,128)(2,1)S(1)} %add_convert_fusion.1.refs_2_), channel_id=1, source_target_pairs={{0,4},{1,5},{2,6},{3,7},{4,0},{5,1},{6,2},{7,3},{8,12},{9,13},{10,... | collective-permute-start | bytes 442376 | tf_op jit(solution)/shard_map/ppermute | solution.py:66
  66.5 9.9 %collective-permute-start.21 = (bf16[4,18432]{1,0:T(4,128)(2,1)S(1)}, bf16[4,18432]{1,0:T(4,128)(2,1)S(1)}, u32[]{:S(2)}, u32[]{:S(2)}) collective-permute-start(bf16[4,18432]{1,0:T(4,128)(2,1)S(1)} %add_convert_fusion.refs_4_), channel_id=1, source_target_pairs={{0,4},{1,5},{2,6},{3,7},{4,0},{5,1},{6,2},{7,3},{8,12},{9,13},{10,... | collective-permute-start | bytes 442376 | tf_op jit(solution)/shard_map/ppermute | solution.py:66
  68.5 7.8 %collective-permute-start.15 = (bf16[4,18432]{1,0:T(4,128)(2,1)S(1)}, bf16[4,18432]{1,0:T(4,128)(2,1)S(1)}, u32[]{:S(2)}, u32[]{:S(2)}) collective-permute-start(bf16[4,18432]{1,0:T(4,128)(2,1)S(1)} %add_convert_fusion.1.refs_2_), channel_id=1, source_target_pairs={{0,2},{1,3},{2,0},{3,1},{4,6},{5,7},{6,4},{7,5},{8,10},{9,11},{10,... | collective-permute-start | bytes 442376 | tf_op jit(solution)/shard_map/ppermute | solution.py:66
  69.6 8.9 %collective-permute-start.23 = (bf16[4,18432]{1,0:T(4,128)(2,1)S(1)}, bf16[4,18432]{1,0:T(4,128)(2,1)S(1)}, u32[]{:S(2)}, u32[]{:S(2)}) collective-permute-start(bf16[4,18432]{1,0:T(4,128)(2,1)S(1)} %collective-permute-done.22.refs_5_), channel_id=1, source_target_pairs={{0,4},{1,5},{2,6},{3,7},{4,0},{5,1},{6,2},{7,3},{8,12},{9,13},{10,... | collective-permute-start | bytes 442376 | tf_op jit(solution)/shard_map/ppermute | solution.py:66
  73.1 5.4 %collective-permute-start.17 = (bf16[4,18432]{1,0:T(4,128)(2,1)S(1)}, bf16[4,18432]{1,0:T(4,128)(2,1)S(1)}, u32[]{:S(2)}, u32[]{:S(2)}) collective-permute-start(bf16[4,18432]{1,0:T(4,128)(2,1)S(1)} %collective-permute-done.16.refs_3_), channel_id=1, source_target_pairs={{0,2},{1,3},{2,0},{3,1},{4,6},{5,7},{6,4},{7,5},{8,10},{9,11},{10,... | collective-permute-start | bytes 442376 | tf_op jit(solution)/shard_map/ppermute | solution.py:66
  (2 other events, 14.5 us)

commit v4 on v3

--- a/solution.py
+++ b/solution.py
@@ -274,19 +274,19 @@
     return run
 
 
-def dots_kernel(*refs, layers, groups, extras):
+def dots_kernel(*refs, groups, extras):
     out_ref, extra_refs = refs[-1], refs[-1 - extras : -1]
     start_ref, tables = (extra_refs[0], extra_refs[1:]) if extras else (None, ())
     slots = refs[0].shape[1]
     at = 2
-    for layer in range(layers):
-        target_refs = refs[at : at + len(groups[layer])]
-        at += len(groups[layer])
+    for place, (layer, starts) in enumerate(groups):
+        target_refs = refs[at : at + len(starts)]
+        at += len(starts)
         examples = [example_of(refs, layer, number) for number in range(4)]
 
         def body(columns, totals):
             pieces, filled = ([], []), 0
-            for start, ref in sorted(zip(groups[layer], target_refs), key=lambda pair: pair[0]):
+            for start, ref in sorted(zip(starts, target_refs), key=lambda pair: pair[0]):
                 index = (layer, slice(None), columns) if len(ref.shape) == 3 else (slice(None), columns)
                 values = ref[index].astype(F32)
                 count = values.shape[0] // 2
@@ -308,7 +308,7 @@
         zero = jnp.zeros((slots, LANES), F32)
         totals = chunks(refs[0])(body, (zero,) * 8)
         for number, total in enumerate(totals):
-            row = layer * 8 + number
+            row = place * 8 + number
             value = jnp.sum(total, axis=0, keepdims=True)
             out_ref[row : row + 1] = value + start_ref[row : row + 1] if start_ref is not None else value
     if tables:
@@ -318,13 +318,11 @@
 
 
 def dots_of(rows, targets, extras=()):
-    layers = len(targets)
-    flat = [*rows] + [array for group in targets for array in group.values()] + [*extras]
-    out_rows = NORMS + layers if len(extras) > 1 else SQUARES
+    flat = [*rows] + [array for group in targets.values() for array in group.values()] + [*extras]
+    out_rows = NORMS + len(targets) if len(extras) > 1 else 8 * len(targets)
+    groups = [(layer, tuple(group)) for layer, group in targets.items()]
     return pl.pallas_call(
-        functools.partial(
-            dots_kernel, layers=layers, groups=[tuple(group) for group in targets], extras=len(extras)
-        ),
+        functools.partial(dots_kernel, groups=groups, extras=len(extras)),
         in_specs=[IN_VMEM] * len(flat),
         out_specs=IN_VMEM,
         out_shape=jax.ShapeDtypeStruct((out_rows, LANES), F32),
@@ -335,7 +333,7 @@
 
 
 def directions_kernel(mine_ref, pair_ref, *refs, count, layer):
-    keep_ref, send_ref = refs[2:]
+    block_refs = refs[2:]
     mine, pair = mine_ref[8 * layer : 8 * layer + 8], pair_ref[8 * layer : 8 * layer + 8]
     products = mine + jnp.concatenate([pair[4:], pair[:4]], axis=0)
     row = NORMS + layer
@@ -354,14 +352,13 @@
     def body(columns, carry):
         gradients = [ref[place, :, columns] for ref, place in examples]
         parts = [sum(weights[2 * number + target] * gradients[number] for number in range(4)) for target in range(2)]
-        for block, ref in enumerate((keep_ref, send_ref)):
-            pieces = []
-            for at in (4 * block, 4 * block + 2):
-                pieces += [parts[0][at : at + 2], parts[1][at : at + 2]]
+        for block, ref in enumerate(block_refs):
+            at = 2 * block
+            pieces = [parts[0][at : at + 2], parts[1][at : at + 2]]
             ref[:, columns] = jnp.concatenate(pieces, axis=0).astype(ref.dtype)
         return carry
 
-    chunks(keep_ref)(body, 0)
+    chunks(block_refs[0])(body, 0)
 
 
 def directions_of(layer, mine, pair, rows, count):
@@ -369,38 +366,31 @@
     return pl.pallas_call(
         functools.partial(directions_kernel, count=count, layer=layer),
         in_specs=[IN_VMEM] * 4,
-        out_specs=[IN_VMEM] * 2,
-        out_shape=[
-            jax.ShapeDtypeStruct((half, row_width), F32),
-            jax.ShapeDtypeStruct((half, row_width), BF16),
-        ],
+        out_specs=[IN_VMEM] * 4,
+        out_shape=[jax.ShapeDtypeStruct((half // 2, row_width), kind) for kind in (F32, BF16, BF16, BF16)],
         compiler_params=pltpu.CompilerParams(vmem_limit_bytes=SMALL_VMEM),
         cost_estimate=pl.CostEstimate(flops=1 << 22, bytes_accessed=3 << 20, transcendentals=0),
         name="directions",
     )(mine, pair, *rows)
 
 
-def halve_kernel(keep_ref, arrived_ref, rest_ref, send_ref):
-    total = keep_ref[...] + arrived_ref[...].astype(F32)
-    rest_ref[...] = total[:4]
-    send_ref[...] = total[4:].astype(BF16)
-
-
-def turn_kernel(keep_ref, arrived_ref, rest_ref, send_ref):
-    total = keep_ref[...] + arrived_ref[...].astype(F32)
+def turn_kernel(keep_ref, *refs):
+    rest_ref, send_ref = refs[-2:]
+    total = keep_ref[...]
+    for ref in refs[:-2]:
+        total += ref[...].astype(F32)
     rest_ref[...] = total
     send_ref[...] = jnp.concatenate([total[1:2], total[0:1], total[3:4], total[2:3]], axis=0).astype(BF16)
 
 
-def add_call(kernel, keep, arrived, rows):
-    width = keep.shape[1]
+def turned(keep, arrived):
     return pl.pallas_call(
-        kernel,
-        out_shape=[jax.ShapeDtypeStruct((rows, width), F32), jax.ShapeDtypeStruct((rows, width), BF16)],
+        turn_kernel,
+        out_shape=[jax.ShapeDtypeStruct(keep.shape, F32), jax.ShapeDtypeStruct(keep.shape, BF16)],
         compiler_params=pltpu.CompilerParams(vmem_limit_bytes=SMALL_VMEM),
         cost_estimate=pl.CostEstimate(flops=1 << 18, bytes_accessed=1 << 20, transcendentals=0),
         name="add",
-    )(keep, arrived)
+    )(keep, *arrived)
 
 
 def paired_local(inputs, grad_key, grad_value, key_down, key_up, value_down, value_up, validation, lengths):
@@ -425,22 +415,26 @@
     arrived = swap(norms, Z2)
 
     slots = [[slot_bits(layer, position) for position in range(8)] for layer in range(layers)]
-    early = [{at: targets[bits] for at, bits in enumerate(row) if bits in (0, *first_bits)} for row in slots]
-    late = [{at: targets[bits] for at, bits in enumerate(row) if bits not in (0, *first_bits)} for row in slots]
+    early = {
+        layer: {at: targets[bits] for at, bits in enumerate(row) if bits in (0, *first_bits)}
+        for layer, row in enumerate(slots)
+    }
+    late = {
+        layer: {at: targets[bits] for at, bits in enumerate(row) if bits not in (0, *first_bits)}
+        for layer, row in enumerate(slots)
+    }
     mine = dots_of(rows, late, [dots_of(rows, early), squares, norms, arrived])
     pair = swap(mine, CORE)
-    early, late = [], []
-    for layer, (first, second) in enumerate(ORDERS):
-        keep, send = directions_of(layer, mine, pair, rows, count)
-        keep, send = add_call(halve_kernel, keep, swap(send, first), 4)
-        keep, send = add_call(turn_kernel, keep, swap(send, second), 4)
+    corrections = [None] * layers
+    for layer in reversed(range(layers)):
+        first, second = ORDERS[layer]
+        keep, *sends = directions_of(layer, mine, pair, rows, count)
+        keep, send = turned(keep, [swap(send, bits) for send, bits in zip(sends, (second, first, first | second))])
         block = (keep + swap(send, Z2).astype(F32)).astype(BF16)
-        from_second = swap(block, second)
-        early.append({0: block, 2: from_second})
-        late.append({4: swap(block, first), 6: swap(from_second, first)})
-    corrections = dots_of(rows, late, [dots_of(rows, early)])
+        blocks = {0: block, 2: swap(block, second), 4: swap(block, first), 6: swap(block, first | second)}
+        corrections[layer] = dots_of(rows, {layer: blocks})
     damping = 0.1 * jnp.sum(mine[NORMS:] + pair[NORMS:], axis=1) / count + 1e-06
-    inner = (mine[:SQUARES] - corrections / count).reshape(layers, 4 * examples, LANES)
+    inner = mine[:SQUARES].reshape(layers, 4 * examples, LANES) - jnp.stack(corrections) / count
     split = 2 * examples
     inner = inner[:, :split] + swap(inner[:, split:], CORE)
     scores = -jnp.sum(jnp.sum(inner, axis=2) / damping[:, None], axis=0)

time: 82 us -> 77.3 us (0.943)
  waiting for transfers between devices: 33.9 us -> 26.4 us
  starting transfers between devices: 27.5 us -> 31.2 us
  Pallas kernels: 19.1 us -> 18.2 us
    ppermute x25 -> x27, waiting for transfers between devices: 33.9 us -> 26.4 us  [swap(): lax.ppermute(values, 'ex', [(index, index ^ bit) for index in range(size)])]
    ppermute x25 -> x27, starting transfers between devices: 27.5 us -> 31.2 us  [swap(): lax.ppermute(values, 'ex', [(index, index ^ bit) for index in range(size)])]
    pallas_call x8 -> x6, Pallas kernels: 6.36 us -> 5.28 us  [the longest x4 4.83 us: dots_of(): pl.pallas_call(functools.partial(dots_kernel, groups=groups, extras=len(e...]
  transfers between devices with their start and end apart: 25 -> 27, of which waited for: 16 -> 18; matrix products, arithmetic and copies ran while one was open for 0% -> 0% of each run, Pallas kernels for 15% -> 15%
where the time goes in v4:
time: 77.3 us; the launch traced here: 77.1 us
  starting transfers between devices  31.2 us (40%)
  waiting for transfers between devices  26.4 us (34%)
  Pallas kernels  18.2 us (24%)
    ppermute x27, starting transfers between devices, swap(): lax.ppermute(values, 'ex', [(index, index ^ bit) for index in range(size)])  31.2 us
    ppermute x27, waiting for transfers between devices, swap(): lax.ppermute(values, 'ex', [(index, index ^ bit) for index in range(size)])  26.4 us
    pallas_call x1, Pallas kernels, gradients_of(): pl.pallas_call(functools.partial(first_gradients_kernel, chunk=2048), in_...  7.55 us
    pallas_call x4, Pallas kernels, dots_of(): pl.pallas_call(functools.partial(dots_kernel, groups=groups, extras=len(e...  4.83 us
    pallas_call x2, Pallas kernels, directions_of(): pl.pallas_call(functools.partial(directions_kernel, count=count, layer=la...  2.71 us
    pallas_call x1, Pallas kernels, gradients_of(): pl.pallas_call(functools.partial(last_gradients_kernel, chunk=2048), in_s...  2.6 us
  transfers between devices with their start and end apart: 27, of which 18 were waited for; matrix products, arithmetic and copies ran while one was open for 0% of the time, Pallas kernels for 15%

profile of v4, /device:TPU:0, one launch (start us, length us, event | category | flops | bytes accessed | tf_op | source)
XLA Modules:
  0.0 77.1 jit_solution(6245262389293633275)
XLA Ops:
  0.0 4.0 %collective-permute-start = (bf16[2,2,18432]{2,1,0:T(2,128)(2,1)}, bf16[2,2,18432]{2,1,0:T(2,128)(2,1)S(1)}, u32[]{:S(2)}, u32[]{:S(2)}) collective-permute-start(bf16[2,2,18432]{2,1,0:T(2,128)(2,1)} %refs_7_.1), channel_id=1, source_target_pairs={{0,8},{1,9},{2,10},{3,11},{4,12},{5,13},{6,14},{7,15},{8,0},{9,1},... | collective-permute-start | bytes 442376 | tf_op jit(solution)/shard_map/ppermute | solution.py:66
  4.0 1.5 %collective-permute-start.1 = (bf16[2,2,18432]{2,1,0:T(2,128)(2,1)}, bf16[2,2,18432]{2,1,0:T(2,128)(2,1)S(1)}, u32[]{:S(2)}, u32[]{:S(2)}) collective-permute-start(bf16[2,2,18432]{2,1,0:T(2,128)(2,1)} %refs_7_.1), channel_id=1, source_target_pairs={{0,2},{1,3},{2,0},{3,1},{4,6},{5,7},{6,4},{7,5},{8,10},{9,11},{10,... | collective-permute-start | bytes 442376 | tf_op jit(solution)/shard_map/ppermute | solution.py:66
  5.6 1.6 %collective-permute-start.2 = (bf16[2,2,18432]{2,1,0:T(2,128)(2,1)}, bf16[2,2,18432]{2,1,0:T(2,128)(2,1)S(1)}, u32[]{:S(2)}, u32[]{:S(2)}) collective-permute-start(bf16[2,2,18432]{2,1,0:T(2,128)(2,1)} %refs_7_.1), channel_id=1, source_target_pairs={{0,4},{1,5},{2,6},{3,7},{4,0},{5,1},{6,2},{7,3},{8,12},{9,13},{10,... | collective-permute-start | bytes 442376 | tf_op jit(solution)/shard_map/ppermute | solution.py:66
  7.5 7.6 %first_gradients.1 = (f32[4,8,18432]{2,1,0:T(8,128)S(1)}, f32[4,8,18432]{2,1,0:T(8,128)S(1)}, f32[4,128]{1,0:T(4,128)S(1)}, bf16[128,8192]{1,0:T(8,128)(2,1)S(1)...) custom-call(s32[1]{0:T(128)} %bitcast.index_ref, ...), custom_call_target="tpu_custom_call" | custom-call | flops 4294967296 | bytes 16777216 | tf_op jit(solution)/shard_map/first_gradients/pallas_call | solution.py:220
  16.0 2.6 %last_gradients.1 = (f32[4,8,18432]{2,1,0:T(8,128)S(1)}, f32[4,8,18432]{2,1,0:T(8,128)S(1)}, f32[4,128]{1,0:T(4,128)S(1)}) custom-call(s32[2]{0:T(128)} %lengths_ref.3, bf16[128,8192]{1,0:T(8,128)(2,1)S(1)} %get-tuple-element.28.x_ref, bf16[128,1024]{1,0:T(8,128)(2,1)S(1)} %get-tuple-element.29.gk_ref, ...), custom_call_target="tpu_custom_call", output_to_operand_aliasing={{0}: (6, {}), {1}: (7, {}), {2}: (8, {})} | custom-call | flops 1073741824 | bytes 4194304 | tf_op jit(solution)/shard_map/last_gradients/pallas_call | solution.py:251
  18.7 1.5 %collective-permute-start.8 = (f32[2,128]{1,0:T(2,128)S(1)}, f32[2,128]{1,0:T(2,128)S(1)}, u32[]{:S(2)}, u32[]{:S(2)}) collective-permute-start(f32[2,128]{1,0:T(2,128)S(1)} %pad_maximum_fusion), channel_id=1, source_target_pairs={{0,2},{1,3},{2,0},{3,1},{4,6},{5,7},{6,4},{7,5},{8,10},{9,11},{10,... | collective-permute-start | bytes 3080 | tf_op jit(solution)/shard_map/ppermute | solution.py:66
  20.8 1.5 %collective-permute-done.8 = f32[2,128]{1,0:T(2,128)S(1)} collective-permute-done((f32[2,128]{1,0:T(2,128)S(1)}, f32[2,128]{1,0:T(2,128)S(1)}, u32[]{:S(2)}, u32[]{:S(2)}) %collective-permute-start.8) | collective-permute-done | bytes 1056 | tf_op jit(solution)/shard_map/ppermute | solution.py:66
  24.5 1.7 %collective-permute-done.6.refs_3_.refs_5_ = bf16[2,2,18432]{2,1,0:T(2,128)(2,1)S(1)} collective-permute-done((bf16[2,2,18432]{2,1,0:T(2,128)(2,1)S(1)}, bf16[2,2,18432]{2,1,0:T(2,128)(2,1)S(1)}, u32[]{:S(2)}, u32[]{:S(2)}) %collective-permute-start.6) | collective-permute-done | bytes 147488 | tf_op jit(solution)/shard_map/ppermute | solution.py:66
  27.0 2.3 %collective-permute-start.10 = (f32[2,128]{1,0:T(2,128)S(1)}, f32[2,128]{1,0:T(2,128)S(1)}, u32[]{:S(2)}, u32[]{:S(2)}) collective-permute-start(f32[2,128]{1,0:T(2,128)S(1)} %fusion.4.refs_10_), channel_id=1, source_target_pairs={{0,8},{1,9},{2,10},{3,11},{4,12},{5,13},{6,14},{7,15},{8,0},{9,1},... | collective-permute-start | bytes 3080 | tf_op jit(solution)/shard_map/ppermute | solution.py:66
  29.3 1.8 %dots.4.refs_8_ = f32[16,128]{1,0:T(8,128)S(1)} custom-call(f32[4,8,18432]{2,1,0:T(8,128)S(1)} %get-tuple-element.36.refs_0_, f32[4,8,18432]{2,1,0:T(8,128)S(1)} %collective-permute-done.4.refs_1_, bf16[2,2,18432]{2,1,0:T(2,128)(2,1)S(1)} %copy-done, bf16[2,2,18432]{2,1,0:T(2,128)(2,1)S(1)} %collective-permute-done.refs_3_.refs_8_, ...), custom_call_target="tpu_custom_call" | custom-call | flops 4194304 | bytes 3145728 | tf_op jit(solution)/shard_map/dots/pallas_call | solution.py:324
  31.9 1.5 %dots.5.mine_ref = f32[22,128]{1,0:T(8,128)S(1)} custom-call(f32[4,8,18432]{2,1,0:T(8,128)S(1)} %get-tuple-element.36.refs_0_, f32[4,8,18432]{2,1,0:T(8,128)S(1)} %collective-permute-done.4.refs_1_, bf16[2,2,18432]{2,1,0:T(2,128)(2,1)S(1)} %collective-permute-done.5.refs_2_.refs_6_, bf16[2,2,18432]{2,1,0:T(2,128)(2,1)S(1)} %collective-permute-done.6.refs_3_.refs_5_, ...), custom_call_target="tpu_custom_call" | custom-call | flops 4194304 | bytes 3145728 | tf_op jit(solution)/shard_map/dots/pallas_call | solution.py:324
  36.1 1.9 %collective-permute-start.12 = (bf16[4,18432]{1,0:T(4,128)(2,1)S(1)}, bf16[4,18432]{1,0:T(4,128)(2,1)S(1)}, u32[]{:S(2)}, u32[]{:S(2)}) collective-permute-start(bf16[4,18432]{1,0:T(4,128)(2,1)S(1)} %get-tuple-element.40), channel_id=1, source_target_pairs={{0,4},{1,5},{2,6},{3,7},{4,0},{5,1},{6,2},{7,3},{8,12},{9,13},{10,... | collective-permute-start | bytes 442376 | tf_op jit(solution)/shard_map/ppermute | solution.py:66
  39.6 1.4 %directions.3 = (f32[4,18432]{1,0:T(4,128)S(1)}, bf16[4,18432]{1,0:T(4,128)(2,1)S(1)}, bf16[4,18432]{1,0:T(4,128)(2,1)S(1)}, bf16[4,18432]{1,0:T(4,128)(2,1)S(1)}) custom-call(f32[22,128]{1,0:T(8,128)S(1)} %dots.5.mine_ref, f32[22,128]{1,0:T(8,128)S(1)} %collective-permute-done.11.pair_ref, f32[4,8,18432]{2,1,0:T(8,128)S(1)} %get-tuple-element.36.refs_0_, ...), custom_call_target="tpu_custom_call" | custom-call | flops 4194304 | bytes 3145728 | tf_op jit(solution)/shard_map/directions/pallas_call | solution.py:366
  42.1 1.9 %collective-permute-start.20 = (bf16[4,18432]{1,0:T(4,128)(2,1)S(1)}, bf16[4,18432]{1,0:T(4,128)(2,1)S(1)}, u32[]{:S(2)}, u32[]{:S(2)}) collective-permute-start(bf16[4,18432]{1,0:T(4,128)(2,1)S(1)} %get-tuple-element.47), channel_id=1, source_target_pairs={{0,4},{1,5},{2,6},{3,7},{4,0},{5,1},{6,2},{7,3},{8,12},{9,13},{10,... | collective-permute-start | bytes 442376 | tf_op jit(solution)/shard_map/ppermute | solution.py:66
  45.2 2.4 %collective-permute-done.13.refs_1_ = bf16[4,18432]{1,0:T(4,128)(2,1)S(1)} collective-permute-done((bf16[4,18432]{1,0:T(4,128)(2,1)S(1)}, bf16[4,18432]{1,0:T(4,128)(2,1)S(1)}, u32[]{:S(2)}, u32[]{:S(2)}) %collective-permute-start.13) | collective-permute-done | bytes 147488 | tf_op jit(solution)/shard_map/ppermute | solution.py:66
  49.0 1.5 %collective-permute-done.19.refs_0_ = bf16[4,18432]{1,0:T(4,128)(2,1)S(1)} collective-permute-done((bf16[4,18432]{1,0:T(4,128)(2,1)S(1)}, bf16[4,18432]{1,0:T(4,128)(2,1)S(1)}, u32[]{:S(2)}, u32[]{:S(2)}) %collective-permute-start.19) | collective-permute-done | bytes 147488 | tf_op jit(solution)/shard_map/ppermute | solution.py:66
  51.0 3.5 %collective-permute-done.21.refs_2_ = bf16[4,18432]{1,0:T(4,128)(2,1)S(1)} collective-permute-done((bf16[4,18432]{1,0:T(4,128)(2,1)S(1)}, bf16[4,18432]{1,0:T(4,128)(2,1)S(1)}, u32[]{:S(2)}, u32[]{:S(2)}) %collective-permute-start.21) | collective-permute-done | bytes 147488 | tf_op jit(solution)/shard_map/ppermute | solution.py:66
  55.3 3.6 %collective-permute-done.15 = bf16[4,18432]{1,0:T(4,128)(2,1)S(1)} collective-permute-done((bf16[4,18432]{1,0:T(4,128)(2,1)S(1)}, bf16[4,18432]{1,0:T(4,128)(2,1)S(1)}, u32[]{:S(2)}, u32[]{:S(2)}) %collective-permute-start.15) | collective-permute-done | bytes 147488 | tf_op jit(solution)/shard_map/ppermute | solution.py:66
  59.0 2.0 %collective-permute-start.17 = (bf16[4,18432]{1,0:T(4,128)(2,1)S(1)}, bf16[4,18432]{1,0:T(4,128)(2,1)S(1)}, u32[]{:S(2)}, u32[]{:S(2)}) collective-permute-start(bf16[4,18432]{1,0:T(4,128)(2,1)S(1)} %add_convert_fusion.1.refs_2_), channel_id=1, source_target_pairs={{0,2},{1,3},{2,0},{3,1},{4,6},{5,7},{6,4},{7,5},{8,10},{9,11},{10,... | collective-permute-start | bytes 442376 | tf_op jit(solution)/shard_map/ppermute | solution.py:66
  61.1 1.4 %collective-permute-start.18 = (bf16[4,18432]{1,0:T(4,128)(2,1)S(1)}, bf16[4,18432]{1,0:T(4,128)(2,1)S(1)}, u32[]{:S(2)}, u32[]{:S(2)}) collective-permute-start(bf16[4,18432]{1,0:T(4,128)(2,1)S(1)} %add_convert_fusion.1.refs_2_), channel_id=1, source_target_pairs={{0,6},{1,7},{2,4},{3,5},{4,2},{5,3},{6,0},{7,1},{8,14},{9,15},{10,... | collective-permute-start | bytes 442376 | tf_op jit(solution)/shard_map/ppermute | solution.py:66
  63.4 1.5 %collective-permute-start.23 = (bf16[4,18432]{1,0:T(4,128)(2,1)S(1)}, bf16[4,18432]{1,0:T(4,128)(2,1)S(1)}, u32[]{:S(2)}, u32[]{:S(2)}) collective-permute-start(bf16[4,18432]{1,0:T(4,128)(2,1)S(1)} %add_convert_fusion.refs_2_), channel_id=1, source_target_pairs={{0,2},{1,3},{2,0},{3,1},{4,6},{5,7},{6,4},{7,5},{8,10},{9,11},{10,... | collective-permute-start | bytes 442376 | tf_op jit(solution)/shard_map/ppermute | solution.py:66
  65.3 1.6 %collective-permute-start.25 = (bf16[4,18432]{1,0:T(4,128)(2,1)S(1)}, bf16[4,18432]{1,0:T(4,128)(2,1)S(1)}, u32[]{:S(2)}, u32[]{:S(2)}) collective-permute-start(bf16[4,18432]{1,0:T(4,128)(2,1)S(1)} %add_convert_fusion.refs_2_), channel_id=1, source_target_pairs={{0,6},{1,7},{2,4},{3,5},{4,2},{5,3},{6,0},{7,1},{8,14},{9,15},{10,... | collective-permute-start | bytes 442376 | tf_op jit(solution)/shard_map/ppermute | solution.py:66
  67.0 2.2 %collective-permute-done.18.refs_5_ = bf16[4,18432]{1,0:T(4,128)(2,1)S(1)} collective-permute-done((bf16[4,18432]{1,0:T(4,128)(2,1)S(1)}, bf16[4,18432]{1,0:T(4,128)(2,1)S(1)}, u32[]{:S(2)}, u32[]{:S(2)}) %collective-permute-start.18) | collective-permute-done | bytes 147488 | tf_op jit(solution)/shard_map/ppermute | solution.py:66
  71.6 2.7 %collective-permute-done.25.refs_5_ = bf16[4,18432]{1,0:T(4,128)(2,1)S(1)} collective-permute-done((bf16[4,18432]{1,0:T(4,128)(2,1)S(1)}, bf16[4,18432]{1,0:T(4,128)(2,1)S(1)}, u32[]{:S(2)}, u32[]{:S(2)}) %collective-permute-start.25) | collective-permute-done | bytes 147488 | tf_op jit(solution)/shard_map/ppermute | solution.py:66
  (56 shorter events, 21.6 us)
Async XLA Ops:
  0.0 15.1 %collective-permute-start = (bf16[2,2,18432]{2,1,0:T(2,128)(2,1)}, bf16[2,2,18432]{2,1,0:T(2,128)(2,1)S(1)}, u32[]{:S(2)}, u32[]{:S(2)}) collective-permute-start(bf16[2,2,18432]{2,1,0:T(2,128)(2,1)} %refs_7_.1), channel_id=1, source_target_pairs={{0,8},{1,9},{2,10},{3,11},{4,12},{5,13},{6,14},{7,15},{8,0},{9,1},... | collective-permute-start | bytes 442376 | tf_op jit(solution)/shard_map/ppermute | solution.py:66
  4.0 11.1 %collective-permute-start.1 = (bf16[2,2,18432]{2,1,0:T(2,128)(2,1)}, bf16[2,2,18432]{2,1,0:T(2,128)(2,1)S(1)}, u32[]{:S(2)}, u32[]{:S(2)}) collective-permute-start(bf16[2,2,18432]{2,1,0:T(2,128)(2,1)} %refs_7_.1), channel_id=1, source_target_pairs={{0,2},{1,3},{2,0},{3,1},{4,6},{5,7},{6,4},{7,5},{8,10},{9,11},{10,... | collective-permute-start | bytes 442376 | tf_op jit(solution)/shard_map/ppermute | solution.py:66
  5.6 9.6 %collective-permute-start.2 = (bf16[2,2,18432]{2,1,0:T(2,128)(2,1)}, bf16[2,2,18432]{2,1,0:T(2,128)(2,1)S(1)}, u32[]{:S(2)}, u32[]{:S(2)}) collective-permute-start(bf16[2,2,18432]{2,1,0:T(2,128)(2,1)} %refs_7_.1), channel_id=1, source_target_pairs={{0,4},{1,5},{2,6},{3,7},{4,0},{5,1},{6,2},{7,3},{8,12},{9,13},{10,... | collective-permute-start | bytes 442376 | tf_op jit(solution)/shard_map/ppermute | solution.py:66
  7.1 8.9 %collective-permute-start.3 = (bf16[2,2,18432]{2,1,0:T(2,128)(2,1)}, bf16[2,2,18432]{2,1,0:T(2,128)(2,1)S(1)}, u32[]{:S(2)}, u32[]{:S(2)}) collective-permute-start(bf16[2,2,18432]{2,1,0:T(2,128)(2,1)} %refs_7_.1), channel_id=1, source_target_pairs={{0,6},{1,7},{2,4},{3,5},{4,2},{5,3},{6,0},{7,1},{8,14},{9,15},{10,... | collective-permute-start | bytes 442376 | tf_op jit(solution)/shard_map/ppermute | solution.py:66
  18.6 10.7 %collective-permute-start.4 = (f32[4,8,18432]{2,1,0:T(8,128)S(1)}, f32[4,8,18432]{2,1,0:T(8,128)S(1)}, u32[]{:S(2)}, u32[]{:S(2)}) collective-permute-start(f32[4,8,18432]{2,1,0:T(8,128)S(1)} %get-tuple-element.37), channel_id=1, source_target_pairs={{0,1},{1,0},{2,3},{3,2},{4,5},{5,4},{6,7},{7,6},{8,9},{9,8},{10,11... | collective-permute-start | bytes 7077896 | tf_op jit(solution)/shard_map/ppermute | solution.py:66
  20.2 6.0 %collective-permute-start.6 = (bf16[2,2,18432]{2,1,0:T(2,128)(2,1)S(1)}, bf16[2,2,18432]{2,1,0:T(2,128)(2,1)S(1)}, u32[]{:S(2)}, u32[]{:S(2)}) collective-permute-start(bf16[2,2,18432]{2,1,0:T(2,128)(2,1)S(1)} %collective-permute-done.refs_3_.refs_8_), channel_id=1, source_target_pairs={{0,2},{1,3},{2,0},{3,1},{4,6},{5,7},{6,4},{7,5},{8,10},{9,11},{10,... | collective-permute-start | bytes 442376 | tf_op jit(solution)/shard_map/ppermute | solution.py:66
  22.4 4.6 %collective-permute-start.9 = (f32[2,128]{1,0:T(2,128)S(1)}, f32[2,128]{1,0:T(2,128)S(1)}, u32[]{:S(2)}, u32[]{:S(2)}) collective-permute-start(f32[2,128]{1,0:T(2,128)S(1)} %fusion.3), channel_id=1, source_target_pairs={{0,4},{1,5},{2,6},{3,7},{4,0},{5,1},{6,2},{7,3},{8,12},{9,13},{10,... | collective-permute-start | bytes 3080 | tf_op jit(solution)/shard_map/ppermute | solution.py:66
  23.6 8.0 %collective-permute-start.5 = (bf16[2,2,18432]{2,1,0:T(2,128)(2,1)S(1)}, bf16[2,2,18432]{2,1,0:T(2,128)(2,1)S(1)}, u32[]{:S(2)}, u32[]{:S(2)}) collective-permute-start(bf16[2,2,18432]{2,1,0:T(2,128)(2,1)S(1)} %collective-permute-done.refs_3_.refs_8_), channel_id=1, source_target_pairs={{0,4},{1,5},{2,6},{3,7},{4,0},{5,1},{6,2},{7,3},{8,12},{9,13},{10,... | collective-permute-start | bytes 442376 | tf_op jit(solution)/shard_map/ppermute | solution.py:66
  26.2 5.8 %collective-permute-start.7 = (bf16[2,2,18432]{2,1,0:T(2,128)(2,1)S(1)}, bf16[2,2,18432]{2,1,0:T(2,128)(2,1)S(1)}, u32[]{:S(2)}, u32[]{:S(2)}) collective-permute-start(bf16[2,2,18432]{2,1,0:T(2,128)(2,1)S(1)} %collective-permute-done.6.refs_3_.refs_5_), channel_id=1, source_target_pairs={{0,4},{1,5},{2,6},{3,7},{4,0},{5,1},{6,2},{7,3},{8,12},{9,13},{10,... | collective-permute-start | bytes 442376 | tf_op jit(solution)/shard_map/ppermute | solution.py:66
  27.0 4.5 %collective-permute-start.10 = (f32[2,128]{1,0:T(2,128)S(1)}, f32[2,128]{1,0:T(2,128)S(1)}, u32[]{:S(2)}, u32[]{:S(2)}) collective-permute-start(f32[2,128]{1,0:T(2,128)S(1)} %fusion.4.refs_10_), channel_id=1, source_target_pairs={{0,8},{1,9},{2,10},{3,11},{4,12},{5,13},{6,14},{7,15},{8,0},{9,1},... | collective-permute-start | bytes 3080 | tf_op jit(solution)/shard_map/ppermute | solution.py:66
  36.1 8.0 %collective-permute-start.12 = (bf16[4,18432]{1,0:T(4,128)(2,1)S(1)}, bf16[4,18432]{1,0:T(4,128)(2,1)S(1)}, u32[]{:S(2)}, u32[]{:S(2)}) collective-permute-start(bf16[4,18432]{1,0:T(4,128)(2,1)S(1)} %get-tuple-element.40), channel_id=1, source_target_pairs={{0,4},{1,5},{2,6},{3,7},{4,0},{5,1},{6,2},{7,3},{8,12},{9,13},{10,... | collective-permute-start | bytes 442376 | tf_op jit(solution)/shard_map/ppermute | solution.py:66
  38.0 9.6 %collective-permute-start.13 = (bf16[4,18432]{1,0:T(4,128)(2,1)S(1)}, bf16[4,18432]{1,0:T(4,128)(2,1)S(1)}, u32[]{:S(2)}, u32[]{:S(2)}) collective-permute-start(bf16[4,18432]{1,0:T(4,128)(2,1)S(1)} %get-tuple-element.41), channel_id=1, source_target_pairs={{0,2},{1,3},{2,0},{3,1},{4,6},{5,7},{6,4},{7,5},{8,10},{9,11},{10,... | collective-permute-start | bytes 442376 | tf_op jit(solution)/shard_map/ppermute | solution.py:66
  39.1 8.5 %collective-permute-start.14 = (bf16[4,18432]{1,0:T(4,128)(2,1)S(1)}, bf16[4,18432]{1,0:T(4,128)(2,1)S(1)}, u32[]{:S(2)}, u32[]{:S(2)}) collective-permute-start(bf16[4,18432]{1,0:T(4,128)(2,1)S(1)} %get-tuple-element.42), channel_id=1, source_target_pairs={{0,6},{1,7},{2,4},{3,5},{4,2},{5,3},{6,0},{7,1},{8,14},{9,15},{10,... | collective-permute-start | bytes 442376 | tf_op jit(solution)/shard_map/ppermute | solution.py:66
  41.0 9.5 %collective-permute-start.19 = (bf16[4,18432]{1,0:T(4,128)(2,1)S(1)}, bf16[4,18432]{1,0:T(4,128)(2,1)S(1)}, u32[]{:S(2)}, u32[]{:S(2)}) collective-permute-start(bf16[4,18432]{1,0:T(4,128)(2,1)S(1)} %get-tuple-element.46), channel_id=1, source_target_pairs={{0,2},{1,3},{2,0},{3,1},{4,6},{5,7},{6,4},{7,5},{8,10},{9,11},{10,... | collective-permute-start | bytes 442376 | tf_op jit(solution)/shard_map/ppermute | solution.py:66
  42.1 8.8 %collective-permute-start.20 = (bf16[4,18432]{1,0:T(4,128)(2,1)S(1)}, bf16[4,18432]{1,0:T(4,128)(2,1)S(1)}, u32[]{:S(2)}, u32[]{:S(2)}) collective-permute-start(bf16[4,18432]{1,0:T(4,128)(2,1)S(1)} %get-tuple-element.47), channel_id=1, source_target_pairs={{0,4},{1,5},{2,6},{3,7},{4,0},{5,1},{6,2},{7,3},{8,12},{9,13},{10,... | collective-permute-start | bytes 442376 | tf_op jit(solution)/shard_map/ppermute | solution.py:66
  44.0 10.5 %collective-permute-start.21 = (bf16[4,18432]{1,0:T(4,128)(2,1)S(1)}, bf16[4,18432]{1,0:T(4,128)(2,1)S(1)}, u32[]{:S(2)}, u32[]{:S(2)}) collective-permute-start(bf16[4,18432]{1,0:T(4,128)(2,1)S(1)} %get-tuple-element.48), channel_id=1, source_target_pairs={{0,6},{1,7},{2,4},{3,5},{4,2},{5,3},{6,0},{7,1},{8,14},{9,15},{10,... | collective-permute-start | bytes 442376 | tf_op jit(solution)/shard_map/ppermute | solution.py:66
  47.8 11.0 %collective-permute-start.15 = (bf16[4,18432]{1,0:T(4,128)(2,1)S(1)}, bf16[4,18432]{1,0:T(4,128)(2,1)S(1)}, u32[]{:S(2)}, u32[]{:S(2)}) collective-permute-start(bf16[4,18432]{1,0:T(4,128)(2,1)S(1)} %get-tuple-element.44), channel_id=1, source_target_pairs={{0,8},{1,9},{2,10},{3,11},{4,12},{5,13},{6,14},{7,15},{8,0},{9,1},... | collective-permute-start | bytes 442376 | tf_op jit(solution)/shard_map/ppermute | solution.py:66
  54.7 8.5 %collective-permute-start.22 = (bf16[4,18432]{1,0:T(4,128)(2,1)S(1)}, bf16[4,18432]{1,0:T(4,128)(2,1)S(1)}, u32[]{:S(2)}, u32[]{:S(2)}) collective-permute-start(bf16[4,18432]{1,0:T(4,128)(2,1)S(1)} %get-tuple-element.50), channel_id=1, source_target_pairs={{0,8},{1,9},{2,10},{3,11},{4,12},{5,13},{6,14},{7,15},{8,0},{9,1},... | collective-permute-start | bytes 442376 | tf_op jit(solution)/shard_map/ppermute | solution.py:66
  58.9 6.3 %collective-permute-start.16 = (bf16[4,18432]{1,0:T(4,128)(2,1)S(1)}, bf16[4,18432]{1,0:T(4,128)(2,1)S(1)}, u32[]{:S(2)}, u32[]{:S(2)}) collective-permute-start(bf16[4,18432]{1,0:T(4,128)(2,1)S(1)} %add_convert_fusion.1.refs_2_), channel_id=1, source_target_pairs={{0,4},{1,5},{2,6},{3,7},{4,0},{5,1},{6,2},{7,3},{8,12},{9,13},{10,... | collective-permute-start | bytes 442376 | tf_op jit(solution)/shard_map/ppermute | solution.py:66
  59.0 8.0 %collective-permute-start.17 = (bf16[4,18432]{1,0:T(4,128)(2,1)S(1)}, bf16[4,18432]{1,0:T(4,128)(2,1)S(1)}, u32[]{:S(2)}, u32[]{:S(2)}) collective-permute-start(bf16[4,18432]{1,0:T(4,128)(2,1)S(1)} %add_convert_fusion.1.refs_2_), channel_id=1, source_target_pairs={{0,2},{1,3},{2,0},{3,1},{4,6},{5,7},{6,4},{7,5},{8,10},{9,11},{10,... | collective-permute-start | bytes 442376 | tf_op jit(solution)/shard_map/ppermute | solution.py:66
  61.1 8.2 %collective-permute-start.18 = (bf16[4,18432]{1,0:T(4,128)(2,1)S(1)}, bf16[4,18432]{1,0:T(4,128)(2,1)S(1)}, u32[]{:S(2)}, u32[]{:S(2)}) collective-permute-start(bf16[4,18432]{1,0:T(4,128)(2,1)S(1)} %add_convert_fusion.1.refs_2_), channel_id=1, source_target_pairs={{0,6},{1,7},{2,4},{3,5},{4,2},{5,3},{6,0},{7,1},{8,14},{9,15},{10,... | collective-permute-start | bytes 442376 | tf_op jit(solution)/shard_map/ppermute | solution.py:66
  63.4 7.2 %collective-permute-start.23 = (bf16[4,18432]{1,0:T(4,128)(2,1)S(1)}, bf16[4,18432]{1,0:T(4,128)(2,1)S(1)}, u32[]{:S(2)}, u32[]{:S(2)}) collective-permute-start(bf16[4,18432]{1,0:T(4,128)(2,1)S(1)} %add_convert_fusion.refs_2_), channel_id=1, source_target_pairs={{0,2},{1,3},{2,0},{3,1},{4,6},{5,7},{6,4},{7,5},{8,10},{9,11},{10,... | collective-permute-start | bytes 442376 | tf_op jit(solution)/shard_map/ppermute | solution.py:66
  64.9 6.7 %collective-permute-start.24 = (bf16[4,18432]{1,0:T(4,128)(2,1)S(1)}, bf16[4,18432]{1,0:T(4,128)(2,1)S(1)}, u32[]{:S(2)}, u32[]{:S(2)}) collective-permute-start(bf16[4,18432]{1,0:T(4,128)(2,1)S(1)} %add_convert_fusion.refs_2_), channel_id=1, source_target_pairs={{0,4},{1,5},{2,6},{3,7},{4,0},{5,1},{6,2},{7,3},{8,12},{9,13},{10,... | collective-permute-start | bytes 442376 | tf_op jit(solution)/shard_map/ppermute | solution.py:66
  65.3 9.0 %collective-permute-start.25 = (bf16[4,18432]{1,0:T(4,128)(2,1)S(1)}, bf16[4,18432]{1,0:T(4,128)(2,1)S(1)}, u32[]{:S(2)}, u32[]{:S(2)}) collective-permute-start(bf16[4,18432]{1,0:T(4,128)(2,1)S(1)} %add_convert_fusion.refs_2_), channel_id=1, source_target_pairs={{0,6},{1,7},{2,4},{3,5},{4,2},{5,3},{6,0},{7,1},{8,14},{9,15},{10,... | collective-permute-start | bytes 442376 | tf_op jit(solution)/shard_map/ppermute | solution.py:66
  (4 other events, 19.4 us)

commit v5 on v4

v5 whole, which is shorter than its diff:
```python
import functools

import jax
import jax.numpy as jnp
from jax import lax
from jax.experimental import pallas as pl
from jax.experimental.pallas import tpu as pltpu
from jax.sharding import PartitionSpec as P

F32 = jnp.float32
BF16 = jnp.bfloat16
NN = (((1,), (0,)), ((), ()))
NT = (((1,), (1,)), ((), ()))
LANES = 128
GRADIENT_VMEM = 18 * 1024 * 1024
SMALL_VMEM = 6 * 1024 * 1024


def general_local(inputs, grad_key, grad_value, key_down, key_up, value_down, value_up, validation, lengths):
    highest = lax.Precision.HIGHEST
    num_layers, local_examples, seq_slots, _ = inputs.shape
    total_count = lax.axis_size("ex") * local_examples
    low_rank = key_down.shape[1]
    token_mask = (
        lax.broadcasted_iota(jnp.int32, (local_examples, seq_slots), 1) < lengths[:, None]
    ).astype(F32)
    dot = functools.partial(jnp.einsum, preferred_element_type=F32)

    def masked(values):
        return (values * token_mask[None, :, :, None]).astype(BF16)

    z_key = masked(dot("lesd,lrd->lesr", inputs, key_down))
    z_value = masked(dot("lesd,lrd->lesr", inputs, value_down))
    y_key = masked(dot("leso,lor->lesr", grad_key, key_up))
    y_value = masked(dot("leso,lor->lesr", grad_value, value_up))
    pieces = [
        dot("lesr,lesd->lerd", y_key, inputs),
        dot("lesr,leso->lero", z_key, grad_key),
        dot("lesr,lesd->lerd", y_value, inputs),
        dot("lesr,leso->lero", z_value, grad_value),
    ]
    gradients = jnp.concatenate(pieces, axis=3).reshape(num_layers, local_examples, -1)
    squares = jnp.sum(gradients * gradients, axis=2)
    damping = 0.1 * lax.psum(jnp.sum(squares, axis=1), "ex") / total_count + 1e-06
    targets = lax.all_gather(validation, "ex", axis=2, tiled=True).astype(F32)
    products = jnp.einsum("lep,lvp->lev", gradients, targets, precision=highest)
    weights = products / (damping[:, None, None] + squares[:, :, None])
    directions = jnp.einsum("lev,lep->lvp", weights, gradients, precision=highest)
    summed = lax.psum(directions, "ex")
    correction = jnp.einsum("lep,lvp->lev", gradients, summed, precision=highest)
    inner = products - correction / total_count
    return -jnp.sum(inner / damping[:, None, None], axis=0)


CORE, Y, Z1, Z2 = 1, 2, 4, 8
QUAD = (Z1, Y, Y | Z1)
SLOTS = [bits | last for bits in (0, *QUAD) for last in (0, Z2)]


def swap(values, bit):
    size = lax.axis_size("ex")
    return lax.ppermute(values, "ex", [(index, index ^ bit) for index in range(size)])


def fold_lanes(values):
    tiles = [values[:, at : at + LANES] for at in range(0, values.shape[1], LANES)]
    while len(tiles) > 1:
        tiles = [sum(tiles[at : at + 2]) for at in range(0, len(tiles), 2)]
    return tiles[0]


def rank_order(index, rank):
    half = rank // 2
    row = lax.broadcasted_iota(jnp.int32, (2 * rank, 2 * rank), 0)
    column = lax.broadcasted_iota(jnp.int32, (2 * rank, 2 * rank), 1)
    position = row % half
    relative = position // 4 * Y + position // 2 % 2 * Z1 + position % 2 * Z2 + row // half % 2
    wanted = jnp.bitwise_xor(relative, jnp.broadcast_to(index, relative.shape)) + row // rank * rank
    return (column == wanted).astype(F32).astype(BF16)


def ordered(order, key, value):
    both = jnp.concatenate([key, value], axis=0)
    return lax.dot_general(order, both, NN, preferred_element_type=F32).astype(BF16)


class Unit:
    def __init__(self, number, length, up_factor, gk, gv, outputs):
        self.number, self.gk, self.gv = number, gk, gv
        self.own_ref, self.other_ref, self.square_ref = outputs
        self.seq, self.narrow = gk.shape
        self.rank = up_factor.shape[0] // 2
        token = lax.broadcasted_iota(jnp.int32, (1, self.seq), 1)
        self.mask = (token < length).astype(F32)
        y_key = lax.dot_general(up_factor[: self.rank], gk, NT, preferred_element_type=F32)
        y_value = lax.dot_general(up_factor[self.rank :], gv, NT, preferred_element_type=F32)
        self.y = (jnp.concatenate([y_key, y_value], axis=0) * self.mask).astype(BF16)
        self.z = jnp.zeros((2 * self.rank, self.seq), F32)
        self.total = jnp.zeros((self.rank // 2, LANES), F32)

    def store(self, values, at):
        columns, half = values.shape[1], self.rank // 2
        self.own_ref[self.number, :, at : at + columns] = values[:half]
        self.other_ref[self.number, :, at : at + columns] = values[half:]
        squared = values * values
        self.total += fold_lanes(squared[:half] + squared[half:])

    def chunk(self, factor, x, at, width):
        self.z += lax.dot_general(factor, x, NT, preferred_element_type=F32)
        down = lax.dot_general(self.y, x, NN, preferred_element_type=F32)
        self.store(down[: self.rank], at)
        self.store(down[self.rank :], width + self.narrow + at)

    def finish(self, width):
        z = (self.z * self.mask).astype(BF16)
        self.store(lax.dot_general(z[: self.rank], self.gk, NN, preferred_element_type=F32), width)
        up_value = lax.dot_general(z[self.rank :], self.gv, NN, preferred_element_type=F32)
        self.store(up_value, 2 * width + self.narrow)
        self.square_ref[self.number : self.number + 1] = jnp.sum(self.total, axis=0, keepdims=True)


def gradients_kernel(
    index_ref,
    lengths_ref,
    x_hbm,
    gk_hbm,
    gv_hbm,
    ak_hbm,
    av_hbm,
    bk_hbm,
    bv_hbm,
    own_ref,
    other_ref,
    square_ref,
    x_ref,
    gk_ref,
    gv_ref,
    a_ref,
    b_ref,
    semaphores,
    *,
    chunks,
):
    outputs = (own_ref, other_ref, square_ref)
    layers, _, rank, width = a_ref.shape
    examples = x_ref.shape[1]
    copies = {}

    def start(name, source, target):
        copies[name] = pltpu.make_async_copy(source, target, semaphores.at[len(copies)])
        copies[name].start()

    def wait(*names):
        for name in names:
            copies[name].wait()

    for layer in range(layers):
        start(("bk", layer), bk_hbm.at[layer], b_ref.at[layer, 0])
        start(("bv", layer), bv_hbm.at[layer], b_ref.at[layer, 1])
        start(("gk", layer), gk_hbm.at[layer], gk_ref.at[layer])
        start(("gv", layer), gv_hbm.at[layer], gv_ref.at[layer])
        start(("ak", layer), ak_hbm.at[layer], a_ref.at[layer, 0])
        start(("av", layer), av_hbm.at[layer], a_ref.at[layer, 1])
        for at in range(0, width, chunks[layer]):
            columns = pl.ds(at, chunks[layer])
            start(("x", layer, at), x_hbm.at[layer, :, :, columns], x_ref.at[layer, :, :, columns])

    order = rank_order(index_ref[0], rank)
    for layer in range(layers):
        wait(("bk", layer), ("bv", layer), ("gk", layer), ("gv", layer))
        up_factor = ordered(order, b_ref[layer, 0], b_ref[layer, 1])
        units = [
            Unit(layer * examples + at, lengths_ref[at], up_factor, gk_ref[layer, at], gv_ref[layer, at], outputs)
            for at in range(examples)
        ]
        wait(("ak", layer), ("av", layer))
        for at in range(0, width, COLUMNS * 2):
            columns = slice(at, at + COLUMNS * 2)
            factor = ordered(order, a_ref[layer, 0, :, columns], a_ref[layer, 1, :, columns])
            if at % chunks[layer] == 0:
                wait(("x", layer, at))
            for example, unit in enumerate(units):
                unit.chunk(factor, x_ref[layer, example, :, columns], at, width)
        for unit in units:
            unit.finish(width)


def gate_kernel(*refs):
    pass


IN_VMEM = pl.BlockSpec(memory_space=pltpu.VMEM)
IN_SMEM = pl.BlockSpec(memory_space=pltpu.SMEM)
ANYWHERE = pl.BlockSpec(memory_space=pl.ANY)
COLUMNS = 1024
STREAMS = (9216, 9216)
SQUARES, NORMS = 16, 20


def in_hbm(array):
    return pltpu.with_memory_space_constraint(array, pltpu.HBM)


def gradients_of(index, lengths, inputs, grad_key, grad_value, key_down, key_up, value_down, value_up, after):
    _, _, seq, width = inputs.shape
    narrow = grad_key.shape[3]
    rank = key_down.shape[1]
    rows = jax.ShapeDtypeStruct((4, rank // 2, 2 * (width + narrow)), F32)
    outputs = [rows, rows, jax.ShapeDtypeStruct((4, LANES), F32)]
    lengths = in_hbm(lengths)
    parameters = pltpu.CompilerParams(vmem_limit_bytes=GRADIENT_VMEM)
    own, other, squares = pl.pallas_call(
        functools.partial(gradients_kernel, chunks=(2048, 8192)),
        in_specs=[IN_SMEM] * 2 + [ANYWHERE] * 7,
        out_specs=[IN_VMEM] * 3,
        out_shape=outputs,
        scratch_shapes=[
            pltpu.VMEM((2, 2, seq, width), BF16),
            pltpu.VMEM((2, 2, seq, narrow), BF16),
            pltpu.VMEM((2, 2, seq, narrow), BF16),
            pltpu.VMEM((2, 2, rank, width), BF16),
            pltpu.VMEM((2, 2, rank, narrow), BF16),
            pltpu.SemaphoreType.DMA((17,)),
        ],
        compiler_params=parameters,
        cost_estimate=pl.CostEstimate(flops=1 << 32, bytes_accessed=1 << 24, transcendentals=0),
        name="gradients",
    )(
        index,
        lengths,
        in_hbm(inputs),
        in_hbm(grad_key),
        in_hbm(grad_value),
        in_hbm(key_down),
        in_hbm(value_down),
        in_hbm(jnp.swapaxes(key_up, 1, 2)),
        in_hbm(jnp.swapaxes(value_up, 1, 2)),
    )
    other, squares = pl.pallas_call(
        gate_kernel,
        in_specs=[ANYWHERE] * (2 + len(after)),
        out_specs=[ANYWHERE] * 2,
        out_shape=outputs[1:],
        input_output_aliases={0: 0, 1: 1},
        compiler_params=pltpu.CompilerParams(vmem_limit_bytes=SMALL_VMEM),
        cost_estimate=pl.CostEstimate(flops=1 << 10, bytes_accessed=1 << 10, transcendentals=0),
        name="gate",
    )(other, squares, *after)
    return own, other, squares


def example_of(refs, layer, number):
    return refs[number // 2], 2 * layer + number % 2


def chunks(width, body, init):
    def step(number, carry):
        return body(pl.multiple_of(number * COLUMNS, COLUMNS), carry)

    return lax.fori_loop(0, width // COLUMNS, step, init)


def dots_kernel(*refs, starts, offset, width, extras):
    target_refs = refs[2 : 2 + len(starts)]
    out_ref, extra_refs = refs[-1], refs[-1 - extras : -1]
    start_ref, tables = (extra_refs[0], extra_refs[1:]) if extras else (None, ())
    slots = refs[0].shape[1]
    for layer in range(2):

        def body(at, totals):
            pieces, filled = ([], []), 0
            for start, ref in zip(starts, target_refs):
                columns = pl.ds(at, COLUMNS)
                if len(ref.shape) == 3:
                    values = ref[layer, :, columns].astype(F32)
                else:
                    values = ref[4 * layer : 4 * layer + 4, columns].astype(F32)
                count = values.shape[0] // 2
                for target in range(2):
                    if start > filled:
                        pieces[target].append(jnp.zeros((start - filled, COLUMNS), F32))
                    pieces[target].append(values[target * count : (target + 1) * count])
                filled = start + count
            if filled < slots:
                for target in range(2):
                    pieces[target].append(jnp.zeros((slots - filled, COLUMNS), F32))
            rows = [jnp.concatenate(group, axis=0) for group in pieces]
            updated = []
            for number, total in enumerate(totals):
                ref, place = example_of(refs, layer, number // 2)
                gradient = ref[place, :, pl.ds(offset + at, COLUMNS)]
                updated.append(total + fold_lanes(gradient * rows[number % 2]))
            return tuple(updated)

        totals = chunks(width, body, (jnp.zeros((slots, LANES), F32),) * 8)
        for number, total in enumerate(totals):
            row = layer * 8 + number
            value = jnp.sum(total, axis=0, keepdims=True)
            out_ref[row : row + 1] = value + start_ref[row : row + 1] if start_ref is not None else value
    if tables:
        squares_ref, norms_ref, arrived_ref = tables
        out_ref[SQUARES:NORMS] = squares_ref[...]
        out_ref[NORMS:] = norms_ref[...] + arrived_ref[...]


def dots_of(rows, targets, extras=(), offset=0):
    flat = [*rows, *targets.values(), *extras]
    width = [*targets.values()][0].shape[-1]
    return pl.pallas_call(
        functools.partial(dots_kernel, starts=tuple(targets), offset=offset, width=width, extras=len(extras)),
        in_specs=[IN_VMEM] * len(flat),
        out_specs=IN_VMEM,
        out_shape=jax.ShapeDtypeStruct((NORMS + 2 if len(extras) > 1 else SQUARES, LANES), F32),
        compiler_params=pltpu.CompilerParams(vmem_limit_bytes=SMALL_VMEM),
        cost_estimate=pl.CostEstimate(flops=1 << 22, bytes_accessed=3 << 20, transcendentals=0),
        name="dots",
    )(*flat)


def directions_kernel(mine_ref, pair_ref, *refs, count, offset, width):
    block_refs = refs[-4:]
    weights = []
    for layer in range(2):
        mine, pair = mine_ref[8 * layer : 8 * layer + 8], pair_ref[8 * layer : 8 * layer + 8]
        products = jnp.sum(mine + jnp.concatenate([pair[4:], pair[:4]], axis=0), axis=1, keepdims=True)
        row = NORMS + layer
        norm = mine_ref[row : row + 1] + pair_ref[row : row + 1]
        damping = 0.1 * jnp.sum(norm, axis=1, keepdims=True) / count + 1e-06
        squares = []
        for number in range(4):
            row = SQUARES + 2 * layer + number % 2
            squares += [(mine_ref if number < 2 else pair_ref)[row : row + 1]] * 2
        scale = damping + jnp.sum(jnp.concatenate(squares, axis=0), axis=1, keepdims=True)
        weights.append(products / scale)

    def body(at, carry):
        parts = []
        for layer in range(2):
            gradients = []
            for number in range(4):
                ref, place = example_of(refs, layer, number)
                gradients.append(ref[place, :, pl.ds(offset + at, COLUMNS)])
            for target in range(2):
                terms = [weights[layer][2 * n + target : 2 * n + target + 1] * gradients[n] for n in range(4)]
                parts.append(sum(terms[1:], terms[0]))
        for block, ref in enumerate(block_refs):
            pieces = [part[2 * block : 2 * block + 2] for part in parts]
            ref[:, pl.ds(at, COLUMNS)] = jnp.concatenate(pieces, axis=0).astype(ref.dtype)
        return carry

    chunks(width, body, 0)


def directions_of(mine, pair, rows, count, offset, width):
    return pl.pallas_call(
        functools.partial(directions_kernel, count=count, offset=offset, width=width),
        in_specs=[IN_VMEM] * 4,
        out_specs=[IN_VMEM] * 4,
        out_shape=[jax.ShapeDtypeStruct((8, width), kind) for kind in (F32, BF16, BF16, BF16)],
        compiler_params=pltpu.CompilerParams(vmem_limit_bytes=SMALL_VMEM),
        cost_estimate=pl.CostEstimate(flops=1 << 22, bytes_accessed=3 << 20, transcendentals=0),
        name="directions",
    )(mine, pair, *rows)


def turn_kernel(keep_ref, *refs):
    rest_ref, send_ref = refs[-2:]
    total = keep_ref[...]
    for ref in refs[:-2]:
        total += ref[...].astype(F32)
    rest_ref[...] = total
    even = lax.broadcasted_iota(jnp.int32, total.shape, 0) % 2 == 0
    below, above = (jnp.concatenate([total[at:], total[:at]], axis=0) for at in (1, 7))
    send_ref[...] = jnp.where(even, below, above).astype(BF16)


def turned(keep, arrived):
    return pl.pallas_call(
        turn_kernel,
        out_shape=[jax.ShapeDtypeStruct(keep.shape, F32), jax.ShapeDtypeStruct(keep.shape, BF16)],
        compiler_params=pltpu.CompilerParams(vmem_limit_bytes=SMALL_VMEM),
        cost_estimate=pl.CostEstimate(flops=1 << 18, bytes_accessed=1 << 20, transcendentals=0),
        name="add",
    )(keep, *arrived)


def paired_local(inputs, grad_key, grad_value, key_down, key_up, value_down, value_up, validation, lengths):
    layers, examples = inputs.shape[:2]
    count = lax.axis_size("ex") * examples
    index = lax.axis_index("ex").astype(jnp.int32)[None]
    arguments = (index, lengths, inputs, grad_key, grad_value, key_down, key_up, value_down, value_up)

    targets = {0: validation}
    first_bits = (Y | Z1, Z2, Y, Z1)
    for bits in first_bits:
        targets[bits] = swap(validation, bits)
    own, other, squares = gradients_of(*arguments, after=[targets[bits] for bits in first_bits])
    rows = (own, swap(other, CORE))
    for bits in (Y, Z1):
        targets[bits | Z2] = swap(targets[Z2], bits)
    targets[Y | Z1 | Z2] = swap(targets[Z1 | Z2], Y)

    norms = jnp.stack([squares[0] + squares[1], squares[2] + squares[3]])
    for bit in (Y, Z1):
        norms = norms + swap(norms, bit)
    arrived = swap(norms, Z2)

    early = {at: targets[bits] for at, bits in enumerate(SLOTS) if bits in (0, *first_bits)}
    late = {at: targets[bits] for at, bits in enumerate(SLOTS) if bits not in (0, *first_bits)}
    mine = dots_of(rows, late, [dots_of(rows, early), squares, norms, arrived])
    pair = swap(mine, CORE)
    corrections, offset = [], 0
    for width in STREAMS:
        keep, *sends = directions_of(mine, pair, rows, count, offset, width)
        keep, send = turned(keep, [swap(send, bits) for send, bits in zip(sends, QUAD)])
        block = (keep + swap(send, Z2).astype(F32)).astype(BF16)
        blocks = {2 * at: swap(block, bits) if bits else block for at, bits in enumerate((0, *QUAD))}
        corrections = [dots_of(rows, blocks, corrections, offset)]
        offset += width
    damping = 0.1 * jnp.sum(mine[NORMS:] + pair[NORMS:], axis=1) / count + 1e-06
    inner = (mine[:SQUARES] - corrections[0] / count).reshape(layers, 4 * examples, LANES)
    split = 2 * examples
    inner = inner[:, :split] + swap(inner[:, split:], CORE)
    scores = -jnp.sum(jnp.sum(inner, axis=2) / damping[:, None], axis=0)
    return scores.reshape(examples, 2)


def solution(mesh):
    in_specs = (
        P(None, ("groups", "ex"), None, None),
        P(None, ("groups", "ex"), None, None),
        P(None, ("groups", "ex"), None, None),
        P(),
        P(),
        P(),
        P(),
        P(None, "groups", "ex"),
        P(("groups", "ex")),
    )
    out_specs = P(("groups", "ex"), None)

    def local(*arguments):
        low_rank = arguments[3].shape[1]
        row_width = 2 * (arguments[0].shape[3] + arguments[1].shape[3])
        paired = lax.axis_size("ex") == low_rank == 16 and arguments[0].shape[:2] == (2, 2)
        paired = paired and row_width == sum(STREAMS)
        return (paired_local if paired else general_local)(*arguments)

    return jax.shard_map(local, mesh=mesh, in_specs=in_specs, out_specs=out_specs, check_vma=False)
```

time: 77.3 us -> 73.9 us (0.956)
  Pallas kernels: 18.2 us -> 14.9 us
  starting transfers between devices: 31.2 us -> 29.7 us
  waiting for transfers between devices: 26.4 us -> 27.8 us
    pallas_call x8, Pallas kernels: 17.7 us -> 14.6 us  [the longest x1 8.32 us: gradients_of(): pl.pallas_call(functools.partial(gradients_kernel, chunks=(2048, 8192)),...]
    ppermute x27, starting transfers between devices: 31.2 us -> 29.7 us  [swap(): lax.ppermute(values, 'ex', [(index, index ^ bit) for index in range(size)])]
    ppermute x27, waiting for transfers between devices: 26.4 us -> 27.8 us  [swap(): lax.ppermute(values, 'ex', [(index, index ^ bit) for index in range(size)])]
  transfers between devices with their start and end apart: 27 -> 27, of which waited for: 18 -> 16; matrix products, arithmetic and copies ran while one was open for 0% -> 0% of each run, Pallas kernels for 15% -> 16%
where the time goes in v5:
time: 73.9 us; the launch traced here: 73.7 us
  starting transfers between devices  29.7 us (40%)
  waiting for transfers between devices  27.8 us (38%)
  Pallas kernels  14.9 us (20%)
    ppermute x27, starting transfers between devices, swap(): lax.ppermute(values, 'ex', [(index, index ^ bit) for index in range(size)])  29.7 us
    ppermute x27, waiting for transfers between devices, swap(): lax.ppermute(values, 'ex', [(index, index ^ bit) for index in range(size)])  27.8 us
    pallas_call x1, Pallas kernels, gradients_of(): pl.pallas_call(functools.partial(gradients_kernel, chunks=(2048, 8192)),...  8.32 us
    pallas_call x4, Pallas kernels, dots_of(): pl.pallas_call(functools.partial(dots_kernel, starts=tuple(targets), offs...  5 us
  transfers between devices with their start and end apart: 27, of which 16 were waited for; matrix products, arithmetic and copies ran while one was open for 0% of the time, Pallas kernels for 16%

profile of v5, /device:TPU:0, one launch (start us, length us, event | category | flops | bytes accessed | tf_op | source)
XLA Modules:
  0.0 73.7 jit_solution(10575968015151911730)
XLA Ops:
  0.0 4.0 %collective-permute-start = (bf16[2,2,18432]{2,1,0:T(2,128)(2,1)}, bf16[2,2,18432]{2,1,0:T(2,128)(2,1)S(1)}, u32[]{:S(2)}, u32[]{:S(2)}) collective-permute-start(bf16[2,2,18432]{2,1,0:T(2,128)(2,1)} %refs_2_.1), channel_id=1, source_target_pairs={{0,6},{1,7},{2,4},{3,5},{4,2},{5,3},{6,0},{7,1},{8,14},{9,15},{10,... | collective-permute-start | bytes 442376 | tf_op jit(solution)/shard_map/ppermute | solution.py:62
  4.0 2.6 %collective-permute-start.1 = (bf16[2,2,18432]{2,1,0:T(2,128)(2,1)}, bf16[2,2,18432]{2,1,0:T(2,128)(2,1)S(1)}, u32[]{:S(2)}, u32[]{:S(2)}) collective-permute-start(bf16[2,2,18432]{2,1,0:T(2,128)(2,1)} %refs_2_.1), channel_id=1, source_target_pairs={{0,8},{1,9},{2,10},{3,11},{4,12},{5,13},{6,14},{7,15},{8,0},{9,1},... | collective-permute-start | bytes 442376 | tf_op jit(solution)/shard_map/ppermute | solution.py:62
  7.5 8.3 %gradients.1 = (f32[4,8,18432]{2,1,0:T(8,128)S(1)}, f32[4,8,18432]{2,1,0:T(8,128)S(1)}, f32[4,128]{1,0:T(4,128)S(1)}) custom-call(s32[1]{0:T(128)} %bitcast.index_ref, s32[2]{0:T(128)} %lengths_ref.1, bf16[2,2,128,8192]{3,2,1,0:T(8,128)(2,1)} %x_hbm.1, bf16[2,2,128,1024]{3,2,1,0:T(8,128)(2,1)} %gk_hbm.1, bf16[2,2,128,1024]{3,2,1,0:T(8,128)(2,1)} %gv_hbm.1, ...), custom_call_target="tpu_custom_call" | custom-call | flops 4294967296 | bytes 16777216 | tf_op jit(solution)/shard_map/gradients/pallas_call | solution.py:212
  16.0 1.6 %collective-permute-start.8 = (f32[2,128]{1,0:T(2,128)S(1)}, f32[2,128]{1,0:T(2,128)S(1)}, u32[]{:S(2)}, u32[]{:S(2)}) collective-permute-start(f32[2,128]{1,0:T(2,128)S(1)} %pad_maximum_fusion), channel_id=1, source_target_pairs={{0,2},{1,3},{2,0},{3,1},{4,6},{5,7},{6,4},{7,5},{8,10},{9,11},{10,... | collective-permute-start | bytes 3080 | tf_op jit(solution)/shard_map/ppermute | solution.py:62
  17.6 1.6 %collective-permute-start.5 = (bf16[2,2,18432]{2,1,0:T(2,128)(2,1)S(1)}, bf16[2,2,18432]{2,1,0:T(2,128)(2,1)S(1)}, u32[]{:S(2)}, u32[]{:S(2)}) collective-permute-start(bf16[2,2,18432]{2,1,0:T(2,128)(2,1)S(1)} %collective-permute-done.1.refs_3_), channel_id=1, source_target_pairs={{0,4},{1,5},{2,6},{3,7},{4,0},{5,1},{6,2},{7,3},{8,12},{9,13},{10,... | collective-permute-start | bytes 442376 | tf_op jit(solution)/shard_map/ppermute | solution.py:62
  19.7 1.6 %collective-permute-start.9 = (f32[2,128]{1,0:T(2,128)S(1)}, f32[2,128]{1,0:T(2,128)S(1)}, u32[]{:S(2)}, u32[]{:S(2)}) collective-permute-start(f32[2,128]{1,0:T(2,128)S(1)} %fusion.3), channel_id=1, source_target_pairs={{0,4},{1,5},{2,6},{3,7},{4,0},{5,1},{6,2},{7,3},{8,12},{9,13},{10,... | collective-permute-start | bytes 3080 | tf_op jit(solution)/shard_map/ppermute | solution.py:62
  21.3 1.5 %collective-permute-start.6 = (bf16[2,2,18432]{2,1,0:T(2,128)(2,1)S(1)}, bf16[2,2,18432]{2,1,0:T(2,128)(2,1)S(1)}, u32[]{:S(2)}, u32[]{:S(2)}) collective-permute-start(bf16[2,2,18432]{2,1,0:T(2,128)(2,1)S(1)} %collective-permute-done.1.refs_3_), channel_id=1, source_target_pairs={{0,2},{1,3},{2,0},{3,1},{4,6},{5,7},{6,4},{7,5},{8,10},{9,11},{10,... | collective-permute-start | bytes 442376 | tf_op jit(solution)/shard_map/ppermute | solution.py:62
  25.3 1.8 %dots.4.refs_5_ = f32[16,128]{1,0:T(8,128)S(1)} custom-call(f32[4,8,18432]{2,1,0:T(8,128)S(1)} %get-tuple-element.22.refs_0_, f32[4,8,18432]{2,1,0:T(8,128)S(1)} %collective-permute-done.4.refs_1_, bf16[2,2,18432]{2,1,0:T(2,128)(2,1)S(1)} %copy-done, bf16[2,2,18432]{2,1,0:T(2,128)(2,1)S(1)} %collective-permute-done.1.refs_3_, ...), custom_call_target="tpu_custom_call" | custom-call | flops 4194304 | bytes 3145728 | tf_op jit(solution)/shard_map/dots/pallas_call | solution.py:309
  27.2 1.5 %collective-permute-done.10.refs_8_ = f32[2,128]{1,0:T(2,128)S(1)} collective-permute-done((f32[2,128]{1,0:T(2,128)S(1)}, f32[2,128]{1,0:T(2,128)S(1)}, u32[]{:S(2)}, u32[]{:S(2)}) %collective-permute-start.10) | collective-permute-done | bytes 1056 | tf_op jit(solution)/shard_map/ppermute | solution.py:62
  29.6 1.5 %dots.5.mine_ref = f32[22,128]{1,0:T(8,128)S(1)} custom-call(f32[4,8,18432]{2,1,0:T(8,128)S(1)} %get-tuple-element.22.refs_0_, f32[4,8,18432]{2,1,0:T(8,128)S(1)} %collective-permute-done.4.refs_1_, bf16[2,2,18432]{2,1,0:T(2,128)(2,1)S(1)} %collective-permute-done.5.refs_2_, bf16[2,2,18432]{2,1,0:T(2,128)(2,1)S(1)} %collective-permute-done.6.refs_3_, ...), custom_call_target="tpu_custom_call" | custom-call | flops 4194304 | bytes 3145728 | tf_op jit(solution)/shard_map/dots/pallas_call | solution.py:309
  33.8 1.4 %collective-permute-start.20 = (bf16[8,9216]{1,0:T(8,128)(2,1)S(1)}, bf16[8,9216]{1,0:T(8,128)(2,1)S(1)}, u32[]{:S(2)}, u32[]{:S(2)}) collective-permute-start(bf16[8,9216]{1,0:T(8,128)(2,1)S(1)} %get-tuple-element.35), channel_id=1, source_target_pairs={{0,2},{1,3},{2,0},{3,1},{4,6},{5,7},{6,4},{7,5},{8,10},{9,11},{10,... | collective-permute-start | bytes 442376 | tf_op jit(solution)/shard_map/ppermute | solution.py:62
  35.3 1.4 %collective-permute-start.21 = (bf16[8,9216]{1,0:T(8,128)(2,1)S(1)}, bf16[8,9216]{1,0:T(8,128)(2,1)S(1)}, u32[]{:S(2)}, u32[]{:S(2)}) collective-permute-start(bf16[8,9216]{1,0:T(8,128)(2,1)S(1)} %get-tuple-element.36), channel_id=1, source_target_pairs={{0,6},{1,7},{2,4},{3,5},{4,2},{5,3},{6,0},{7,1},{8,14},{9,15},{10,... | collective-permute-start | bytes 442376 | tf_op jit(solution)/shard_map/ppermute | solution.py:62
  38.1 1.4 %collective-permute-start.13 = (bf16[8,9216]{1,0:T(8,128)(2,1)S(1)}, bf16[8,9216]{1,0:T(8,128)(2,1)S(1)}, u32[]{:S(2)}, u32[]{:S(2)}) collective-permute-start(bf16[8,9216]{1,0:T(8,128)(2,1)S(1)} %get-tuple-element.29), channel_id=1, source_target_pairs={{0,2},{1,3},{2,0},{3,1},{4,6},{5,7},{6,4},{7,5},{8,10},{9,11},{10,... | collective-permute-start | bytes 442376 | tf_op jit(solution)/shard_map/ppermute | solution.py:62
  39.8 1.6 %collective-permute-start.14 = (bf16[8,9216]{1,0:T(8,128)(2,1)S(1)}, bf16[8,9216]{1,0:T(8,128)(2,1)S(1)}, u32[]{:S(2)}, u32[]{:S(2)}) collective-permute-start(bf16[8,9216]{1,0:T(8,128)(2,1)S(1)} %get-tuple-element.30), channel_id=1, source_target_pairs={{0,6},{1,7},{2,4},{3,5},{4,2},{5,3},{6,0},{7,1},{8,14},{9,15},{10,... | collective-permute-start | bytes 442376 | tf_op jit(solution)/shard_map/ppermute | solution.py:62
  41.4 2.2 %collective-permute-done.21.refs_2_ = bf16[8,9216]{1,0:T(8,128)(2,1)S(1)} collective-permute-done((bf16[8,9216]{1,0:T(8,128)(2,1)S(1)}, bf16[8,9216]{1,0:T(8,128)(2,1)S(1)}, u32[]{:S(2)}, u32[]{:S(2)}) %collective-permute-start.21) | collective-permute-done | bytes 147488 | tf_op jit(solution)/shard_map/ppermute | solution.py:62
  44.5 3.3 %collective-permute-done.12.refs_0_ = bf16[8,9216]{1,0:T(8,128)(2,1)S(1)} collective-permute-done((bf16[8,9216]{1,0:T(8,128)(2,1)S(1)}, bf16[8,9216]{1,0:T(8,128)(2,1)S(1)}, u32[]{:S(2)}, u32[]{:S(2)}) %collective-permute-start.12) | collective-permute-done | bytes 147488 | tf_op jit(solution)/shard_map/ppermute | solution.py:62
  47.8 3.9 %collective-permute-done.14.refs_2_ = bf16[8,9216]{1,0:T(8,128)(2,1)S(1)} collective-permute-done((bf16[8,9216]{1,0:T(8,128)(2,1)S(1)}, bf16[8,9216]{1,0:T(8,128)(2,1)S(1)}, u32[]{:S(2)}, u32[]{:S(2)}) %collective-permute-start.14) | collective-permute-done | bytes 147488 | tf_op jit(solution)/shard_map/ppermute | solution.py:62
  55.2 1.5 %collective-permute-start.25 = (bf16[8,9216]{1,0:T(8,128)(2,1)S(1)}, bf16[8,9216]{1,0:T(8,128)(2,1)S(1)}, u32[]{:S(2)}, u32[]{:S(2)}) collective-permute-start(bf16[8,9216]{1,0:T(8,128)(2,1)S(1)} %add_convert_fusion.refs_2_), channel_id=1, source_target_pairs={{0,6},{1,7},{2,4},{3,5},{4,2},{5,3},{6,0},{7,1},{8,14},{9,15},{10,... | collective-permute-start | bytes 442376 | tf_op jit(solution)/shard_map/ppermute | solution.py:62
  56.6 3.2 %collective-permute-done.15 = bf16[8,9216]{1,0:T(8,128)(2,1)S(1)} collective-permute-done((bf16[8,9216]{1,0:T(8,128)(2,1)S(1)}, bf16[8,9216]{1,0:T(8,128)(2,1)S(1)}, u32[]{:S(2)}, u32[]{:S(2)}) %collective-permute-start.15) | collective-permute-done | bytes 147488 | tf_op jit(solution)/shard_map/ppermute | solution.py:62
  60.0 1.3 %collective-permute-start.17 = (bf16[8,9216]{1,0:T(8,128)(2,1)S(1)}, bf16[8,9216]{1,0:T(8,128)(2,1)S(1)}, u32[]{:S(2)}, u32[]{:S(2)}) collective-permute-start(bf16[8,9216]{1,0:T(8,128)(2,1)S(1)} %add_convert_fusion.1.refs_2_), channel_id=1, source_target_pairs={{0,2},{1,3},{2,0},{3,1},{4,6},{5,7},{6,4},{7,5},{8,10},{9,11},{10,... | collective-permute-start | bytes 442376 | tf_op jit(solution)/shard_map/ppermute | solution.py:62
  61.3 1.3 %collective-permute-done.23.refs_3_ = bf16[8,9216]{1,0:T(8,128)(2,1)S(1)} collective-permute-done((bf16[8,9216]{1,0:T(8,128)(2,1)S(1)}, bf16[8,9216]{1,0:T(8,128)(2,1)S(1)}, u32[]{:S(2)}, u32[]{:S(2)}) %collective-permute-start.23) | collective-permute-done | bytes 147488 | tf_op jit(solution)/shard_map/ppermute | solution.py:62
  63.6 2.2 %collective-permute-done.25.refs_5_ = bf16[8,9216]{1,0:T(8,128)(2,1)S(1)} collective-permute-done((bf16[8,9216]{1,0:T(8,128)(2,1)S(1)}, bf16[8,9216]{1,0:T(8,128)(2,1)S(1)}, u32[]{:S(2)}, u32[]{:S(2)}) %collective-permute-start.25) | collective-permute-done | bytes 147488 | tf_op jit(solution)/shard_map/ppermute | solution.py:62
  66.6 2.2 %collective-permute-done.16.refs_3_ = bf16[8,9216]{1,0:T(8,128)(2,1)S(1)} collective-permute-done((bf16[8,9216]{1,0:T(8,128)(2,1)S(1)}, bf16[8,9216]{1,0:T(8,128)(2,1)S(1)}, u32[]{:S(2)}, u32[]{:S(2)}) %collective-permute-start.16) | collective-permute-done | bytes 147488 | tf_op jit(solution)/shard_map/ppermute | solution.py:62
  68.9 2.0 %collective-permute-done.18.refs_5_ = bf16[8,9216]{1,0:T(8,128)(2,1)S(1)} collective-permute-done((bf16[8,9216]{1,0:T(8,128)(2,1)S(1)}, bf16[8,9216]{1,0:T(8,128)(2,1)S(1)}, u32[]{:S(2)}, u32[]{:S(2)}) %collective-permute-start.18) | collective-permute-done | bytes 147488 | tf_op jit(solution)/shard_map/ppermute | solution.py:62
  (56 shorter events, 18.6 us)
Async XLA Ops:
  0.0 15.9 %collective-permute-start = (bf16[2,2,18432]{2,1,0:T(2,128)(2,1)}, bf16[2,2,18432]{2,1,0:T(2,128)(2,1)S(1)}, u32[]{:S(2)}, u32[]{:S(2)}) collective-permute-start(bf16[2,2,18432]{2,1,0:T(2,128)(2,1)} %refs_2_.1), channel_id=1, source_target_pairs={{0,6},{1,7},{2,4},{3,5},{4,2},{5,3},{6,0},{7,1},{8,14},{9,15},{10,... | collective-permute-start | bytes 442376 | tf_op jit(solution)/shard_map/ppermute | solution.py:62
  4.0 11.9 %collective-permute-start.1 = (bf16[2,2,18432]{2,1,0:T(2,128)(2,1)}, bf16[2,2,18432]{2,1,0:T(2,128)(2,1)S(1)}, u32[]{:S(2)}, u32[]{:S(2)}) collective-permute-start(bf16[2,2,18432]{2,1,0:T(2,128)(2,1)} %refs_2_.1), channel_id=1, source_target_pairs={{0,8},{1,9},{2,10},{3,11},{4,12},{5,13},{6,14},{7,15},{8,0},{9,1},... | collective-permute-start | bytes 442376 | tf_op jit(solution)/shard_map/ppermute | solution.py:62
  6.6 9.3 %collective-permute-start.2 = (bf16[2,2,18432]{2,1,0:T(2,128)(2,1)}, bf16[2,2,18432]{2,1,0:T(2,128)(2,1)S(1)}, u32[]{:S(2)}, u32[]{:S(2)}) collective-permute-start(bf16[2,2,18432]{2,1,0:T(2,128)(2,1)} %refs_2_.1), channel_id=1, source_target_pairs={{0,2},{1,3},{2,0},{3,1},{4,6},{5,7},{6,4},{7,5},{8,10},{9,11},{10,... | collective-permute-start | bytes 442376 | tf_op jit(solution)/shard_map/ppermute | solution.py:62
  7.1 8.8 %collective-permute-start.3 = (bf16[2,2,18432]{2,1,0:T(2,128)(2,1)}, bf16[2,2,18432]{2,1,0:T(2,128)(2,1)S(1)}, u32[]{:S(2)}, u32[]{:S(2)}) collective-permute-start(bf16[2,2,18432]{2,1,0:T(2,128)(2,1)} %refs_2_.1), channel_id=1, source_target_pairs={{0,4},{1,5},{2,6},{3,7},{4,0},{5,1},{6,2},{7,3},{8,12},{9,13},{10,... | collective-permute-start | bytes 442376 | tf_op jit(solution)/shard_map/ppermute | solution.py:62
  15.9 9.4 %collective-permute-start.4 = (f32[4,8,18432]{2,1,0:T(8,128)S(1)}, f32[4,8,18432]{2,1,0:T(8,128)S(1)}, u32[]{:S(2)}, u32[]{:S(2)}) collective-permute-start(f32[4,8,18432]{2,1,0:T(8,128)S(1)} %get-tuple-element.25), channel_id=1, source_target_pairs={{0,1},{1,0},{2,3},{3,2},{4,5},{5,4},{6,7},{7,6},{8,9},{9,8},{10,11... | collective-permute-start | bytes 7077896 | tf_op jit(solution)/shard_map/ppermute | solution.py:62
  17.6 6.0 %collective-permute-start.5 = (bf16[2,2,18432]{2,1,0:T(2,128)(2,1)S(1)}, bf16[2,2,18432]{2,1,0:T(2,128)(2,1)S(1)}, u32[]{:S(2)}, u32[]{:S(2)}) collective-permute-start(bf16[2,2,18432]{2,1,0:T(2,128)(2,1)S(1)} %collective-permute-done.1.refs_3_), channel_id=1, source_target_pairs={{0,4},{1,5},{2,6},{3,7},{4,0},{5,1},{6,2},{7,3},{8,12},{9,13},{10,... | collective-permute-start | bytes 442376 | tf_op jit(solution)/shard_map/ppermute | solution.py:62
  19.7 4.4 %collective-permute-start.9 = (f32[2,128]{1,0:T(2,128)S(1)}, f32[2,128]{1,0:T(2,128)S(1)}, u32[]{:S(2)}, u32[]{:S(2)}) collective-permute-start(f32[2,128]{1,0:T(2,128)S(1)} %fusion.3), channel_id=1, source_target_pairs={{0,4},{1,5},{2,6},{3,7},{4,0},{5,1},{6,2},{7,3},{8,12},{9,13},{10,... | collective-permute-start | bytes 3080 | tf_op jit(solution)/shard_map/ppermute | solution.py:62
  21.3 7.3 %collective-permute-start.6 = (bf16[2,2,18432]{2,1,0:T(2,128)(2,1)S(1)}, bf16[2,2,18432]{2,1,0:T(2,128)(2,1)S(1)}, u32[]{:S(2)}, u32[]{:S(2)}) collective-permute-start(bf16[2,2,18432]{2,1,0:T(2,128)(2,1)S(1)} %collective-permute-done.1.refs_3_), channel_id=1, source_target_pairs={{0,2},{1,3},{2,0},{3,1},{4,6},{5,7},{6,4},{7,5},{8,10},{9,11},{10,... | collective-permute-start | bytes 442376 | tf_op jit(solution)/shard_map/ppermute | solution.py:62
  23.6 6.0 %collective-permute-start.7 = (bf16[2,2,18432]{2,1,0:T(2,128)(2,1)S(1)}, bf16[2,2,18432]{2,1,0:T(2,128)(2,1)S(1)}, u32[]{:S(2)}, u32[]{:S(2)}) collective-permute-start(bf16[2,2,18432]{2,1,0:T(2,128)(2,1)S(1)} %collective-permute-done.5.refs_2_), channel_id=1, source_target_pairs={{0,2},{1,3},{2,0},{3,1},{4,6},{5,7},{6,4},{7,5},{8,10},{9,11},{10,... | collective-permute-start | bytes 442376 | tf_op jit(solution)/shard_map/ppermute | solution.py:62
  24.1 4.5 %collective-permute-start.10 = (f32[2,128]{1,0:T(2,128)S(1)}, f32[2,128]{1,0:T(2,128)S(1)}, u32[]{:S(2)}, u32[]{:S(2)}) collective-permute-start(f32[2,128]{1,0:T(2,128)S(1)} %fusion.4.refs_7_), channel_id=1, source_target_pairs={{0,8},{1,9},{2,10},{3,11},{4,12},{5,13},{6,14},{7,15},{8,0},{9,1},... | collective-permute-start | bytes 3080 | tf_op jit(solution)/shard_map/ppermute | solution.py:62
  33.1 6.8 %collective-permute-start.19 = (bf16[8,9216]{1,0:T(8,128)(2,1)S(1)}, bf16[8,9216]{1,0:T(8,128)(2,1)S(1)}, u32[]{:S(2)}, u32[]{:S(2)}) collective-permute-start(bf16[8,9216]{1,0:T(8,128)(2,1)S(1)} %get-tuple-element.34), channel_id=1, source_target_pairs={{0,4},{1,5},{2,6},{3,7},{4,0},{5,1},{6,2},{7,3},{8,12},{9,13},{10,... | collective-permute-start | bytes 442376 | tf_op jit(solution)/shard_map/ppermute | solution.py:62
  33.8 7.6 %collective-permute-start.20 = (bf16[8,9216]{1,0:T(8,128)(2,1)S(1)}, bf16[8,9216]{1,0:T(8,128)(2,1)S(1)}, u32[]{:S(2)}, u32[]{:S(2)}) collective-permute-start(bf16[8,9216]{1,0:T(8,128)(2,1)S(1)} %get-tuple-element.35), channel_id=1, source_target_pairs={{0,2},{1,3},{2,0},{3,1},{4,6},{5,7},{6,4},{7,5},{8,10},{9,11},{10,... | collective-permute-start | bytes 442376 | tf_op jit(solution)/shard_map/ppermute | solution.py:62
  35.3 8.4 %collective-permute-start.21 = (bf16[8,9216]{1,0:T(8,128)(2,1)S(1)}, bf16[8,9216]{1,0:T(8,128)(2,1)S(1)}, u32[]{:S(2)}, u32[]{:S(2)}) collective-permute-start(bf16[8,9216]{1,0:T(8,128)(2,1)S(1)} %get-tuple-element.36), channel_id=1, source_target_pairs={{0,6},{1,7},{2,4},{3,5},{4,2},{5,3},{6,0},{7,1},{8,14},{9,15},{10,... | collective-permute-start | bytes 442376 | tf_op jit(solution)/shard_map/ppermute | solution.py:62
  37.3 10.5 %collective-permute-start.12 = (bf16[8,9216]{1,0:T(8,128)(2,1)S(1)}, bf16[8,9216]{1,0:T(8,128)(2,1)S(1)}, u32[]{:S(2)}, u32[]{:S(2)}) collective-permute-start(bf16[8,9216]{1,0:T(8,128)(2,1)S(1)} %get-tuple-element.28), channel_id=1, source_target_pairs={{0,4},{1,5},{2,6},{3,7},{4,0},{5,1},{6,2},{7,3},{8,12},{9,13},{10,... | collective-permute-start | bytes 442376 | tf_op jit(solution)/shard_map/ppermute | solution.py:62
  38.1 9.7 %collective-permute-start.13 = (bf16[8,9216]{1,0:T(8,128)(2,1)S(1)}, bf16[8,9216]{1,0:T(8,128)(2,1)S(1)}, u32[]{:S(2)}, u32[]{:S(2)}) collective-permute-start(bf16[8,9216]{1,0:T(8,128)(2,1)S(1)} %get-tuple-element.29), channel_id=1, source_target_pairs={{0,2},{1,3},{2,0},{3,1},{4,6},{5,7},{6,4},{7,5},{8,10},{9,11},{10,... | collective-permute-start | bytes 442376 | tf_op jit(solution)/shard_map/ppermute | solution.py:62
  39.8 11.8 %collective-permute-start.14 = (bf16[8,9216]{1,0:T(8,128)(2,1)S(1)}, bf16[8,9216]{1,0:T(8,128)(2,1)S(1)}, u32[]{:S(2)}, u32[]{:S(2)}) collective-permute-start(bf16[8,9216]{1,0:T(8,128)(2,1)S(1)} %get-tuple-element.30), channel_id=1, source_target_pairs={{0,6},{1,7},{2,4},{3,5},{4,2},{5,3},{6,0},{7,1},{8,14},{9,15},{10,... | collective-permute-start | bytes 442376 | tf_op jit(solution)/shard_map/ppermute | solution.py:62
  43.8 9.2 %collective-permute-start.22 = (bf16[8,9216]{1,0:T(8,128)(2,1)S(1)}, bf16[8,9216]{1,0:T(8,128)(2,1)S(1)}, u32[]{:S(2)}, u32[]{:S(2)}) collective-permute-start(bf16[8,9216]{1,0:T(8,128)(2,1)S(1)} %get-tuple-element.38), channel_id=1, source_target_pairs={{0,8},{1,9},{2,10},{3,11},{4,12},{5,13},{6,14},{7,15},{8,0},{9,1},... | collective-permute-start | bytes 442376 | tf_op jit(solution)/shard_map/ppermute | solution.py:62
  51.8 8.1 %collective-permute-start.15 = (bf16[8,9216]{1,0:T(8,128)(2,1)S(1)}, bf16[8,9216]{1,0:T(8,128)(2,1)S(1)}, u32[]{:S(2)}, u32[]{:S(2)}) collective-permute-start(bf16[8,9216]{1,0:T(8,128)(2,1)S(1)} %get-tuple-element.32), channel_id=1, source_target_pairs={{0,8},{1,9},{2,10},{3,11},{4,12},{5,13},{6,14},{7,15},{8,0},{9,1},... | collective-permute-start | bytes 442376 | tf_op jit(solution)/shard_map/ppermute | solution.py:62
  53.1 9.5 %collective-permute-start.23 = (bf16[8,9216]{1,0:T(8,128)(2,1)S(1)}, bf16[8,9216]{1,0:T(8,128)(2,1)S(1)}, u32[]{:S(2)}, u32[]{:S(2)}) collective-permute-start(bf16[8,9216]{1,0:T(8,128)(2,1)S(1)} %add_convert_fusion.refs_2_), channel_id=1, source_target_pairs={{0,4},{1,5},{2,6},{3,7},{4,0},{5,1},{6,2},{7,3},{8,12},{9,13},{10,... | collective-permute-start | bytes 442376 | tf_op jit(solution)/shard_map/ppermute | solution.py:62
  53.9 9.7 %collective-permute-start.24 = (bf16[8,9216]{1,0:T(8,128)(2,1)S(1)}, bf16[8,9216]{1,0:T(8,128)(2,1)S(1)}, u32[]{:S(2)}, u32[]{:S(2)}) collective-permute-start(bf16[8,9216]{1,0:T(8,128)(2,1)S(1)} %add_convert_fusion.refs_2_), channel_id=1, source_target_pairs={{0,2},{1,3},{2,0},{3,1},{4,6},{5,7},{6,4},{7,5},{8,10},{9,11},{10,... | collective-permute-start | bytes 442376 | tf_op jit(solution)/shard_map/ppermute | solution.py:62
  55.2 10.6 %collective-permute-start.25 = (bf16[8,9216]{1,0:T(8,128)(2,1)S(1)}, bf16[8,9216]{1,0:T(8,128)(2,1)S(1)}, u32[]{:S(2)}, u32[]{:S(2)}) collective-permute-start(bf16[8,9216]{1,0:T(8,128)(2,1)S(1)} %add_convert_fusion.refs_2_), channel_id=1, source_target_pairs={{0,6},{1,7},{2,4},{3,5},{4,2},{5,3},{6,0},{7,1},{8,14},{9,15},{10,... | collective-permute-start | bytes 442376 | tf_op jit(solution)/shard_map/ppermute | solution.py:62
  59.9 8.9 %collective-permute-start.16 = (bf16[8,9216]{1,0:T(8,128)(2,1)S(1)}, bf16[8,9216]{1,0:T(8,128)(2,1)S(1)}, u32[]{:S(2)}, u32[]{:S(2)}) collective-permute-start(bf16[8,9216]{1,0:T(8,128)(2,1)S(1)} %add_convert_fusion.1.refs_2_), channel_id=1, source_target_pairs={{0,4},{1,5},{2,6},{3,7},{4,0},{5,1},{6,2},{7,3},{8,12},{9,13},{10,... | collective-permute-start | bytes 442376 | tf_op jit(solution)/shard_map/ppermute | solution.py:62
  60.0 8.9 %collective-permute-start.17 = (bf16[8,9216]{1,0:T(8,128)(2,1)S(1)}, bf16[8,9216]{1,0:T(8,128)(2,1)S(1)}, u32[]{:S(2)}, u32[]{:S(2)}) collective-permute-start(bf16[8,9216]{1,0:T(8,128)(2,1)S(1)} %add_convert_fusion.1.refs_2_), channel_id=1, source_target_pairs={{0,2},{1,3},{2,0},{3,1},{4,6},{5,7},{6,4},{7,5},{8,10},{9,11},{10,... | collective-permute-start | bytes 442376 | tf_op jit(solution)/shard_map/ppermute | solution.py:62
  62.6 8.3 %collective-permute-start.18 = (bf16[8,9216]{1,0:T(8,128)(2,1)S(1)}, bf16[8,9216]{1,0:T(8,128)(2,1)S(1)}, u32[]{:S(2)}, u32[]{:S(2)}) collective-permute-start(bf16[8,9216]{1,0:T(8,128)(2,1)S(1)} %add_convert_fusion.1.refs_2_), channel_id=1, source_target_pairs={{0,6},{1,7},{2,4},{3,5},{4,2},{5,3},{6,0},{7,1},{8,14},{9,15},{10,... | collective-permute-start | bytes 442376 | tf_op jit(solution)/shard_map/ppermute | solution.py:62
  (4 other events, 15.6 us)

commit v6 on v5

--- a/solution.py
+++ b/solution.py
@@ -405,8 +405,8 @@
         norms = norms + swap(norms, bit)
     arrived = swap(norms, Z2)
 
-    early = {at: targets[bits] for at, bits in enumerate(SLOTS) if bits in (0, *first_bits)}
-    late = {at: targets[bits] for at, bits in enumerate(SLOTS) if bits not in (0, *first_bits)}
+    early = {at: targets[bits] for at, bits in enumerate(SLOTS) if bits != Y | Z1 | Z2}
+    late = {at: targets[bits] for at, bits in enumerate(SLOTS) if bits == Y | Z1 | Z2}
     mine = dots_of(rows, late, [dots_of(rows, early), squares, norms, arrived])
     pair = swap(mine, CORE)
     corrections, offset = [], 0
@@ -414,7 +414,11 @@
         keep, *sends = directions_of(mine, pair, rows, count, offset, width)
         keep, send = turned(keep, [swap(send, bits) for send, bits in zip(sends, QUAD)])
         block = (keep + swap(send, Z2).astype(F32)).astype(BF16)
-        blocks = {2 * at: swap(block, bits) if bits else block for at, bits in enumerate((0, *QUAD))}
+        blocks = {0: block, 2: swap(block, Z1), 4: swap(block, Y)}
+        is_last = offset + width == sum(STREAMS)
+        blocks[6] = swap(block, Y | Z1) if is_last else swap(blocks[2], Y)
+        if is_last:
+            corrections = [dots_of(rows, {at: blocks.pop(at) for at in (0, 2)}, corrections, offset)]
         corrections = [dots_of(rows, blocks, corrections, offset)]
         offset += width
     damping = 0.1 * jnp.sum(mine[NORMS:] + pair[NORMS:], axis=1) / count + 1e-06

time: 73.9 us -> 72.6 us (0.982)
  waiting for transfers between devices: 27.8 us -> 26.7 us
    ppermute x27, waiting for transfers between devices: 27.8 us -> 26.7 us  [swap(): lax.ppermute(values, 'ex', [(index, index ^ bit) for index in range(size)])]
    pallas_call x4 -> x5, Pallas kernels: 5 us -> 5.16 us  [dots_of(): pl.pallas_call(functools.partial(dots_kernel, starts=tuple(targets), offs...]
  transfers between devices with their start and end apart: 27 -> 27, of which waited for: 16 -> 16; matrix products, arithmetic and copies ran while one was open for 0% -> 0% of each run, Pallas kernels for 16% -> 18%
where the time goes in v6:
time: 72.6 us; the launch traced here: 72.4 us
  starting transfers between devices  29.4 us (40%)
  waiting for transfers between devices  26.7 us (37%)
  Pallas kernels  15 us (21%)
    ppermute x27, starting transfers between devices, swap(): lax.ppermute(values, 'ex', [(index, index ^ bit) for index in range(size)])  29.4 us
    ppermute x27, waiting for transfers between devices, swap(): lax.ppermute(values, 'ex', [(index, index ^ bit) for index in range(size)])  26.7 us
    pallas_call x1, Pallas kernels, gradients_of(): pl.pallas_call(functools.partial(gradients_kernel, chunks=(2048, 8192)),...  8.32 us
    pallas_call x5, Pallas kernels, dots_of(): pl.pallas_call(functools.partial(dots_kernel, starts=tuple(targets), offs...  5.16 us
  transfers between devices with their start and end apart: 27, of which 16 were waited for; matrix products, arithmetic and copies ran while one was open for 0% of the time, Pallas kernels for 18%

profile of v6, /device:TPU:0, one launch (start us, length us, event | category | flops | bytes accessed | tf_op | source)
XLA Modules:
  0.0 72.4 jit_solution(18018149129510087018)
XLA Ops:
  0.0 4.0 %collective-permute-start = (bf16[2,2,18432]{2,1,0:T(2,128)(2,1)}, bf16[2,2,18432]{2,1,0:T(2,128)(2,1)S(1)}, u32[]{:S(2)}, u32[]{:S(2)}) collective-permute-start(bf16[2,2,18432]{2,1,0:T(2,128)(2,1)} %refs_2_.1), channel_id=1, source_target_pairs={{0,6},{1,7},{2,4},{3,5},{4,2},{5,3},{6,0},{7,1},{8,14},{9,15},{10,... | collective-permute-start | bytes 442376 | tf_op jit(solution)/shard_map/ppermute | solution.py:62
  4.0 2.6 %collective-permute-start.1 = (bf16[2,2,18432]{2,1,0:T(2,128)(2,1)}, bf16[2,2,18432]{2,1,0:T(2,128)(2,1)S(1)}, u32[]{:S(2)}, u32[]{:S(2)}) collective-permute-start(bf16[2,2,18432]{2,1,0:T(2,128)(2,1)} %refs_2_.1), channel_id=1, source_target_pairs={{0,8},{1,9},{2,10},{3,11},{4,12},{5,13},{6,14},{7,15},{8,0},{9,1},... | collective-permute-start | bytes 442376 | tf_op jit(solution)/shard_map/ppermute | solution.py:62
  7.5 8.3 %gradients.1 = (f32[4,8,18432]{2,1,0:T(8,128)S(1)}, f32[4,8,18432]{2,1,0:T(8,128)S(1)}, f32[4,128]{1,0:T(4,128)S(1)}) custom-call(s32[1]{0:T(128)} %bitcast.index_ref, s32[2]{0:T(128)} %lengths_ref.1, bf16[2,2,128,8192]{3,2,1,0:T(8,128)(2,1)} %x_hbm.1, bf16[2,2,128,1024]{3,2,1,0:T(8,128)(2,1)} %gk_hbm.1, bf16[2,2,128,1024]{3,2,1,0:T(8,128)(2,1)} %gv_hbm.1, ...), custom_call_target="tpu_custom_call" | custom-call | flops 4294967296 | bytes 16777216 | tf_op jit(solution)/shard_map/gradients/pallas_call | solution.py:212
  16.0 1.6 %collective-permute-start.8 = (f32[2,128]{1,0:T(2,128)S(1)}, f32[2,128]{1,0:T(2,128)S(1)}, u32[]{:S(2)}, u32[]{:S(2)}) collective-permute-start(f32[2,128]{1,0:T(2,128)S(1)} %pad_maximum_fusion), channel_id=1, source_target_pairs={{0,2},{1,3},{2,0},{3,1},{4,6},{5,7},{6,4},{7,5},{8,10},{9,11},{10,... | collective-permute-start | bytes 3080 | tf_op jit(solution)/shard_map/ppermute | solution.py:62
  17.6 1.6 %collective-permute-start.5 = (bf16[2,2,18432]{2,1,0:T(2,128)(2,1)S(1)}, bf16[2,2,18432]{2,1,0:T(2,128)(2,1)S(1)}, u32[]{:S(2)}, u32[]{:S(2)}) collective-permute-start(bf16[2,2,18432]{2,1,0:T(2,128)(2,1)S(1)} %collective-permute-done.1.refs_3_), channel_id=1, source_target_pairs={{0,4},{1,5},{2,6},{3,7},{4,0},{5,1},{6,2},{7,3},{8,12},{9,13},{10,... | collective-permute-start | bytes 442376 | tf_op jit(solution)/shard_map/ppermute | solution.py:62
  19.7 1.6 %collective-permute-start.9 = (f32[2,128]{1,0:T(2,128)S(1)}, f32[2,128]{1,0:T(2,128)S(1)}, u32[]{:S(2)}, u32[]{:S(2)}) collective-permute-start(f32[2,128]{1,0:T(2,128)S(1)} %fusion.3), channel_id=1, source_target_pairs={{0,4},{1,5},{2,6},{3,7},{4,0},{5,1},{6,2},{7,3},{8,12},{9,13},{10,... | collective-permute-start | bytes 3080 | tf_op jit(solution)/shard_map/ppermute | solution.py:62
  21.3 1.5 %collective-permute-start.7 = (bf16[2,2,18432]{2,1,0:T(2,128)(2,1)S(1)}, bf16[2,2,18432]{2,1,0:T(2,128)(2,1)S(1)}, u32[]{:S(2)}, u32[]{:S(2)}) collective-permute-start(bf16[2,2,18432]{2,1,0:T(2,128)(2,1)S(1)} %collective-permute-done.1.refs_3_), channel_id=1, source_target_pairs={{0,2},{1,3},{2,0},{3,1},{4,6},{5,7},{6,4},{7,5},{8,10},{9,11},{10,... | collective-permute-start | bytes 442376 | tf_op jit(solution)/shard_map/ppermute | solution.py:62
  24.1 1.2 %collective-permute-start.10 = (f32[2,128]{1,0:T(2,128)S(1)}, f32[2,128]{1,0:T(2,128)S(1)}, u32[]{:S(2)}, u32[]{:S(2)}) collective-permute-start(f32[2,128]{1,0:T(2,128)S(1)} %fusion.4.refs_5_), channel_id=1, source_target_pairs={{0,8},{1,9},{2,10},{3,11},{4,12},{5,13},{6,14},{7,15},{8,0},{9,1},... | collective-permute-start | bytes 3080 | tf_op jit(solution)/shard_map/ppermute | solution.py:62
  25.3 2.1 %collective-permute-done.7.refs_7_ = bf16[2,2,18432]{2,1,0:T(2,128)(2,1)S(1)} collective-permute-done((bf16[2,2,18432]{2,1,0:T(2,128)(2,1)S(1)}, bf16[2,2,18432]{2,1,0:T(2,128)(2,1)S(1)}, u32[]{:S(2)}, u32[]{:S(2)}) %collective-permute-start.7) | collective-permute-done | bytes 147488 | tf_op jit(solution)/shard_map/ppermute | solution.py:62
  27.4 2.1 %dots.5.refs_3_ = f32[16,128]{1,0:T(8,128)S(1)} custom-call(f32[4,8,18432]{2,1,0:T(8,128)S(1)} %get-tuple-element.22.refs_0_, f32[4,8,18432]{2,1,0:T(8,128)S(1)} %collective-permute-done.4.refs_1_, bf16[2,2,18432]{2,1,0:T(2,128)(2,1)S(1)} %copy-done, bf16[2,2,18432]{2,1,0:T(2,128)(2,1)S(1)} %collective-permute-done.1.refs_3_, ...), custom_call_target="tpu_custom_call" | custom-call | flops 4194304 | bytes 3145728 | tf_op jit(solution)/shard_map/dots/pallas_call | solution.py:309
  30.8 1.2 %collective-permute-done.11.pair_ref = f32[22,128]{1,0:T(8,128)S(1)} collective-permute-done((f32[22,128]{1,0:T(8,128)S(1)}, f32[22,128]{1,0:T(8,128)S(1)}, u32[]{:S(2)}, u32[]{:S(2)}) %collective-permute-start.11) | collective-permute-done | bytes 11296 | tf_op jit(solution)/shard_map/ppermute | solution.py:62
  33.3 1.4 %collective-permute-start.20 = (bf16[8,9216]{1,0:T(8,128)(2,1)S(1)}, bf16[8,9216]{1,0:T(8,128)(2,1)S(1)}, u32[]{:S(2)}, u32[]{:S(2)}) collective-permute-start(bf16[8,9216]{1,0:T(8,128)(2,1)S(1)} %get-tuple-element.35), channel_id=1, source_target_pairs={{0,2},{1,3},{2,0},{3,1},{4,6},{5,7},{6,4},{7,5},{8,10},{9,11},{10,... | collective-permute-start | bytes 442376 | tf_op jit(solution)/shard_map/ppermute | solution.py:62
  34.8 1.4 %collective-permute-start.21 = (bf16[8,9216]{1,0:T(8,128)(2,1)S(1)}, bf16[8,9216]{1,0:T(8,128)(2,1)S(1)}, u32[]{:S(2)}, u32[]{:S(2)}) collective-permute-start(bf16[8,9216]{1,0:T(8,128)(2,1)S(1)} %get-tuple-element.36), channel_id=1, source_target_pairs={{0,6},{1,7},{2,4},{3,5},{4,2},{5,3},{6,0},{7,1},{8,14},{9,15},{10,... | collective-permute-start | bytes 442376 | tf_op jit(solution)/shard_map/ppermute | solution.py:62
  37.6 1.4 %collective-permute-start.13 = (bf16[8,9216]{1,0:T(8,128)(2,1)S(1)}, bf16[8,9216]{1,0:T(8,128)(2,1)S(1)}, u32[]{:S(2)}, u32[]{:S(2)}) collective-permute-start(bf16[8,9216]{1,0:T(8,128)(2,1)S(1)} %get-tuple-element.29), channel_id=1, source_target_pairs={{0,2},{1,3},{2,0},{3,1},{4,6},{5,7},{6,4},{7,5},{8,10},{9,11},{10,... | collective-permute-start | bytes 442376 | tf_op jit(solution)/shard_map/ppermute | solution.py:62
  39.4 1.4 %collective-permute-start.14 = (bf16[8,9216]{1,0:T(8,128)(2,1)S(1)}, bf16[8,9216]{1,0:T(8,128)(2,1)S(1)}, u32[]{:S(2)}, u32[]{:S(2)}) collective-permute-start(bf16[8,9216]{1,0:T(8,128)(2,1)S(1)} %get-tuple-element.30), channel_id=1, source_target_pairs={{0,6},{1,7},{2,4},{3,5},{4,2},{5,3},{6,0},{7,1},{8,14},{9,15},{10,... | collective-permute-start | bytes 442376 | tf_op jit(solution)/shard_map/ppermute | solution.py:62
  40.9 2.8 %collective-permute-done.21.refs_2_ = bf16[8,9216]{1,0:T(8,128)(2,1)S(1)} collective-permute-done((bf16[8,9216]{1,0:T(8,128)(2,1)S(1)}, bf16[8,9216]{1,0:T(8,128)(2,1)S(1)}, u32[]{:S(2)}, u32[]{:S(2)}) %collective-permute-start.21) | collective-permute-done | bytes 147488 | tf_op jit(solution)/shard_map/ppermute | solution.py:62
  44.1 1.6 %collective-permute-done.12.refs_0_ = bf16[8,9216]{1,0:T(8,128)(2,1)S(1)} collective-permute-done((bf16[8,9216]{1,0:T(8,128)(2,1)S(1)}, bf16[8,9216]{1,0:T(8,128)(2,1)S(1)}, u32[]{:S(2)}, u32[]{:S(2)}) %collective-permute-start.12) | collective-permute-done | bytes 147488 | tf_op jit(solution)/shard_map/ppermute | solution.py:62
  45.7 6.1 %collective-permute-done.14.refs_2_ = bf16[8,9216]{1,0:T(8,128)(2,1)S(1)} collective-permute-done((bf16[8,9216]{1,0:T(8,128)(2,1)S(1)}, bf16[8,9216]{1,0:T(8,128)(2,1)S(1)}, u32[]{:S(2)}, u32[]{:S(2)}) %collective-permute-start.14) | collective-permute-done | bytes 147488 | tf_op jit(solution)/shard_map/ppermute | solution.py:62
  53.2 2.2 %collective-permute-start.15 = (bf16[8,9216]{1,0:T(8,128)(2,1)S(1)}, bf16[8,9216]{1,0:T(8,128)(2,1)S(1)}, u32[]{:S(2)}, u32[]{:S(2)}) collective-permute-start(bf16[8,9216]{1,0:T(8,128)(2,1)S(1)} %get-tuple-element.32), channel_id=1, source_target_pairs={{0,8},{1,9},{2,10},{3,11},{4,12},{5,13},{6,14},{7,15},{8,0},{9,1},... | collective-permute-start | bytes 442376 | tf_op jit(solution)/shard_map/ppermute | solution.py:62
  55.4 4.3 %collective-permute-done.23.refs_3_ = bf16[8,9216]{1,0:T(8,128)(2,1)S(1)} collective-permute-done((bf16[8,9216]{1,0:T(8,128)(2,1)S(1)}, bf16[8,9216]{1,0:T(8,128)(2,1)S(1)}, u32[]{:S(2)}, u32[]{:S(2)}) %collective-permute-start.23) | collective-permute-done | bytes 147488 | tf_op jit(solution)/shard_map/ppermute | solution.py:62
  60.1 1.7 %collective-permute-done.15 = bf16[8,9216]{1,0:T(8,128)(2,1)S(1)} collective-permute-done((bf16[8,9216]{1,0:T(8,128)(2,1)S(1)}, bf16[8,9216]{1,0:T(8,128)(2,1)S(1)}, u32[]{:S(2)}, u32[]{:S(2)}) %collective-permute-start.15) | collective-permute-done | bytes 147488 | tf_op jit(solution)/shard_map/ppermute | solution.py:62
  62.8 2.6 %collective-permute-start.17 = (bf16[8,9216]{1,0:T(8,128)(2,1)S(1)}, bf16[8,9216]{1,0:T(8,128)(2,1)S(1)}, u32[]{:S(2)}, u32[]{:S(2)}) collective-permute-start(bf16[8,9216]{1,0:T(8,128)(2,1)S(1)} %add_convert_fusion.1.refs_2_), channel_id=1, source_target_pairs={{0,6},{1,7},{2,4},{3,5},{4,2},{5,3},{6,0},{7,1},{8,14},{9,15},{10,... | collective-permute-start | bytes 442376 | tf_op jit(solution)/shard_map/ppermute | solution.py:62
  68.0 1.7 %collective-permute-done.16.refs_2_ = bf16[8,9216]{1,0:T(8,128)(2,1)S(1)} collective-permute-done((bf16[8,9216]{1,0:T(8,128)(2,1)S(1)}, bf16[8,9216]{1,0:T(8,128)(2,1)S(1)}, u32[]{:S(2)}, u32[]{:S(2)}) %collective-permute-start.16) | collective-permute-done | bytes 147488 | tf_op jit(solution)/shard_map/ppermute | solution.py:62
  70.5 1.1 %collective-permute-done.26 = f32[2,4,128]{2,1,0:T(4,128)S(1)} collective-permute-done((f32[2,4,128]{2,1,0:T(4,128)S(1)}, f32[2,4,128]{2,1,0:T(4,128)S(1)}, u32[]{:S(2)}, u32[]{:S(2)}) %collective-permute-start.26) | collective-permute-done | bytes 4128 | tf_op jit(solution)/shard_map/ppermute | solution.py:62
  (57 shorter events, 14.7 us)
Async XLA Ops:
  0.0 15.9 %collective-permute-start = (bf16[2,2,18432]{2,1,0:T(2,128)(2,1)}, bf16[2,2,18432]{2,1,0:T(2,128)(2,1)S(1)}, u32[]{:S(2)}, u32[]{:S(2)}) collective-permute-start(bf16[2,2,18432]{2,1,0:T(2,128)(2,1)} %refs_2_.1), channel_id=1, source_target_pairs={{0,6},{1,7},{2,4},{3,5},{4,2},{5,3},{6,0},{7,1},{8,14},{9,15},{10,... | collective-permute-start | bytes 442376 | tf_op jit(solution)/shard_map/ppermute | solution.py:62
  4.0 11.9 %collective-permute-start.1 = (bf16[2,2,18432]{2,1,0:T(2,128)(2,1)}, bf16[2,2,18432]{2,1,0:T(2,128)(2,1)S(1)}, u32[]{:S(2)}, u32[]{:S(2)}) collective-permute-start(bf16[2,2,18432]{2,1,0:T(2,128)(2,1)} %refs_2_.1), channel_id=1, source_target_pairs={{0,8},{1,9},{2,10},{3,11},{4,12},{5,13},{6,14},{7,15},{8,0},{9,1},... | collective-permute-start | bytes 442376 | tf_op jit(solution)/shard_map/ppermute | solution.py:62
  6.6 9.3 %collective-permute-start.2 = (bf16[2,2,18432]{2,1,0:T(2,128)(2,1)}, bf16[2,2,18432]{2,1,0:T(2,128)(2,1)S(1)}, u32[]{:S(2)}, u32[]{:S(2)}) collective-permute-start(bf16[2,2,18432]{2,1,0:T(2,128)(2,1)} %refs_2_.1), channel_id=1, source_target_pairs={{0,2},{1,3},{2,0},{3,1},{4,6},{5,7},{6,4},{7,5},{8,10},{9,11},{10,... | collective-permute-start | bytes 442376 | tf_op jit(solution)/shard_map/ppermute | solution.py:62
  7.1 8.8 %collective-permute-start.3 = (bf16[2,2,18432]{2,1,0:T(2,128)(2,1)}, bf16[2,2,18432]{2,1,0:T(2,128)(2,1)S(1)}, u32[]{:S(2)}, u32[]{:S(2)}) collective-permute-start(bf16[2,2,18432]{2,1,0:T(2,128)(2,1)} %refs_2_.1), channel_id=1, source_target_pairs={{0,4},{1,5},{2,6},{3,7},{4,0},{5,1},{6,2},{7,3},{8,12},{9,13},{10,... | collective-permute-start | bytes 442376 | tf_op jit(solution)/shard_map/ppermute | solution.py:62
  15.9 11.5 %collective-permute-start.4 = (f32[4,8,18432]{2,1,0:T(8,128)S(1)}, f32[4,8,18432]{2,1,0:T(8,128)S(1)}, u32[]{:S(2)}, u32[]{:S(2)}) collective-permute-start(f32[4,8,18432]{2,1,0:T(8,128)S(1)} %get-tuple-element.25), channel_id=1, source_target_pairs={{0,1},{1,0},{2,3},{3,2},{4,5},{5,4},{6,7},{7,6},{8,9},{9,8},{10,11... | collective-permute-start | bytes 7077896 | tf_op jit(solution)/shard_map/ppermute | solution.py:62
  17.6 6.0 %collective-permute-start.5 = (bf16[2,2,18432]{2,1,0:T(2,128)(2,1)S(1)}, bf16[2,2,18432]{2,1,0:T(2,128)(2,1)S(1)}, u32[]{:S(2)}, u32[]{:S(2)}) collective-permute-start(bf16[2,2,18432]{2,1,0:T(2,128)(2,1)S(1)} %collective-permute-done.1.refs_3_), channel_id=1, source_target_pairs={{0,4},{1,5},{2,6},{3,7},{4,0},{5,1},{6,2},{7,3},{8,12},{9,13},{10,... | collective-permute-start | bytes 442376 | tf_op jit(solution)/shard_map/ppermute | solution.py:62
  19.7 4.4 %collective-permute-start.9 = (f32[2,128]{1,0:T(2,128)S(1)}, f32[2,128]{1,0:T(2,128)S(1)}, u32[]{:S(2)}, u32[]{:S(2)}) collective-permute-start(f32[2,128]{1,0:T(2,128)S(1)} %fusion.3), channel_id=1, source_target_pairs={{0,4},{1,5},{2,6},{3,7},{4,0},{5,1},{6,2},{7,3},{8,12},{9,13},{10,... | collective-permute-start | bytes 3080 | tf_op jit(solution)/shard_map/ppermute | solution.py:62
  21.3 6.1 %collective-permute-start.7 = (bf16[2,2,18432]{2,1,0:T(2,128)(2,1)S(1)}, bf16[2,2,18432]{2,1,0:T(2,128)(2,1)S(1)}, u32[]{:S(2)}, u32[]{:S(2)}) collective-permute-start(bf16[2,2,18432]{2,1,0:T(2,128)(2,1)S(1)} %collective-permute-done.1.refs_3_), channel_id=1, source_target_pairs={{0,2},{1,3},{2,0},{3,1},{4,6},{5,7},{6,4},{7,5},{8,10},{9,11},{10,... | collective-permute-start | bytes 442376 | tf_op jit(solution)/shard_map/ppermute | solution.py:62
  23.6 6.0 %collective-permute-start.6 = (bf16[2,2,18432]{2,1,0:T(2,128)(2,1)S(1)}, bf16[2,2,18432]{2,1,0:T(2,128)(2,1)S(1)}, u32[]{:S(2)}, u32[]{:S(2)}) collective-permute-start(bf16[2,2,18432]{2,1,0:T(2,128)(2,1)S(1)} %collective-permute-done.5.refs_5_), channel_id=1, source_target_pairs={{0,2},{1,3},{2,0},{3,1},{4,6},{5,7},{6,4},{7,5},{8,10},{9,11},{10,... | collective-permute-start | bytes 442376 | tf_op jit(solution)/shard_map/ppermute | solution.py:62
  24.1 5.4 %collective-permute-start.10 = (f32[2,128]{1,0:T(2,128)S(1)}, f32[2,128]{1,0:T(2,128)S(1)}, u32[]{:S(2)}, u32[]{:S(2)}) collective-permute-start(f32[2,128]{1,0:T(2,128)S(1)} %fusion.4.refs_5_), channel_id=1, source_target_pairs={{0,8},{1,9},{2,10},{3,11},{4,12},{5,13},{6,14},{7,15},{8,0},{9,1},... | collective-permute-start | bytes 3080 | tf_op jit(solution)/shard_map/ppermute | solution.py:62
  32.6 6.8 %collective-permute-start.19 = (bf16[8,9216]{1,0:T(8,128)(2,1)S(1)}, bf16[8,9216]{1,0:T(8,128)(2,1)S(1)}, u32[]{:S(2)}, u32[]{:S(2)}) collective-permute-start(bf16[8,9216]{1,0:T(8,128)(2,1)S(1)} %get-tuple-element.34), channel_id=1, source_target_pairs={{0,4},{1,5},{2,6},{3,7},{4,0},{5,1},{6,2},{7,3},{8,12},{9,13},{10,... | collective-permute-start | bytes 442376 | tf_op jit(solution)/shard_map/ppermute | solution.py:62
  33.3 7.6 %collective-permute-start.20 = (bf16[8,9216]{1,0:T(8,128)(2,1)S(1)}, bf16[8,9216]{1,0:T(8,128)(2,1)S(1)}, u32[]{:S(2)}, u32[]{:S(2)}) collective-permute-start(bf16[8,9216]{1,0:T(8,128)(2,1)S(1)} %get-tuple-element.35), channel_id=1, source_target_pairs={{0,2},{1,3},{2,0},{3,1},{4,6},{5,7},{6,4},{7,5},{8,10},{9,11},{10,... | collective-permute-start | bytes 442376 | tf_op jit(solution)/shard_map/ppermute | solution.py:62
  34.8 8.9 %collective-permute-start.21 = (bf16[8,9216]{1,0:T(8,128)(2,1)S(1)}, bf16[8,9216]{1,0:T(8,128)(2,1)S(1)}, u32[]{:S(2)}, u32[]{:S(2)}) collective-permute-start(bf16[8,9216]{1,0:T(8,128)(2,1)S(1)} %get-tuple-element.36), channel_id=1, source_target_pairs={{0,6},{1,7},{2,4},{3,5},{4,2},{5,3},{6,0},{7,1},{8,14},{9,15},{10,... | collective-permute-start | bytes 442376 | tf_op jit(solution)/shard_map/ppermute | solution.py:62
  36.8 8.9 %collective-permute-start.12 = (bf16[8,9216]{1,0:T(8,128)(2,1)S(1)}, bf16[8,9216]{1,0:T(8,128)(2,1)S(1)}, u32[]{:S(2)}, u32[]{:S(2)}) collective-permute-start(bf16[8,9216]{1,0:T(8,128)(2,1)S(1)} %get-tuple-element.28), channel_id=1, source_target_pairs={{0,4},{1,5},{2,6},{3,7},{4,0},{5,1},{6,2},{7,3},{8,12},{9,13},{10,... | collective-permute-start | bytes 442376 | tf_op jit(solution)/shard_map/ppermute | solution.py:62
  37.6 8.2 %collective-permute-start.13 = (bf16[8,9216]{1,0:T(8,128)(2,1)S(1)}, bf16[8,9216]{1,0:T(8,128)(2,1)S(1)}, u32[]{:S(2)}, u32[]{:S(2)}) collective-permute-start(bf16[8,9216]{1,0:T(8,128)(2,1)S(1)} %get-tuple-element.29), channel_id=1, source_target_pairs={{0,2},{1,3},{2,0},{3,1},{4,6},{5,7},{6,4},{7,5},{8,10},{9,11},{10,... | collective-permute-start | bytes 442376 | tf_op jit(solution)/shard_map/ppermute | solution.py:62
  39.4 12.5 %collective-permute-start.14 = (bf16[8,9216]{1,0:T(8,128)(2,1)S(1)}, bf16[8,9216]{1,0:T(8,128)(2,1)S(1)}, u32[]{:S(2)}, u32[]{:S(2)}) collective-permute-start(bf16[8,9216]{1,0:T(8,128)(2,1)S(1)} %get-tuple-element.30), channel_id=1, source_target_pairs={{0,6},{1,7},{2,4},{3,5},{4,2},{5,3},{6,0},{7,1},{8,14},{9,15},{10,... | collective-permute-start | bytes 442376 | tf_op jit(solution)/shard_map/ppermute | solution.py:62
  43.8 9.2 %collective-permute-start.22 = (bf16[8,9216]{1,0:T(8,128)(2,1)S(1)}, bf16[8,9216]{1,0:T(8,128)(2,1)S(1)}, u32[]{:S(2)}, u32[]{:S(2)}) collective-permute-start(bf16[8,9216]{1,0:T(8,128)(2,1)S(1)} %get-tuple-element.38), channel_id=1, source_target_pairs={{0,8},{1,9},{2,10},{3,11},{4,12},{5,13},{6,14},{7,15},{8,0},{9,1},... | collective-permute-start | bytes 442376 | tf_op jit(solution)/shard_map/ppermute | solution.py:62
  53.1 6.6 %collective-permute-start.23 = (bf16[8,9216]{1,0:T(8,128)(2,1)S(1)}, bf16[8,9216]{1,0:T(8,128)(2,1)S(1)}, u32[]{:S(2)}, u32[]{:S(2)}) collective-permute-start(bf16[8,9216]{1,0:T(8,128)(2,1)S(1)} %add_convert_fusion.refs_2_), channel_id=1, source_target_pairs={{0,4},{1,5},{2,6},{3,7},{4,0},{5,1},{6,2},{7,3},{8,12},{9,13},{10,... | collective-permute-start | bytes 442376 | tf_op jit(solution)/shard_map/ppermute | solution.py:62
  53.2 8.6 %collective-permute-start.15 = (bf16[8,9216]{1,0:T(8,128)(2,1)S(1)}, bf16[8,9216]{1,0:T(8,128)(2,1)S(1)}, u32[]{:S(2)}, u32[]{:S(2)}) collective-permute-start(bf16[8,9216]{1,0:T(8,128)(2,1)S(1)} %get-tuple-element.32), channel_id=1, source_target_pairs={{0,8},{1,9},{2,10},{3,11},{4,12},{5,13},{6,14},{7,15},{8,0},{9,1},... | collective-permute-start | bytes 442376 | tf_op jit(solution)/shard_map/ppermute | solution.py:62
  55.4 10.1 %collective-permute-start.24 = (bf16[8,9216]{1,0:T(8,128)(2,1)S(1)}, bf16[8,9216]{1,0:T(8,128)(2,1)S(1)}, u32[]{:S(2)}, u32[]{:S(2)}) collective-permute-start(bf16[8,9216]{1,0:T(8,128)(2,1)S(1)} %add_convert_fusion.refs_2_), channel_id=1, source_target_pairs={{0,2},{1,3},{2,0},{3,1},{4,6},{5,7},{6,4},{7,5},{8,10},{9,11},{10,... | collective-permute-start | bytes 442376 | tf_op jit(solution)/shard_map/ppermute | solution.py:62
  59.7 6.9 %collective-permute-start.25 = (bf16[8,9216]{1,0:T(8,128)(2,1)S(1)}, bf16[8,9216]{1,0:T(8,128)(2,1)S(1)}, u32[]{:S(2)}, u32[]{:S(2)}) collective-permute-start(bf16[8,9216]{1,0:T(8,128)(2,1)S(1)} %collective-permute-done.23.refs_3_), channel_id=1, source_target_pairs={{0,2},{1,3},{2,0},{3,1},{4,6},{5,7},{6,4},{7,5},{8,10},{9,11},{10,... | collective-permute-start | bytes 442376 | tf_op jit(solution)/shard_map/ppermute | solution.py:62
  61.8 5.5 %collective-permute-start.18 = (bf16[8,9216]{1,0:T(8,128)(2,1)S(1)}, bf16[8,9216]{1,0:T(8,128)(2,1)S(1)}, u32[]{:S(2)}, u32[]{:S(2)}) collective-permute-start(bf16[8,9216]{1,0:T(8,128)(2,1)S(1)} %add_convert_fusion.1.refs_2_), channel_id=1, source_target_pairs={{0,4},{1,5},{2,6},{3,7},{4,0},{5,1},{6,2},{7,3},{8,12},{9,13},{10,... | collective-permute-start | bytes 442376 | tf_op jit(solution)/shard_map/ppermute | solution.py:62
  61.9 7.8 %collective-permute-start.16 = (bf16[8,9216]{1,0:T(8,128)(2,1)S(1)}, bf16[8,9216]{1,0:T(8,128)(2,1)S(1)}, u32[]{:S(2)}, u32[]{:S(2)}) collective-permute-start(bf16[8,9216]{1,0:T(8,128)(2,1)S(1)} %add_convert_fusion.1.refs_2_), channel_id=1, source_target_pairs={{0,2},{1,3},{2,0},{3,1},{4,6},{5,7},{6,4},{7,5},{8,10},{9,11},{10,... | collective-permute-start | bytes 442376 | tf_op jit(solution)/shard_map/ppermute | solution.py:62
  62.8 6.9 %collective-permute-start.17 = (bf16[8,9216]{1,0:T(8,128)(2,1)S(1)}, bf16[8,9216]{1,0:T(8,128)(2,1)S(1)}, u32[]{:S(2)}, u32[]{:S(2)}) collective-permute-start(bf16[8,9216]{1,0:T(8,128)(2,1)S(1)} %add_convert_fusion.1.refs_2_), channel_id=1, source_target_pairs={{0,6},{1,7},{2,4},{3,5},{4,2},{5,3},{6,0},{7,1},{8,14},{9,15},{10,... | collective-permute-start | bytes 442376 | tf_op jit(solution)/shard_map/ppermute | solution.py:62
  (4 other events, 17.7 us)

commit v7 on v6

--- a/solution.py
+++ b/solution.py
@@ -174,8 +174,8 @@
             for at in range(examples)
         ]
         wait(("ak", layer), ("av", layer))
-        for at in range(0, width, COLUMNS * 2):
-            columns = slice(at, at + COLUMNS * 2)
+        for at in range(0, width, INPUT_COLUMNS):
+            columns = slice(at, at + INPUT_COLUMNS)
             factor = ordered(order, a_ref[layer, 0, :, columns], a_ref[layer, 1, :, columns])
             if at % chunks[layer] == 0:
                 wait(("x", layer, at))
@@ -192,7 +192,8 @@
 IN_VMEM = pl.BlockSpec(memory_space=pltpu.VMEM)
 IN_SMEM = pl.BlockSpec(memory_space=pltpu.SMEM)
 ANYWHERE = pl.BlockSpec(memory_space=pl.ANY)
-COLUMNS = 1024
+COLUMNS = 1536
+INPUT_COLUMNS = 2048
 STREAMS = (9216, 9216)
 SQUARES, NORMS = 16, 20
 
@@ -210,7 +211,7 @@
     lengths = in_hbm(lengths)
     parameters = pltpu.CompilerParams(vmem_limit_bytes=GRADIENT_VMEM)
     own, other, squares = pl.pallas_call(
-        functools.partial(gradients_kernel, chunks=(2048, 8192)),
+        functools.partial(gradients_kernel, chunks=(INPUT_COLUMNS, width)),
         in_specs=[IN_SMEM] * 2 + [ANYWHERE] * 7,
         out_specs=[IN_VMEM] * 3,
         out_shape=outputs,

time: 72.6 us -> 72.5 us (level)
  transfers between devices with their start and end apart: 27 -> 27, of which waited for: 16 -> 16; matrix products, arithmetic and copies ran while one was open for 0% -> 0% of each run, Pallas kernels for 18% -> 17%
where the time goes in v7:
time: 72.5 us; the launch traced here: 72.3 us
  starting transfers between devices  29.4 us (41%)
  waiting for transfers between devices  26.8 us (37%)
  Pallas kernels  14.8 us (20%)
    ppermute x27, starting transfers between devices, swap(): lax.ppermute(values, 'ex', [(index, index ^ bit) for index in range(size)])  29.4 us
    ppermute x27, waiting for transfers between devices, swap(): lax.ppermute(values, 'ex', [(index, index ^ bit) for index in range(size)])  26.8 us
    pallas_call x1, Pallas kernels, gradients_of(): pl.pallas_call(functools.partial(gradients_kernel, chunks=(INPUT_COLUMNS,...  8.32 us
    pallas_call x5, Pallas kernels, dots_of(): pl.pallas_call(functools.partial(dots_kernel, starts=tuple(targets), offs...  5.01 us
  transfers between devices with their start and end apart: 27, of which 16 were waited for; matrix products, arithmetic and copies ran while one was open for 0% of the time, Pallas kernels for 17%

profile of v7, /device:TPU:0, one launch (start us, length us, event | category | flops | bytes accessed | tf_op | source)
XLA Modules:
  0.0 72.3 jit_solution(10647205526719622107)
XLA Ops:
  0.0 4.0 %collective-permute-start = (bf16[2,2,18432]{2,1,0:T(2,128)(2,1)}, bf16[2,2,18432]{2,1,0:T(2,128)(2,1)S(1)}, u32[]{:S(2)}, u32[]{:S(2)}) collective-permute-start(bf16[2,2,18432]{2,1,0:T(2,128)(2,1)} %refs_2_.1), channel_id=1, source_target_pairs={{0,6},{1,7},{2,4},{3,5},{4,2},{5,3},{6,0},{7,1},{8,14},{9,15},{10,... | collective-permute-start | bytes 442376 | tf_op jit(solution)/shard_map/ppermute | solution.py:62
  4.0 2.6 %collective-permute-start.1 = (bf16[2,2,18432]{2,1,0:T(2,128)(2,1)}, bf16[2,2,18432]{2,1,0:T(2,128)(2,1)S(1)}, u32[]{:S(2)}, u32[]{:S(2)}) collective-permute-start(bf16[2,2,18432]{2,1,0:T(2,128)(2,1)} %refs_2_.1), channel_id=1, source_target_pairs={{0,8},{1,9},{2,10},{3,11},{4,12},{5,13},{6,14},{7,15},{8,0},{9,1},... | collective-permute-start | bytes 442376 | tf_op jit(solution)/shard_map/ppermute | solution.py:62
  7.5 8.3 %gradients.1 = (f32[4,8,18432]{2,1,0:T(8,128)S(1)}, f32[4,8,18432]{2,1,0:T(8,128)S(1)}, f32[4,128]{1,0:T(4,128)S(1)}) custom-call(s32[1]{0:T(128)} %bitcast.index_ref, s32[2]{0:T(128)} %lengths_ref.1, bf16[2,2,128,8192]{3,2,1,0:T(8,128)(2,1)} %x_hbm.1, bf16[2,2,128,1024]{3,2,1,0:T(8,128)(2,1)} %gk_hbm.1, bf16[2,2,128,1024]{3,2,1,0:T(8,128)(2,1)} %gv_hbm.1, ...), custom_call_target="tpu_custom_call" | custom-call | flops 4294967296 | bytes 16777216 | tf_op jit(solution)/shard_map/gradients/pallas_call | solution.py:213
  16.0 1.6 %collective-permute-start.8 = (f32[2,128]{1,0:T(2,128)S(1)}, f32[2,128]{1,0:T(2,128)S(1)}, u32[]{:S(2)}, u32[]{:S(2)}) collective-permute-start(f32[2,128]{1,0:T(2,128)S(1)} %pad_maximum_fusion), channel_id=1, source_target_pairs={{0,2},{1,3},{2,0},{3,1},{4,6},{5,7},{6,4},{7,5},{8,10},{9,11},{10,... | collective-permute-start | bytes 3080 | tf_op jit(solution)/shard_map/ppermute | solution.py:62
  17.6 1.6 %collective-permute-start.5 = (bf16[2,2,18432]{2,1,0:T(2,128)(2,1)S(1)}, bf16[2,2,18432]{2,1,0:T(2,128)(2,1)S(1)}, u32[]{:S(2)}, u32[]{:S(2)}) collective-permute-start(bf16[2,2,18432]{2,1,0:T(2,128)(2,1)S(1)} %collective-permute-done.1.refs_3_), channel_id=1, source_target_pairs={{0,4},{1,5},{2,6},{3,7},{4,0},{5,1},{6,2},{7,3},{8,12},{9,13},{10,... | collective-permute-start | bytes 442376 | tf_op jit(solution)/shard_map/ppermute | solution.py:62
  19.7 1.6 %collective-permute-start.9 = (f32[2,128]{1,0:T(2,128)S(1)}, f32[2,128]{1,0:T(2,128)S(1)}, u32[]{:S(2)}, u32[]{:S(2)}) collective-permute-start(f32[2,128]{1,0:T(2,128)S(1)} %fusion.3), channel_id=1, source_target_pairs={{0,4},{1,5},{2,6},{3,7},{4,0},{5,1},{6,2},{7,3},{8,12},{9,13},{10,... | collective-permute-start | bytes 3080 | tf_op jit(solution)/shard_map/ppermute | solution.py:62
  21.3 1.5 %collective-permute-start.7 = (bf16[2,2,18432]{2,1,0:T(2,128)(2,1)S(1)}, bf16[2,2,18432]{2,1,0:T(2,128)(2,1)S(1)}, u32[]{:S(2)}, u32[]{:S(2)}) collective-permute-start(bf16[2,2,18432]{2,1,0:T(2,128)(2,1)S(1)} %collective-permute-done.1.refs_3_), channel_id=1, source_target_pairs={{0,2},{1,3},{2,0},{3,1},{4,6},{5,7},{6,4},{7,5},{8,10},{9,11},{10,... | collective-permute-start | bytes 442376 | tf_op jit(solution)/shard_map/ppermute | solution.py:62
  24.1 1.2 %collective-permute-start.10 = (f32[2,128]{1,0:T(2,128)S(1)}, f32[2,128]{1,0:T(2,128)S(1)}, u32[]{:S(2)}, u32[]{:S(2)}) collective-permute-start(f32[2,128]{1,0:T(2,128)S(1)} %fusion.4.refs_5_), channel_id=1, source_target_pairs={{0,8},{1,9},{2,10},{3,11},{4,12},{5,13},{6,14},{7,15},{8,0},{9,1},... | collective-permute-start | bytes 3080 | tf_op jit(solution)/shard_map/ppermute | solution.py:62
  25.3 2.1 %collective-permute-done.7.refs_7_ = bf16[2,2,18432]{2,1,0:T(2,128)(2,1)S(1)} collective-permute-done((bf16[2,2,18432]{2,1,0:T(2,128)(2,1)S(1)}, bf16[2,2,18432]{2,1,0:T(2,128)(2,1)S(1)}, u32[]{:S(2)}, u32[]{:S(2)}) %collective-permute-start.7) | collective-permute-done | bytes 147488 | tf_op jit(solution)/shard_map/ppermute | solution.py:62
  27.4 2.0 %dots.5.refs_3_ = f32[16,128]{1,0:T(8,128)S(1)} custom-call(f32[4,8,18432]{2,1,0:T(8,128)S(1)} %get-tuple-element.22.refs_0_, f32[4,8,18432]{2,1,0:T(8,128)S(1)} %collective-permute-done.4.refs_1_, bf16[2,2,18432]{2,1,0:T(2,128)(2,1)S(1)} %copy-done, bf16[2,2,18432]{2,1,0:T(2,128)(2,1)S(1)} %collective-permute-done.1.refs_3_, ...), custom_call_target="tpu_custom_call" | custom-call | flops 4194304 | bytes 3145728 | tf_op jit(solution)/shard_map/dots/pallas_call | solution.py:310
  30.7 1.2 %collective-permute-done.11.pair_ref = f32[22,128]{1,0:T(8,128)S(1)} collective-permute-done((f32[22,128]{1,0:T(8,128)S(1)}, f32[22,128]{1,0:T(8,128)S(1)}, u32[]{:S(2)}, u32[]{:S(2)}) %collective-permute-start.11) | collective-permute-done | bytes 11296 | tf_op jit(solution)/shard_map/ppermute | solution.py:62
  33.2 1.4 %collective-permute-start.20 = (bf16[8,9216]{1,0:T(8,128)(2,1)S(1)}, bf16[8,9216]{1,0:T(8,128)(2,1)S(1)}, u32[]{:S(2)}, u32[]{:S(2)}) collective-permute-start(bf16[8,9216]{1,0:T(8,128)(2,1)S(1)} %get-tuple-element.35), channel_id=1, source_target_pairs={{0,2},{1,3},{2,0},{3,1},{4,6},{5,7},{6,4},{7,5},{8,10},{9,11},{10,... | collective-permute-start | bytes 442376 | tf_op jit(solution)/shard_map/ppermute | solution.py:62
  34.7 1.4 %collective-permute-start.21 = (bf16[8,9216]{1,0:T(8,128)(2,1)S(1)}, bf16[8,9216]{1,0:T(8,128)(2,1)S(1)}, u32[]{:S(2)}, u32[]{:S(2)}) collective-permute-start(bf16[8,9216]{1,0:T(8,128)(2,1)S(1)} %get-tuple-element.36), channel_id=1, source_target_pairs={{0,6},{1,7},{2,4},{3,5},{4,2},{5,3},{6,0},{7,1},{8,14},{9,15},{10,... | collective-permute-start | bytes 442376 | tf_op jit(solution)/shard_map/ppermute | solution.py:62
  37.4 1.4 %collective-permute-start.13 = (bf16[8,9216]{1,0:T(8,128)(2,1)S(1)}, bf16[8,9216]{1,0:T(8,128)(2,1)S(1)}, u32[]{:S(2)}, u32[]{:S(2)}) collective-permute-start(bf16[8,9216]{1,0:T(8,128)(2,1)S(1)} %get-tuple-element.29), channel_id=1, source_target_pairs={{0,2},{1,3},{2,0},{3,1},{4,6},{5,7},{6,4},{7,5},{8,10},{9,11},{10,... | collective-permute-start | bytes 442376 | tf_op jit(solution)/shard_map/ppermute | solution.py:62
  39.3 1.4 %collective-permute-start.14 = (bf16[8,9216]{1,0:T(8,128)(2,1)S(1)}, bf16[8,9216]{1,0:T(8,128)(2,1)S(1)}, u32[]{:S(2)}, u32[]{:S(2)}) collective-permute-start(bf16[8,9216]{1,0:T(8,128)(2,1)S(1)} %get-tuple-element.30), channel_id=1, source_target_pairs={{0,6},{1,7},{2,4},{3,5},{4,2},{5,3},{6,0},{7,1},{8,14},{9,15},{10,... | collective-permute-start | bytes 442376 | tf_op jit(solution)/shard_map/ppermute | solution.py:62
  40.9 2.7 %collective-permute-done.21.refs_2_ = bf16[8,9216]{1,0:T(8,128)(2,1)S(1)} collective-permute-done((bf16[8,9216]{1,0:T(8,128)(2,1)S(1)}, bf16[8,9216]{1,0:T(8,128)(2,1)S(1)}, u32[]{:S(2)}, u32[]{:S(2)}) %collective-permute-start.21) | collective-permute-done | bytes 147488 | tf_op jit(solution)/shard_map/ppermute | solution.py:62
  44.0 1.6 %collective-permute-done.12.refs_0_ = bf16[8,9216]{1,0:T(8,128)(2,1)S(1)} collective-permute-done((bf16[8,9216]{1,0:T(8,128)(2,1)S(1)}, bf16[8,9216]{1,0:T(8,128)(2,1)S(1)}, u32[]{:S(2)}, u32[]{:S(2)}) %collective-permute-start.12) | collective-permute-done | bytes 147488 | tf_op jit(solution)/shard_map/ppermute | solution.py:62
  45.6 6.1 %collective-permute-done.14.refs_2_ = bf16[8,9216]{1,0:T(8,128)(2,1)S(1)} collective-permute-done((bf16[8,9216]{1,0:T(8,128)(2,1)S(1)}, bf16[8,9216]{1,0:T(8,128)(2,1)S(1)}, u32[]{:S(2)}, u32[]{:S(2)}) %collective-permute-start.14) | collective-permute-done | bytes 147488 | tf_op jit(solution)/shard_map/ppermute | solution.py:62
  51.8 1.1 %collective-permute-done.22 = bf16[8,9216]{1,0:T(8,128)(2,1)S(1)} collective-permute-done((bf16[8,9216]{1,0:T(8,128)(2,1)S(1)}, bf16[8,9216]{1,0:T(8,128)(2,1)S(1)}, u32[]{:S(2)}, u32[]{:S(2)}) %collective-permute-start.22) | collective-permute-done | bytes 147488 | tf_op jit(solution)/shard_map/ppermute | solution.py:62
  53.0 2.2 %collective-permute-start.15 = (bf16[8,9216]{1,0:T(8,128)(2,1)S(1)}, bf16[8,9216]{1,0:T(8,128)(2,1)S(1)}, u32[]{:S(2)}, u32[]{:S(2)}) collective-permute-start(bf16[8,9216]{1,0:T(8,128)(2,1)S(1)} %get-tuple-element.32), channel_id=1, source_target_pairs={{0,8},{1,9},{2,10},{3,11},{4,12},{5,13},{6,14},{7,15},{8,0},{9,1},... | collective-permute-start | bytes 442376 | tf_op jit(solution)/shard_map/ppermute | solution.py:62
  55.3 4.3 %collective-permute-done.23.refs_3_ = bf16[8,9216]{1,0:T(8,128)(2,1)S(1)} collective-permute-done((bf16[8,9216]{1,0:T(8,128)(2,1)S(1)}, bf16[8,9216]{1,0:T(8,128)(2,1)S(1)}, u32[]{:S(2)}, u32[]{:S(2)}) %collective-permute-start.23) | collective-permute-done | bytes 147488 | tf_op jit(solution)/shard_map/ppermute | solution.py:62
  59.9 1.7 %collective-permute-done.15 = bf16[8,9216]{1,0:T(8,128)(2,1)S(1)} collective-permute-done((bf16[8,9216]{1,0:T(8,128)(2,1)S(1)}, bf16[8,9216]{1,0:T(8,128)(2,1)S(1)}, u32[]{:S(2)}, u32[]{:S(2)}) %collective-permute-start.15) | collective-permute-done | bytes 147488 | tf_op jit(solution)/shard_map/ppermute | solution.py:62
  62.7 2.6 %collective-permute-start.17 = (bf16[8,9216]{1,0:T(8,128)(2,1)S(1)}, bf16[8,9216]{1,0:T(8,128)(2,1)S(1)}, u32[]{:S(2)}, u32[]{:S(2)}) collective-permute-start(bf16[8,9216]{1,0:T(8,128)(2,1)S(1)} %add_convert_fusion.1.refs_2_), channel_id=1, source_target_pairs={{0,6},{1,7},{2,4},{3,5},{4,2},{5,3},{6,0},{7,1},{8,14},{9,15},{10,... | collective-permute-start | bytes 442376 | tf_op jit(solution)/shard_map/ppermute | solution.py:62
  67.9 1.7 %collective-permute-done.16.refs_2_ = bf16[8,9216]{1,0:T(8,128)(2,1)S(1)} collective-permute-done((bf16[8,9216]{1,0:T(8,128)(2,1)S(1)}, bf16[8,9216]{1,0:T(8,128)(2,1)S(1)}, u32[]{:S(2)}, u32[]{:S(2)}) %collective-permute-start.16) | collective-permute-done | bytes 147488 | tf_op jit(solution)/shard_map/ppermute | solution.py:62
  (57 shorter events, 14.7 us)
Async XLA Ops:
  0.0 15.9 %collective-permute-start = (bf16[2,2,18432]{2,1,0:T(2,128)(2,1)}, bf16[2,2,18432]{2,1,0:T(2,128)(2,1)S(1)}, u32[]{:S(2)}, u32[]{:S(2)}) collective-permute-start(bf16[2,2,18432]{2,1,0:T(2,128)(2,1)} %refs_2_.1), channel_id=1, source_target_pairs={{0,6},{1,7},{2,4},{3,5},{4,2},{5,3},{6,0},{7,1},{8,14},{9,15},{10,... | collective-permute-start | bytes 442376 | tf_op jit(solution)/shard_map/ppermute | solution.py:62
  4.0 11.9 %collective-permute-start.1 = (bf16[2,2,18432]{2,1,0:T(2,128)(2,1)}, bf16[2,2,18432]{2,1,0:T(2,128)(2,1)S(1)}, u32[]{:S(2)}, u32[]{:S(2)}) collective-permute-start(bf16[2,2,18432]{2,1,0:T(2,128)(2,1)} %refs_2_.1), channel_id=1, source_target_pairs={{0,8},{1,9},{2,10},{3,11},{4,12},{5,13},{6,14},{7,15},{8,0},{9,1},... | collective-permute-start | bytes 442376 | tf_op jit(solution)/shard_map/ppermute | solution.py:62
  6.6 9.3 %collective-permute-start.2 = (bf16[2,2,18432]{2,1,0:T(2,128)(2,1)}, bf16[2,2,18432]{2,1,0:T(2,128)(2,1)S(1)}, u32[]{:S(2)}, u32[]{:S(2)}) collective-permute-start(bf16[2,2,18432]{2,1,0:T(2,128)(2,1)} %refs_2_.1), channel_id=1, source_target_pairs={{0,2},{1,3},{2,0},{3,1},{4,6},{5,7},{6,4},{7,5},{8,10},{9,11},{10,... | collective-permute-start | bytes 442376 | tf_op jit(solution)/shard_map/ppermute | solution.py:62
  7.1 8.8 %collective-permute-start.3 = (bf16[2,2,18432]{2,1,0:T(2,128)(2,1)}, bf16[2,2,18432]{2,1,0:T(2,128)(2,1)S(1)}, u32[]{:S(2)}, u32[]{:S(2)}) collective-permute-start(bf16[2,2,18432]{2,1,0:T(2,128)(2,1)} %refs_2_.1), channel_id=1, source_target_pairs={{0,4},{1,5},{2,6},{3,7},{4,0},{5,1},{6,2},{7,3},{8,12},{9,13},{10,... | collective-permute-start | bytes 442376 | tf_op jit(solution)/shard_map/ppermute | solution.py:62
  15.9 11.5 %collective-permute-start.4 = (f32[4,8,18432]{2,1,0:T(8,128)S(1)}, f32[4,8,18432]{2,1,0:T(8,128)S(1)}, u32[]{:S(2)}, u32[]{:S(2)}) collective-permute-start(f32[4,8,18432]{2,1,0:T(8,128)S(1)} %get-tuple-element.25), channel_id=1, source_target_pairs={{0,1},{1,0},{2,3},{3,2},{4,5},{5,4},{6,7},{7,6},{8,9},{9,8},{10,11... | collective-permute-start | bytes 7077896 | tf_op jit(solution)/shard_map/ppermute | solution.py:62
  17.6 6.0 %collective-permute-start.5 = (bf16[2,2,18432]{2,1,0:T(2,128)(2,1)S(1)}, bf16[2,2,18432]{2,1,0:T(2,128)(2,1)S(1)}, u32[]{:S(2)}, u32[]{:S(2)}) collective-permute-start(bf16[2,2,18432]{2,1,0:T(2,128)(2,1)S(1)} %collective-permute-done.1.refs_3_), channel_id=1, source_target_pairs={{0,4},{1,5},{2,6},{3,7},{4,0},{5,1},{6,2},{7,3},{8,12},{9,13},{10,... | collective-permute-start | bytes 442376 | tf_op jit(solution)/shard_map/ppermute | solution.py:62
  19.7 4.4 %collective-permute-start.9 = (f32[2,128]{1,0:T(2,128)S(1)}, f32[2,128]{1,0:T(2,128)S(1)}, u32[]{:S(2)}, u32[]{:S(2)}) collective-permute-start(f32[2,128]{1,0:T(2,128)S(1)} %fusion.3), channel_id=1, source_target_pairs={{0,4},{1,5},{2,6},{3,7},{4,0},{5,1},{6,2},{7,3},{8,12},{9,13},{10,... | collective-permute-start | bytes 3080 | tf_op jit(solution)/shard_map/ppermute | solution.py:62
  21.3 6.1 %collective-permute-start.7 = (bf16[2,2,18432]{2,1,0:T(2,128)(2,1)S(1)}, bf16[2,2,18432]{2,1,0:T(2,128)(2,1)S(1)}, u32[]{:S(2)}, u32[]{:S(2)}) collective-permute-start(bf16[2,2,18432]{2,1,0:T(2,128)(2,1)S(1)} %collective-permute-done.1.refs_3_), channel_id=1, source_target_pairs={{0,2},{1,3},{2,0},{3,1},{4,6},{5,7},{6,4},{7,5},{8,10},{9,11},{10,... | collective-permute-start | bytes 442376 | tf_op jit(solution)/shard_map/ppermute | solution.py:62
  23.6 6.0 %collective-permute-start.6 = (bf16[2,2,18432]{2,1,0:T(2,128)(2,1)S(1)}, bf16[2,2,18432]{2,1,0:T(2,128)(2,1)S(1)}, u32[]{:S(2)}, u32[]{:S(2)}) collective-permute-start(bf16[2,2,18432]{2,1,0:T(2,128)(2,1)S(1)} %collective-permute-done.5.refs_5_), channel_id=1, source_target_pairs={{0,2},{1,3},{2,0},{3,1},{4,6},{5,7},{6,4},{7,5},{8,10},{9,11},{10,... | collective-permute-start | bytes 442376 | tf_op jit(solution)/shard_map/ppermute | solution.py:62
  24.1 5.4 %collective-permute-start.10 = (f32[2,128]{1,0:T(2,128)S(1)}, f32[2,128]{1,0:T(2,128)S(1)}, u32[]{:S(2)}, u32[]{:S(2)}) collective-permute-start(f32[2,128]{1,0:T(2,128)S(1)} %fusion.4.refs_5_), channel_id=1, source_target_pairs={{0,8},{1,9},{2,10},{3,11},{4,12},{5,13},{6,14},{7,15},{8,0},{9,1},... | collective-permute-start | bytes 3080 | tf_op jit(solution)/shard_map/ppermute | solution.py:62
  32.5 6.8 %collective-permute-start.19 = (bf16[8,9216]{1,0:T(8,128)(2,1)S(1)}, bf16[8,9216]{1,0:T(8,128)(2,1)S(1)}, u32[]{:S(2)}, u32[]{:S(2)}) collective-permute-start(bf16[8,9216]{1,0:T(8,128)(2,1)S(1)} %get-tuple-element.34), channel_id=1, source_target_pairs={{0,4},{1,5},{2,6},{3,7},{4,0},{5,1},{6,2},{7,3},{8,12},{9,13},{10,... | collective-permute-start | bytes 442376 | tf_op jit(solution)/shard_map/ppermute | solution.py:62
  33.2 7.6 %collective-permute-start.20 = (bf16[8,9216]{1,0:T(8,128)(2,1)S(1)}, bf16[8,9216]{1,0:T(8,128)(2,1)S(1)}, u32[]{:S(2)}, u32[]{:S(2)}) collective-permute-start(bf16[8,9216]{1,0:T(8,128)(2,1)S(1)} %get-tuple-element.35), channel_id=1, source_target_pairs={{0,2},{1,3},{2,0},{3,1},{4,6},{5,7},{6,4},{7,5},{8,10},{9,11},{10,... | collective-permute-start | bytes 442376 | tf_op jit(solution)/shard_map/ppermute | solution.py:62
  34.7 8.9 %collective-permute-start.21 = (bf16[8,9216]{1,0:T(8,128)(2,1)S(1)}, bf16[8,9216]{1,0:T(8,128)(2,1)S(1)}, u32[]{:S(2)}, u32[]{:S(2)}) collective-permute-start(bf16[8,9216]{1,0:T(8,128)(2,1)S(1)} %get-tuple-element.36), channel_id=1, source_target_pairs={{0,6},{1,7},{2,4},{3,5},{4,2},{5,3},{6,0},{7,1},{8,14},{9,15},{10,... | collective-permute-start | bytes 442376 | tf_op jit(solution)/shard_map/ppermute | solution.py:62
  36.7 8.9 %collective-permute-start.12 = (bf16[8,9216]{1,0:T(8,128)(2,1)S(1)}, bf16[8,9216]{1,0:T(8,128)(2,1)S(1)}, u32[]{:S(2)}, u32[]{:S(2)}) collective-permute-start(bf16[8,9216]{1,0:T(8,128)(2,1)S(1)} %get-tuple-element.28), channel_id=1, source_target_pairs={{0,4},{1,5},{2,6},{3,7},{4,0},{5,1},{6,2},{7,3},{8,12},{9,13},{10,... | collective-permute-start | bytes 442376 | tf_op jit(solution)/shard_map/ppermute | solution.py:62
  37.4 8.2 %collective-permute-start.13 = (bf16[8,9216]{1,0:T(8,128)(2,1)S(1)}, bf16[8,9216]{1,0:T(8,128)(2,1)S(1)}, u32[]{:S(2)}, u32[]{:S(2)}) collective-permute-start(bf16[8,9216]{1,0:T(8,128)(2,1)S(1)} %get-tuple-element.29), channel_id=1, source_target_pairs={{0,2},{1,3},{2,0},{3,1},{4,6},{5,7},{6,4},{7,5},{8,10},{9,11},{10,... | collective-permute-start | bytes 442376 | tf_op jit(solution)/shard_map/ppermute | solution.py:62
  39.3 12.4 %collective-permute-start.14 = (bf16[8,9216]{1,0:T(8,128)(2,1)S(1)}, bf16[8,9216]{1,0:T(8,128)(2,1)S(1)}, u32[]{:S(2)}, u32[]{:S(2)}) collective-permute-start(bf16[8,9216]{1,0:T(8,128)(2,1)S(1)} %get-tuple-element.30), channel_id=1, source_target_pairs={{0,6},{1,7},{2,4},{3,5},{4,2},{5,3},{6,0},{7,1},{8,14},{9,15},{10,... | collective-permute-start | bytes 442376 | tf_op jit(solution)/shard_map/ppermute | solution.py:62
  43.7 9.2 %collective-permute-start.22 = (bf16[8,9216]{1,0:T(8,128)(2,1)S(1)}, bf16[8,9216]{1,0:T(8,128)(2,1)S(1)}, u32[]{:S(2)}, u32[]{:S(2)}) collective-permute-start(bf16[8,9216]{1,0:T(8,128)(2,1)S(1)} %get-tuple-element.38), channel_id=1, source_target_pairs={{0,8},{1,9},{2,10},{3,11},{4,12},{5,13},{6,14},{7,15},{8,0},{9,1},... | collective-permute-start | bytes 442376 | tf_op jit(solution)/shard_map/ppermute | solution.py:62
  53.0 6.6 %collective-permute-start.23 = (bf16[8,9216]{1,0:T(8,128)(2,1)S(1)}, bf16[8,9216]{1,0:T(8,128)(2,1)S(1)}, u32[]{:S(2)}, u32[]{:S(2)}) collective-permute-start(bf16[8,9216]{1,0:T(8,128)(2,1)S(1)} %add_convert_fusion.refs_2_), channel_id=1, source_target_pairs={{0,4},{1,5},{2,6},{3,7},{4,0},{5,1},{6,2},{7,3},{8,12},{9,13},{10,... | collective-permute-start | bytes 442376 | tf_op jit(solution)/shard_map/ppermute | solution.py:62
  53.0 8.6 %collective-permute-start.15 = (bf16[8,9216]{1,0:T(8,128)(2,1)S(1)}, bf16[8,9216]{1,0:T(8,128)(2,1)S(1)}, u32[]{:S(2)}, u32[]{:S(2)}) collective-permute-start(bf16[8,9216]{1,0:T(8,128)(2,1)S(1)} %get-tuple-element.32), channel_id=1, source_target_pairs={{0,8},{1,9},{2,10},{3,11},{4,12},{5,13},{6,14},{7,15},{8,0},{9,1},... | collective-permute-start | bytes 442376 | tf_op jit(solution)/shard_map/ppermute | solution.py:62
  55.3 10.1 %collective-permute-start.24 = (bf16[8,9216]{1,0:T(8,128)(2,1)S(1)}, bf16[8,9216]{1,0:T(8,128)(2,1)S(1)}, u32[]{:S(2)}, u32[]{:S(2)}) collective-permute-start(bf16[8,9216]{1,0:T(8,128)(2,1)S(1)} %add_convert_fusion.refs_2_), channel_id=1, source_target_pairs={{0,2},{1,3},{2,0},{3,1},{4,6},{5,7},{6,4},{7,5},{8,10},{9,11},{10,... | collective-permute-start | bytes 442376 | tf_op jit(solution)/shard_map/ppermute | solution.py:62
  59.6 6.9 %collective-permute-start.25 = (bf16[8,9216]{1,0:T(8,128)(2,1)S(1)}, bf16[8,9216]{1,0:T(8,128)(2,1)S(1)}, u32[]{:S(2)}, u32[]{:S(2)}) collective-permute-start(bf16[8,9216]{1,0:T(8,128)(2,1)S(1)} %collective-permute-done.23.refs_3_), channel_id=1, source_target_pairs={{0,2},{1,3},{2,0},{3,1},{4,6},{5,7},{6,4},{7,5},{8,10},{9,11},{10,... | collective-permute-start | bytes 442376 | tf_op jit(solution)/shard_map/ppermute | solution.py:62
  61.7 5.6 %collective-permute-start.18 = (bf16[8,9216]{1,0:T(8,128)(2,1)S(1)}, bf16[8,9216]{1,0:T(8,128)(2,1)S(1)}, u32[]{:S(2)}, u32[]{:S(2)}) collective-permute-start(bf16[8,9216]{1,0:T(8,128)(2,1)S(1)} %add_convert_fusion.1.refs_2_), channel_id=1, source_target_pairs={{0,4},{1,5},{2,6},{3,7},{4,0},{5,1},{6,2},{7,3},{8,12},{9,13},{10,... | collective-permute-start | bytes 442376 | tf_op jit(solution)/shard_map/ppermute | solution.py:62
  61.8 7.8 %collective-permute-start.16 = (bf16[8,9216]{1,0:T(8,128)(2,1)S(1)}, bf16[8,9216]{1,0:T(8,128)(2,1)S(1)}, u32[]{:S(2)}, u32[]{:S(2)}) collective-permute-start(bf16[8,9216]{1,0:T(8,128)(2,1)S(1)} %add_convert_fusion.1.refs_2_), channel_id=1, source_target_pairs={{0,2},{1,3},{2,0},{3,1},{4,6},{5,7},{6,4},{7,5},{8,10},{9,11},{10,... | collective-permute-start | bytes 442376 | tf_op jit(solution)/shard_map/ppermute | solution.py:62
  62.7 6.9 %collective-permute-start.17 = (bf16[8,9216]{1,0:T(8,128)(2,1)S(1)}, bf16[8,9216]{1,0:T(8,128)(2,1)S(1)}, u32[]{:S(2)}, u32[]{:S(2)}) collective-permute-start(bf16[8,9216]{1,0:T(8,128)(2,1)S(1)} %add_convert_fusion.1.refs_2_), channel_id=1, source_target_pairs={{0,6},{1,7},{2,4},{3,5},{4,2},{5,3},{6,0},{7,1},{8,14},{9,15},{10,... | collective-permute-start | bytes 442376 | tf_op jit(solution)/shard_map/ppermute | solution.py:62
  (4 other events, 17.7 us)
